TPU v7x, 32 devices: a whole 2x2x4 slice. The times are simulated.
32 devices in a mesh: wide: 8 (over y, x, core), narrow: 4 (over z).
Axes of the slice: x: 2, y: 2, z: 4, core: 2. Of those that a mesh axis runs over, the one named last changes fastest.
Arguments:
- hidden: bfloat16 [128, 4096], P('wide'), may hold values from -6 to 6
- conv_cache: bfloat16 [3, 8192, 128], P(None, ('wide', 'narrow')), may hold values from -6 to 6
- ssm_cache: bfloat16 [8192, 16, 128], P(('wide', 'narrow')), may hold values from -6 to 6
- mixer_gain: float32 [4096], replicated, may hold values from 0.1 to 1.9
- in_weight: bfloat16 [2, 8192, 4096], P(None, ('wide', 'narrow')), may hold values from -0.09375 to 0.09375
- conv_weight: float32 [4, 8192], P(None, ('wide', 'narrow')), may hold values from -3 to 3
- conv_bias: float32 [8192], P(('wide', 'narrow')), may hold values from -3 to 3
- select_weight: bfloat16 [8192, 288], P(('wide', 'narrow')), may hold values from -0.125 to 0.125
- step_gain: float32 [256], replicated, may hold values from 0.1 to 1.9
- step_weight: bfloat16 [8192, 256], P(('wide', 'narrow')), may hold values from -0.375 to 0.375
- step_bias: float32 [8192], P(('wide', 'narrow')), may hold values from -5 to -1
- decay_log: float32 [8192, 16], P(('wide', 'narrow')), may hold values from 0 to 2.8
- skip_gain: float32 [8192], P(('wide', 'narrow')), may hold values from 0.5 to 1.5
- out_weight: bfloat16 [8192, 4096], P(('wide', 'narrow')), may hold values from -0.125 to 0.125
- ffn_gain: float32 [4096], replicated, may hold values from 0.1 to 1.9
- gate_proj: bfloat16 [4096, 98304], P(None, ('wide', 'narrow')), may hold values from -0.09375 to 0.09375
- up_proj: bfloat16 [4096, 98304], P(None, ('wide', 'narrow')), may hold values from -0.09375 to 0.09375
- down_proj: bfloat16 [98304, 4096], P(('wide', 'narrow')), may hold values from -0.109375 to 0.109375
- route_experts: int32 [128, 2], P('wide'), may hold values from 0 to 7, all different within a row; in each aligned block of 16 rows (0 to 15, 16 to 31, ...) at most 10 rows name the same one
- route_share: float32 [128, 2], P('wide'), may hold values from 0.2 to 1
Outputs:
- layer_out: bfloat16 [128, 4096], P('wide', 'narrow')
- new_state: bfloat16 [8192, 16, 128], P(('wide', 'narrow'))
Inputs may be any that keep to these rules, and one draw needn't show every extreme that they name: `route_experts`: each row names two different experts. Among the 16 rows of one index of wide (aligned blocks), no expert is named by more than 10 rows, and in every draw some block has an expert named by exactly 10 rows.
All inputs are finite; a program needn't handle non-finite values.
Results may differ from a plain program's by a relative error of at most 0.017.
Values may be sent and summed in bfloat16 or wider, within the bound.
No kernel may reach another device: no remote copies, remote signals or barrier semaphores. Data moves between devices by JAX's collectives and lax.ppermute only.
A program may use at most 128 MiB of HBM per device.

v0:
```python
import jax
import jax.numpy as jnp
from jax import lax
from jax.sharding import PartitionSpec as P

EXPERTS = 8
CAPACITY = 10


def rms_scale(values, gain):
    mean_square = jnp.mean(values * values, axis=-1, keepdims=True)
    return values * lax.rsqrt(mean_square + 1e-06) * gain


def on_device(
    hidden,
    conv_cache,
    ssm_cache,
    mixer_gain,
    in_weight,
    conv_weight,
    conv_bias,
    select_weight,
    step_gain,
    step_weight,
    step_bias,
    decay_log,
    skip_gain,
    out_weight,
    ffn_gain,
    gate_proj,
    up_proj,
    down_proj,
    route_experts,
    route_share,
):
    narrow_count = lax.axis_size("narrow")
    wide_count = lax.axis_size("wide")
    local_rows = hidden.shape[0]
    width = hidden.shape[1]
    rank_width = step_weight.shape[1]
    state_width = decay_log.shape[1]
    topk_count = route_experts.shape[1]
    hidden_f = hidden.astype(jnp.float32)
    normed = rms_scale(hidden_f, mixer_gain).astype(jnp.bfloat16)
    projected = jnp.einsum(
        "kcd,rd->kcr",
        in_weight,
        lax.all_gather(normed, "wide", axis=0, tiled=True),
        preferred_element_type=jnp.float32,
    )
    x_input = projected[0]
    z_gate = projected[1]
    history = conv_cache.astype(jnp.float32)
    pre_conv = conv_bias[:, None] + conv_weight[3][:, None] * x_input
    for tap in range(3):
        pre_conv = pre_conv + conv_weight[tap][:, None] * history[tap]
    conved = jax.nn.silu(pre_conv)
    conved_bf = conved.astype(jnp.bfloat16)
    select_part = jnp.einsum(
        "cr,cj->rj", conved_bf, select_weight, preferred_element_type=jnp.float32
    )
    selected = lax.psum(select_part, ("wide", "narrow"))
    step_low = rms_scale(selected[:, :rank_width], step_gain).astype(jnp.bfloat16)
    step_size = jax.nn.softplus(
        jnp.dot(step_weight, step_low.T, preferred_element_type=jnp.float32) + step_bias[:, None]
    )
    in_coef = selected[:, rank_width : rank_width + state_width].T
    out_coef = selected[:, rank_width + state_width :].T
    decay = jnp.exp(-step_size[:, None, :] * jnp.exp(decay_log)[:, :, None])
    state_f = (
        decay * ssm_cache.astype(jnp.float32)
        + (step_size * conved)[:, None, :] * in_coef[None, :, :]
    )
    gated = (
        (jnp.sum(state_f * out_coef[None, :, :], axis=1) + skip_gain[:, None] * conved)
        * jax.nn.silu(z_gate)
    ).astype(jnp.bfloat16)
    partial_sum = lax.psum_scatter(
        jnp.einsum("cr,cd->rd", gated, out_weight, preferred_element_type=jnp.float32).astype(
            jnp.bfloat16
        ),
        "wide",
        scatter_dimension=0,
        tiled=True,
    )
    summed = lax.psum(partial_sum, "narrow").astype(jnp.float32)
    residual = (hidden_f + summed).astype(jnp.bfloat16)
    residual_f = residual.astype(jnp.float32)
    ffn_in = rms_scale(residual_f, ffn_gain).astype(jnp.bfloat16)
    assign = route_experts.reshape(-1)
    hits = (assign[:, None] == jnp.arange(EXPERTS, dtype=jnp.int32)[None, :]).astype(jnp.int32)
    earlier = jnp.cumsum(hits, axis=0) - hits
    slot = jnp.sum(earlier * hits, axis=1)
    target = assign * CAPACITY + slot
    placer = jnp.arange(EXPERTS * CAPACITY, dtype=jnp.int32)[:, None] == target[None, :]
    repeated = jnp.repeat(ffn_in, topk_count, axis=0)
    packed = jnp.dot(
        placer.astype(jnp.bfloat16), repeated, preferred_element_type=jnp.float32
    ).astype(jnp.bfloat16)
    group = wide_count // EXPERTS
    outgoing = jnp.repeat(packed.reshape(EXPERTS, CAPACITY, width), group, axis=0)
    arrived = lax.all_to_all(outgoing, "wide", split_axis=0, concat_axis=0, tiled=True)
    flat_in = arrived.reshape(-1, arrived.shape[2])
    gate_act = jnp.dot(flat_in, gate_proj, preferred_element_type=jnp.float32)
    up_act = jnp.dot(flat_in, up_proj, preferred_element_type=jnp.float32)
    inner = (jax.nn.silu(gate_act) * up_act).astype(jnp.bfloat16)
    result = jnp.dot(inner, down_proj, preferred_element_type=jnp.float32)
    expert_out = result.reshape(arrived.shape[0], arrived.shape[1], result.shape[1])
    weighted = (
        (placer.astype(jnp.float32) * route_share.reshape(-1)[None, :])
        .reshape(EXPERTS * CAPACITY, local_rows, topk_count)
        .sum(axis=2)
    )
    returned = lax.all_to_all(
        expert_out.astype(jnp.bfloat16), "wide", split_axis=0, concat_axis=0, tiled=True
    ).astype(expert_out.dtype)
    grouped = (
        returned.reshape(EXPERTS, group, CAPACITY, width)
        .sum(axis=1)
        .reshape(EXPERTS * CAPACITY, width)
    )
    combined = jnp.dot(
        weighted.T, grouped, precision=lax.Precision.HIGHEST, preferred_element_type=jnp.float32
    )
    ffn_cols = lax.psum_scatter(
        combined.astype(jnp.bfloat16), "narrow", scatter_dimension=1, tiled=True
    ).astype(jnp.float32)
    col_share = width // narrow_count
    own_cols = lax.dynamic_slice_in_dim(
        residual_f, lax.axis_index("narrow") * col_share, col_share, 1
    )
    layer_out = (own_cols + ffn_cols).astype(jnp.bfloat16)
    return (layer_out, state_f.astype(jnp.bfloat16))


def solution(mesh):
    placed = (
        P("wide", None),
        P(None, ("wide", "narrow"), None),
        P(("wide", "narrow"), None, None),
        P(),
        P(None, ("wide", "narrow"), None),
        P(None, ("wide", "narrow")),
        P(("wide", "narrow")),
        P(("wide", "narrow"), None),
        P(),
        P(("wide", "narrow"), None),
        P(("wide", "narrow")),
        P(("wide", "narrow"), None),
        P(("wide", "narrow")),
        P(("wide", "narrow"), None),
        P(),
        P(None, ("wide", "narrow")),
        P(None, ("wide", "narrow")),
        P(("wide", "narrow"), None),
        P("wide", None),
        P("wide", None),
    )
    return jax.shard_map(
        on_device,
        mesh=mesh,
        in_specs=placed,
        out_specs=(P("wide", "narrow"), P(("wide", "narrow"), None, None)),
        check_vma=False,
    )
```

profile of v0, /device:TPU:0, one launch (start us, length us, event | category | flops | bytes accessed | tf_op | source)
XLA Modules:
  0.0 347.0 jit_solution(10784696896810893148)
XLA Ops:
  7.2 1.2 fusion.10
  8.4 1.7 fusion.12
  10.1 0.0 all-reduce.3.cloned.1.call-start
  10.2 1.1 copy.56
  11.3 0.8 fusion.34
  12.2 24.5 %all-gather.2.cloned.1.call-done = bf16[128,4096]{1,0:T(8,128)(2,1)} async-done(((bf16[16,4096]{1,0:T(8,128)(2,1)}), bf16[128,4096]{1,0:T(8,128)(2,1)}) %all-gather.2.cloned.1.call-update) | async-done | bytes 1048592 | tf_op jit(solution)/shard_map/all_gather | solution.py:49
  36.7 4.0 %convolution_bitcast_fusion = f32[2,256,128]{1,2,0:T(8,128)S(1)} fusion(bf16[2,256,4096]{2,1,0:T(8,128)(2,1)} %param.24, bf16[128,4096]{1,0:T(8,128)(2,1)} %all-gather.2.cloned.1.call-done), kind=kOutput, calls=%fused_computation.9 | convolution fusion | flops 536870912 | bytes 5505024 | tf_op jit(solution)/shard_map/kcd,rd->kcr/dot_general | solution.py:46
  40.8 0.1 divide_multiply_fusion
  40.8 0.9 fusion.26
  41.7 0.0 reduce-scatter.3.cloned.1.call-start
  41.8 0.1 copy.58
  41.9 121.6 %all-reduce.3.cloned.1.call-done = f32[128,288]{0,1:T(8,128)} async-done(((f32[128,288]{0,1:T(8,128)}), f32[128,288]{0,1:T(8,128)}) %all-reduce.3.cloned.1.call-update) | async-done | bytes 147472 | tf_op jit(solution)/shard_map/psum | solution.py:63
  163.5 1.0 multiply_reduce_fusion.2
  164.5 1.3 fusion.33
  165.8 0.1 copy.57
  165.9 0.1 copy.59
  166.0 0.7 slice_bitcast_fusion.6
  166.7 3.3 fusion.1
  170.0 0.1 copy.60
  170.1 1.4 convolution_convert_fusion
  171.6 0.0 all-reduce.5.cloned.1.call-start
  171.6 0.1 copy.61
  171.7 0.1 eq.36
  171.8 0.1 fusion.30
  171.9 0.1 reduce_window_sum.11
  171.9 0.2 select_reduce_fusion.1
  172.1 37.6 %reduce-scatter.3.cloned.1.call-done = bf16[16,4096]{1,0:T(8,128)(2,1)} async-done(((bf16[128,4096]{1,0:T(8,128)(2,1)}), bf16[16,4096]{1,0:T(8,128)(2,1)}) %reduce-scatter.3.cloned.1.call-update) | async-done | bytes 131088 | tf_op jit(solution)/shard_map/reduce_scatter | solution.py:79
  209.7 36.6 %all-reduce.5.cloned.1.call-done = bf16[16,4096]{1,0:T(8,128)(2,1)} async-done(((bf16[16,4096]{1,0:T(8,128)(2,1)}), bf16[16,4096]{1,0:T(8,128)(2,1)}) %all-reduce.5.cloned.1.call-update) | async-done | bytes 131088 | tf_op jit(solution)/shard_map/psum | solution.py:87
  246.3 1.1 fusion.14
  247.4 1.0 multiply_convert_fusion
  248.4 0.2 broadcast_in_dim.2
  248.6 0.1 reshape.85
  248.7 0.3 convolution_convert_fusion.1
  249.0 0.2 reshape_broadcast_in_dim_reshape.3
  249.3 18.8 %all_to_all.10 = bf16[8,10,4096]{2,1,0:T(8,128)(2,1)S(1)} all-to-all(bf16[8,10,4096]{2,1,0:T(8,128)(2,1)S(1)} %reshape_broadcast_in_dim_reshape.3), channel_id=1, replica_groups=mesh['wide'=8,'narrow'=4] {'wide'}, dimensions={0} | all-to-all | bytes 1310720 | tf_op jit(solution)/shard_map/all_to_all | solution.py:103
  268.0 0.2 reshape.86
  268.3 10.4 %fusion.35 = f32[80,3072]{1,0:T(8,128)S(1)} fusion(bf16[80,4096]{1,0:T(8,128)(2,1)S(1)} %reshape.86, bf16[4096,3072]{1,0:T(8,128)(2,1)} %param.35), kind=kOutput, calls=%fused_computation.72 | convolution fusion | flops 2013265920 | bytes 26804224 | tf_op jit(solution)/shard_map/dot_general | solution.py:105
  278.7 19.9 %convolution_convert_fusion.2 = bf16[80,4096]{1,0:T(8,128)(2,1)S(1)} fusion(bf16[3072,4096]{1,0:T(8,128)(2,1)} %param.37, bf16[80,4096]{1,0:T(8,128)(2,1)S(1)} %reshape.86, bf16[4096,3072]{1,0:T(8,128)(2,1)} %param.36, f32[80,3072]{1,0:T(8,128)S(1)} %fusion.35), kind=kOutput, calls=%fused_computation.2 | convolution fusion | flops 4028334080 | bytes 52625408 | tf_op jit(solution)/shard_map/dot_general | solution.py:108
  298.6 1.2 convert_element_type.82
  299.8 3.6 %all-to-all-start.1 = ((bf16[8,10,4096]{2,1,0:T(8,128)(2,1)}), bf16[8,10,4096]{2,1,0:T(8,128)(2,1)S(1)}, u32[]{:S(2)}, u32[]{:S(2)}) async-start(bf16[8,10,4096]{2,1,0:T(8,128)(2,1)} %convert_element_type.82), calls=%async_computation.2 | async-start | bytes 2097152 | tf_op jit(solution)/shard_map/all_to_all | solution.py:115
  303.4 0.1 reduce_sum.64
  303.5 0.1 copy.62
  303.6 0.1 select_reduce_fusion
  303.7 15.0 %all-to-all-done.1 = bf16[8,10,4096]{2,1,0:T(8,128)(2,1)S(1)} async-done(((bf16[8,10,4096]{2,1,0:T(8,128)(2,1)}), bf16[8,10,4096]{2,1,0:T(8,128)(2,1)S(1)}, u32[]{:S(2)}, u32[]{:S(2)}) %all-to-all-start.1) | async-done | bytes 655392 | tf_op jit(solution)/shard_map/all_to_all | solution.py:115
  318.7 1.1 reshape.87
  319.8 2.1 convolution_convert_fusion.3
  321.9 17.2 %reduce-scatter.5.cloned.1.call-done = bf16[16,1024]{1,0:T(8,128)(2,1)} async-done(((bf16[16,4096]{1,0:T(8,128)(2,1)}), bf16[16,1024]{1,0:T(8,128)(2,1)}) %reduce-scatter.5.cloned.1.call-update) | async-done | bytes 32784 | tf_op jit(solution)/shard_map/reduce_scatter | solution.py:126
  339.1 1.4 add_convert_fusion
  (40 shorter events, 0.3 us)
Async XLA Ops:
  7.2 162.9 %copy-start = (bf16[256,4096]{1,0:T(8,128)(2,1)S(1)}, bf16[256,4096]{1,0:T(8,128)(2,1)}, u32[]{:S(2)}) copy-start(bf16[256,4096]{1,0:T(8,128)(2,1)} %param.33) | copy-start | bytes 6291460
  7.2 29.5 %all-gather.2.cloned.1.call-start = ((), (), s32[]{:S(2)}) async-start(), calls=%async_computation.4 | async-start | bytes 1179648 | tf_op jit(solution)/shard_map/all_gather | solution.py:49
  10.1 153.4 %all-reduce.3.cloned.1.call-start = ((), (), s32[]{:S(2)}) async-start(), calls=%async_computation.5 | async-start | bytes 294912 | tf_op jit(solution)/shard_map/psum | solution.py:63
  12.1 28.6 %copy-start.8 = (f32[256]{0:T(256)S(1)}, f32[256]{0:T(256)}, u32[]{:S(2)}) copy-start(f32[256]{0:T(256)} %param.26) | copy-start | bytes 3076
  12.1 28.7 %copy-start.3 = (bf16[256,288]{0,1:T(8,128)(2,1)S(1)}, bf16[256,288]{0,1:T(8,128)(2,1)}, u32[]{:S(2)}) copy-start(bf16[256,288]{0,1:T(8,128)(2,1)} %param.27) | copy-start | bytes 442372
  12.1 29.7 %copy-start.6 = (f32[256,16]{0,1:T(8,128)S(1)}, f32[256,16]{0,1:T(8,128)}, u32[]{:S(2)}) copy-start(f32[256,16]{0,1:T(8,128)} %param.31) | copy-start | bytes 49156
  12.1 152.4 %copy-start.4 = (bf16[256,256]{1,0:T(8,128)(2,1)S(1)}, bf16[256,256]{1,0:T(8,128)(2,1)}, u32[]{:S(2)}) copy-start(bf16[256,256]{1,0:T(8,128)(2,1)} %param.29) | copy-start | bytes 393220
  12.1 152.3 %copy-start.9 = (f32[256]{0:T(256)S(1)}, f32[256]{0:T(256)}, u32[]{:S(2)}) copy-start(f32[256]{0:T(256)} %param.30) | copy-start | bytes 3076
  12.2 152.3 %copy-start.10 = (f32[256]{0:T(256)S(1)}, f32[256]{0:T(256)}, u32[]{:S(2)}) copy-start(f32[256]{0:T(256)} %param.28) | copy-start | bytes 3076
  41.7 168.0 %reduce-scatter.3.cloned.1.call-start = ((), (), s32[]{:S(2)}) async-start(), calls=%async_computation.6 | async-start | bytes 1179648 | tf_op jit(solution)/shard_map/reduce_scatter | solution.py:79
  41.9 128.2 %copy-start.12 = (f32[256]{0:T(256)S(1)}, f32[256]{0:T(256)}, u32[]{:S(2)}) copy-start(f32[256]{0:T(256)} %param.32) | copy-start | bytes 3076
  170.1 1.5 copy-start.7
  170.1 76.3 %copy-start.2 = (bf16[16,4096]{1,0:T(8,128)(2,1)S(1)}, bf16[16,4096]{1,0:T(8,128)(2,1)}, u32[]{:S(2)}) copy-start(bf16[16,4096]{1,0:T(8,128)(2,1)} %param.20) | copy-start | bytes 393220
  170.1 77.3 %copy-start.5 = (f32[4096]{0:T(1024)S(1)}, f32[4096]{0:T(1024)}, u32[]{:S(2)}) copy-start(f32[4096]{0:T(1024)} %param.34) | copy-start | bytes 49156
  171.6 74.8 %all-reduce.5.cloned.1.call-start = ((), (), s32[]{:S(2)}) async-start(), calls=%async_computation.7 | async-start | bytes 262144 | tf_op jit(solution)/shard_map/psum | solution.py:87
  298.6 5.0 %copy-start.11 = (f32[16,2]{0,1:T(2,128)S(1)}, f32[16,2]{0,1:T(2,128)}, u32[]{:S(2)}) copy-start(f32[16,2]{0,1:T(2,128)} %param.39) | copy-start | bytes 388
  298.6 41.9 %copy-start.1 = (bf16[256,4096]{1,0:T(8,128)(2,1)S(1)}, bf16[256,4096]{1,0:T(8,128)(2,1)}, u32[]{:S(2)}) copy-start(bf16[256,4096]{1,0:T(8,128)(2,1)} %param.33) | copy-start | bytes 6291460
  299.8 18.9 %all-to-all-start.1 = ((bf16[8,10,4096]{2,1,0:T(8,128)(2,1)}), bf16[8,10,4096]{2,1,0:T(8,128)(2,1)S(1)}, u32[]{:S(2)}, u32[]{:S(2)}) async-start(bf16[8,10,4096]{2,1,0:T(8,128)(2,1)} %convert_element_type.82), calls=%async_computation.2 | async-start | bytes 2097152 | tf_op jit(solution)/shard_map/all_to_all | solution.py:115
  303.4 35.8 %reduce-scatter.5.cloned.1.call-start = ((), (), s32[]{:S(2)}) async-start(), calls=%async_computation.8 | async-start | bytes 163840 | tf_op jit(solution)/shard_map/reduce_scatter | solution.py:126
Sparse Core Ops, SparseCore 0:
  10.5 26.1 all-gather.1
  42.8 120.6 all-reduce.2
  171.7 37.9 reduce-scatter.2
  211.9 34.4 all-reduce.4
  322.0 17.0 reduce-scatter.4
where the time goes:
time: 348 us; the launch traced here: 347 us
  waiting for transfers between devices  253 us (73%)
  matrix products  40.3 us (12%)
  blocking collectives  18.8 us (5%)
  between operations  14.1 us (4%)
  other arithmetic  11 us (3%)
  local copies, waits for them, and re-layouts  6.43 us (2%)
  starting transfers between devices  3.76 us (1%)
    psum x1, waiting for transfers between devices, on_device(): selected = lax.psum(select_part, ('wide', 'narrow'))  122 us
    reduce_scatter x1, waiting for transfers between devices, on_device(): lax.psum_scatter(jnp.einsum('cr,cd->rd', gated, out_weight, preferred_ele...  37.6 us
    psum x1, waiting for transfers between devices, on_device(): summed = lax.psum(partial_sum, 'narrow').astype(jnp.float32)  36.6 us
    all_gather x1, waiting for transfers between devices, on_device(): lax.all_gather(normed, 'wide', axis=0, tiled=True)  24.5 us
    dot_general x1, matrix products, on_device(): result = jnp.dot(inner, down_proj, preferred_element_type=jnp.float32)  19.9 us
    all_to_all x1, blocking collectives, on_device(): lax.all_to_all(outgoing, 'wide', split_axis=0, concat_axis=0, tiled=True)  18.8 us
    reduce_scatter x1, waiting for transfers between devices, on_device(): lax.psum_scatter(combined.astype(jnp.bfloat16), 'narrow', scatter_dimensi...  17.2 us
    all_to_all x1, waiting for transfers between devices, on_device(): lax.all_to_all(expert_out.astype(jnp.bfloat16), 'wide', split_axis=0, con...  15 us
  transfers between devices with their start and end apart: 6, of which 6 were waited for; matrix products, arithmetic and copies ran while one was open for 1% of the time, Pallas kernels for 0%

commit v1 on v0

v1 whole, which is shorter than its diff:
```python
import functools

import jax
import jax.numpy as jnp
from jax import lax
from jax.experimental import pallas as pl
from jax.experimental.pallas import tpu as pltpu
from jax.sharding import PartitionSpec as P

EXPERTS = 8
EPS = 1e-06
MIB = 1 << 20
LANES = 128
F32 = jnp.float32
BF16 = jnp.bfloat16


def f32(values):
    return values.astype(F32)


def kernel_call(body, outs, args, scalars=1, scratch=(), limit=32):
    smem = pl.BlockSpec(memory_space=pltpu.SMEM)
    vmem = pl.BlockSpec(memory_space=pltpu.VMEM)
    return pl.pallas_call(
        body,
        out_shape=[jax.ShapeDtypeStruct(shape, dtype) for shape, dtype in outs],
        in_specs=[smem] * scalars + [vmem] * (len(args) - scalars),
        out_specs=[vmem] * len(outs),
        scratch_shapes=scratch,
        compiler_params=pltpu.CompilerParams(vmem_limit_bytes=limit * MIB),
    )(*args)


def normalized(block, gain):
    values = f32(block)
    mean_square = jnp.mean(values * values, axis=-1, keepdims=True)
    return (values * lax.rsqrt(mean_square + EPS) * gain).astype(BF16)


def sigmoid_times(values):
    return values / (1.0 + jnp.exp(-values))


def project_kernel(
    blocks,
    place,
    *refs,
):
    rows = refs[:blocks]
    gain, weight, cache, columns, select, conved_out, gate_out, keep, send, normed, selected = refs[
        blocks:
    ]
    me = place[0]
    count = rows[0].shape[0]
    for j in range(blocks):
        start = pl.multiple_of((me ^ j) * count, count)
        normed[pl.ds(start, count), :] = normalized(rows[j][...], gain[...])
    dims = (((1,), (1,)), ((), ()))
    x_input = lax.dot_general(weight[0], normed[...], dims, preferred_element_type=F32)
    pre_conv = columns[:, 4:5] + columns[:, 3:4] * x_input
    for tap in range(3):
        pre_conv = pre_conv + columns[:, tap : tap + 1] * f32(cache[tap])
    conved = sigmoid_times(pre_conv)
    conved_out[...] = conved
    selected[...] = jnp.dot(select[...], conved.astype(BF16), preferred_element_type=F32)
    half = keep.shape[0]
    side = me & 1
    keep[...] = selected[pl.ds(pl.multiple_of(side * half, 16), half), :].astype(BF16)
    send[...] = selected[pl.ds(pl.multiple_of((1 - side) * half, 16), half), :].astype(BF16)
    z_gate = lax.dot_general(weight[1], normed[...], dims, preferred_element_type=F32)
    gate_out[...] = sigmoid_times(z_gate)


def state_kernel(
    blocks,
    place,
    own_half,
    other_half,
    step_gain,
    step_weight,
    columns,
    conved,
    gate,
    cache,
    rates,
    out_weight,
    new_state,
    keep,
    send,
    selected,
    step,
    driven,
    mixed,
    turned,
):
    me = place[0]
    side = me & 1
    half = own_half.shape[0]
    channels, states, rows = cache.shape
    rank = step_weight.shape[1]
    count = rows // blocks
    selected[pl.ds(pl.multiple_of(side * half, 16), half), :] = f32(own_half[...])
    selected[pl.ds(pl.multiple_of((1 - side) * half, 16), half), :] = f32(other_half[...])
    low = selected[:rank, :]
    mean_square = jnp.mean(low * low, axis=0, keepdims=True)
    step_low = (low * lax.rsqrt(mean_square + EPS) * step_gain[...]).astype(BF16)
    raw = jnp.dot(step_weight[...], step_low, preferred_element_type=F32) + columns[:, 5:6]
    sizes = jnp.maximum(raw, 0.0) + jnp.log1p(jnp.exp(-jnp.abs(raw)))
    step[...] = sizes
    driven[...] = sizes * conved[...]
    in_coef = selected[rank : rank + states, :]
    out_coef = selected[rank + states :, :]

    def channel(c, carry):
        one = pl.ds(c, 1)
        state = jnp.exp(step[one, :] * rates[c]) * f32(cache[c]) + driven[one, :] * in_coef
        new_state[c] = state.astype(BF16)
        mixed[one, :] = jnp.sum(state * out_coef, axis=0, keepdims=True)
        return carry

    lax.fori_loop(0, channels, channel, 0, unroll=8)
    gated = (mixed[...] + columns[:, 6:7] * conved[...]) * gate[...]
    turned[...] = gated.T
    parts = []
    for side_of in range(2):
        for k in range(blocks // 2):
            start = pl.multiple_of((me ^ (2 * k + side_of)) * count, count)
            parts.append(turned[pl.ds(start, count), :].astype(BF16))
    left = jnp.concatenate(parts, axis=0)
    kept = keep.shape[0]
    width = out_weight.shape[1]
    piece = 512 if width % 512 == 0 else width
    for start in range(0, width, piece):
        span = slice(start, start + piece)
        partial = jnp.dot(left, out_weight[:, span], preferred_element_type=F32).astype(BF16)
        keep[:, span] = partial[:kept]
        send[:, span] = partial[kept:]


def split_kernel(keep, got, *outs):
    count = outs[0].shape[0]
    for k, out in enumerate(outs):
        span = slice(k * count, (k + 1) * count)
        out[...] = (f32(keep[span, :]) + f32(got[span, :])).astype(BF16)


def add_kernel(*refs):
    total = f32(refs[0][...])
    for ref in refs[1:-1]:
        total = total + f32(ref[...])
    refs[-1][...] = total.astype(refs[-1].dtype)


def residual_kernel(mine, got, hidden, experts, share, out):
    width = hidden.shape[1]
    residual = f32(hidden[...]) + (f32(mine[...]) + f32(got[...]))
    out[:, :width] = residual.astype(BF16)
    lane = lax.broadcasted_iota(jnp.int32, (hidden.shape[0], LANES), 1)
    first = lane < LANES // 2
    number = jnp.where(first, lane, lane - LANES // 2)
    dense = jnp.zeros(lane.shape, F32)
    for k in range(experts.shape[1]):
        dense = dense + jnp.where(number == experts[:, k : k + 1], share[:, k : k + 1], 0.0)
    upper = dense.astype(BF16)
    lower = (dense - f32(upper)).astype(BF16)
    out[:, width:] = jnp.where(first, f32(upper), f32(lower)).astype(BF16)


def expert_kernel(blocks, group, place, *refs):
    rows = refs[:blocks]
    gain, gate_proj, up_proj, down_proj, keep, send, normed, share, total = refs[blocks:]
    index = pl.program_id(0)
    count = rows[0].shape[0]
    width = gain.shape[1]

    @pl.when(index == 0)
    def _():
        expert = place[0] // group
        lane = lax.broadcasted_iota(jnp.int32, (count, LANES), 1)
        wanted = (lane == expert) | (lane == expert + LANES // 2)
        for j in range(blocks):
            span = slice(j * count, (j + 1) * count)
            normed[span, :] = normalized(rows[j][:, :width], gain[...])
            shares = jnp.where(wanted, f32(rows[j][:, width:]), 0.0)
            share[span, :] = jnp.broadcast_to(
                jnp.sum(shares, axis=1, keepdims=True), (count, LANES)
            )

    inputs = normed[...]
    gate_act = jnp.dot(inputs, gate_proj[...], preferred_element_type=F32)
    up_act = jnp.dot(inputs, up_proj[...], preferred_element_type=F32)
    inner = (sigmoid_times(gate_act) * up_act).astype(BF16)
    added = jnp.dot(inner, down_proj[...], preferred_element_type=F32)

    @pl.when(index == 0)
    def _():
        total[...] = added

    @pl.when(index > 0)
    def _():
        total[...] += added

    @pl.when(index == pl.num_programs(0) - 1)
    def _():
        weighted = (total[...] * share[:, :1]).astype(BF16)
        kept = keep.shape[0]
        keep[...] = weighted[:kept]
        send[...] = weighted[kept:]


def columns_kernel(place, *refs):
    outs = refs[-place_count(refs) :]
    ins = refs[: -len(outs)]
    size = outs[0].shape[1]
    me = place[1]
    for k, out in enumerate(outs):
        span = pl.ds(pl.multiple_of((me ^ k) * size, size), size)
        total = f32(ins[0][:, span])
        for ref in ins[1:]:
            total = total + f32(ref[:, span])
        out[...] = total.astype(BF16)


def place_count(refs):
    return refs[0].shape[1] // refs[-1].shape[1]


def final_kernel(place, residual, *refs):
    out = refs[-1]
    size = out.shape[1]
    span = pl.ds(pl.multiple_of(place[1] * size, size), size)
    total = f32(refs[0][...])
    for ref in refs[1:-1]:
        total = total + f32(ref[...])
    out[...] = (f32(residual[:, span]) + total).astype(BF16)


def on_device(
    hidden,
    conv_cache,
    ssm_cache,
    mixer_gain,
    in_weight,
    conv_weight,
    conv_bias,
    select_weight,
    step_gain,
    step_weight,
    step_bias,
    decay_log,
    skip_gain,
    out_weight,
    ffn_gain,
    gate_proj,
    up_proj,
    down_proj,
    route_experts,
    route_share,
):
    narrow_count = lax.axis_size("narrow")
    wide_count = lax.axis_size("wide")
    chips = wide_count // 2
    count, width = hidden.shape
    rows = count * wide_count
    channels, states = decay_log.shape
    chosen = select_weight.shape[1]
    hidden_units = gate_proj.shape[1]

    def swap(values):
        return lax.ppermute(values, "wide", [(i, i ^ 1) for i in range(wide_count)])

    def to_chip(values, k):
        return lax.ppermute(values, "wide", [(i, i ^ (2 * k)) for i in range(wide_count)])

    def to_narrow(values, k):
        return lax.ppermute(values, "narrow", [(i, i ^ k) for i in range(narrow_count)])

    def plane_gather(block):
        same = [block] + [to_chip(block, k) for k in range(1, chips)]
        other = [swap(item) for item in same]
        return same, other

    def plane_scatter(keep, got):
        parts = kernel_call(split_kernel, [((count, width), BF16)] * chips, (keep, got), scalars=0)
        return [parts[0]] + [to_chip(parts[k], k) for k in range(1, chips)]

    def add(*items):
        return kernel_call(add_kernel, [(items[0].shape, BF16)], items, scalars=0)[0]

    place = jnp.stack([lax.axis_index("wide"), lax.axis_index("narrow")]).astype(jnp.int32)
    columns = jnp.concatenate(
        [conv_weight.T, jnp.stack([conv_bias, step_bias, skip_gain], axis=1)], axis=1
    )
    rates = jnp.broadcast_to(-jnp.exp(decay_log)[:, :, None], (channels, states, rows))

    same, other = plane_gather(hidden)
    interleaved = [item for pair in zip(same, other) for item in pair]
    half = chosen // 2
    conved, gate, keep, send = kernel_call(
        functools.partial(project_kernel, wide_count),
        [
            ((channels, rows), F32),
            ((channels, rows), F32),
            ((half, rows), BF16),
            ((half, rows), BF16),
        ],
        (place, *interleaved, mixer_gain[None, :], in_weight, conv_cache, columns, select_weight.T),
        scratch=[pltpu.VMEM((rows, width), BF16), pltpu.VMEM((chosen, rows), F32)],
    )
    part = add(keep, swap(send))
    part = add(part, *[to_chip(part, k) for k in range(1, chips)])
    part = add(part, *[to_narrow(part, k) for k in range(1, narrow_count)])
    new_state, keep, send = kernel_call(
        functools.partial(state_kernel, wide_count),
        [
            (ssm_cache.shape, BF16),
            ((rows // 2, width), BF16),
            ((rows // 2, width), BF16),
        ],
        (
            place,
            part,
            swap(part),
            step_gain[:, None],
            step_weight,
            columns,
            conved,
            gate,
            ssm_cache,
            rates,
            out_weight,
        ),
        scratch=[
            pltpu.VMEM((chosen, rows), F32),
            pltpu.VMEM((channels, rows), F32),
            pltpu.VMEM((channels, rows), F32),
            pltpu.VMEM((channels, rows), F32),
            pltpu.VMEM((rows, channels), F32),
        ],
    )
    parts = plane_scatter(keep, swap(send))
    mine = add(*parts)
    step = 1
    while 2 * step < narrow_count:
        mine = add(mine, to_narrow(mine, step))
        step *= 2
    (residual,) = kernel_call(
        residual_kernel,
        [((count, width + LANES), BF16)],
        (mine, to_narrow(mine, step), hidden, route_experts, route_share),
        scalars=0,
    )
    same, other = plane_gather(residual)
    block = next(size for size in (256, 128, hidden_units) if hidden_units % size == 0)
    whole = pl.BlockSpec(memory_space=pltpu.VMEM)
    keep, send = pl.pallas_call(
        functools.partial(expert_kernel, wide_count, wide_count // EXPERTS),
        grid=(hidden_units // block,),
        out_shape=[jax.ShapeDtypeStruct((rows // 2, width), BF16)] * 2,
        in_specs=[pl.BlockSpec(memory_space=pltpu.SMEM)]
        + [whole] * (wide_count + 1)
        + [pl.BlockSpec((width, block), lambda i: (0, i))] * 2
        + [pl.BlockSpec((block, width), lambda i: (i, 0))],
        out_specs=[whole] * 2,
        scratch_shapes=[
            pltpu.VMEM((rows, width), BF16),
            pltpu.VMEM((rows, LANES), F32),
            pltpu.VMEM((rows, width), F32),
        ],
        compiler_params=pltpu.CompilerParams(vmem_limit_bytes=48 * MIB),
    )(place, *same, *other, ffn_gain[None, :], gate_proj, up_proj, down_proj)
    parts = plane_scatter(keep, swap(send))
    col_share = width // narrow_count
    shares = kernel_call(
        columns_kernel, [((count, col_share), BF16)] * narrow_count, (place, *parts)
    )
    (layer_out,) = kernel_call(
        final_kernel,
        [((count, col_share), BF16)],
        (
            place,
            residual,
            shares[0],
            *[to_narrow(shares[k], k) for k in range(1, narrow_count)],
        ),
    )
    return (layer_out, new_state)


def solution(mesh):
    placed = (
        P("wide", None),
        P(None, ("wide", "narrow"), None),
        P(("wide", "narrow"), None, None),
        P(),
        P(None, ("wide", "narrow"), None),
        P(None, ("wide", "narrow")),
        P(("wide", "narrow")),
        P(("wide", "narrow"), None),
        P(),
        P(("wide", "narrow"), None),
        P(("wide", "narrow")),
        P(("wide", "narrow"), None),
        P(("wide", "narrow")),
        P(("wide", "narrow"), None),
        P(),
        P(None, ("wide", "narrow")),
        P(None, ("wide", "narrow")),
        P(("wide", "narrow"), None),
        P("wide", None),
        P("wide", None),
    )
    return jax.shard_map(
        on_device,
        mesh=mesh,
        in_specs=placed,
        out_specs=(P("wide", "narrow"), P(("wide", "narrow"), None, None)),
        check_vma=False,
    )
```

time: 348 us -> 135 us (0.39)
  waiting for transfers between devices: 253 us -> 50.7 us
  matrix products: 40.3 us -> 0 us
  Pallas kernels: 0 us -> 37.8 us
  starting transfers between devices: 3.76 us -> 29.5 us
  blocking collectives: 18.8 us -> 0 us
  between operations: 14.1 us -> 0.81 us
  other arithmetic: 11 us -> 1.55 us
  local copies, waits for them, and re-layouts: 6.43 us -> 14.1 us
    psum x2 -> x0, waiting for transfers between devices: 158 us -> none  [the longest x1 122 us: on_device(): selected = lax.psum(select_part, ('wide', 'narrow'))]
    reduce_scatter x2 -> x0, waiting for transfers between devices: 54.8 us -> none  [the longest x1 37.6 us: on_device(): lax.psum_scatter(jnp.einsum('cr,cd->rd', gated, out_weight, preferred_ele...]
    ppermute x0 -> x35, waiting for transfers between devices: none -> 50.7 us  [the longest x15 26.6 us: to_chip(): lax.ppermute(values, 'wide', [(i, i ^ 2 * k) for i in range(wide_count)])]
    dot_general x8 -> x0, matrix products: 40.3 us -> none  [the longest x1 19.9 us: on_device(): result = jnp.dot(inner, down_proj, preferred_element_type=jnp.float32)]
    pallas_call x0 -> x13, Pallas kernels: none -> 37.8 us  [the longest x1 28.6 us: on_device(): pl.pallas_call(functools.partial(expert_kernel, wide_count, wide_count //...]
    ppermute x0 -> x35, starting transfers between devices: none -> 29.5 us  [the longest x15 18.8 us: to_chip(): lax.ppermute(values, 'wide', [(i, i ^ 2 * k) for i in range(wide_count)])]
    all_gather x1 -> x0, waiting for transfers between devices: 24.5 us -> none  [on_device(): lax.all_gather(normed, 'wide', axis=0, tiled=True)]
    all_to_all x1 -> x0, blocking collectives: 18.8 us -> none  [on_device(): lax.all_to_all(outgoing, 'wide', split_axis=0, concat_axis=0, tiled=True)]
  transfers between devices with their start and end apart: 6 -> 35, of which waited for: 6 -> 22; matrix products, arithmetic and copies ran while one was open for 1% -> 3% of each run, Pallas kernels for 0% -> 0%
where the time goes in v1:
time: 135 us
  waiting for transfers between devices  50.7 us (38%)
  Pallas kernels  37.8 us (28%)
  starting transfers between devices  29.5 us (22%)
  local copies, waits for them, and re-layouts  14.1 us (10%)
  other arithmetic  1.55 us (1%)
    pallas_call x1, Pallas kernels, on_device(): pl.pallas_call(functools.partial(expert_kernel, wide_count, wide_count //...  28.6 us
    ppermute x15, waiting for transfers between devices, to_chip(): lax.ppermute(values, 'wide', [(i, i ^ 2 * k) for i in range(wide_count)])  26.6 us
    ppermute x15, starting transfers between devices, to_chip(): lax.ppermute(values, 'wide', [(i, i ^ 2 * k) for i in range(wide_count)])  18.8 us
    ppermute x8, waiting for transfers between devices, to_narrow(): lax.ppermute(values, 'narrow', [(i, i ^ k) for i in range(narrow_count)])  18.5 us
    unnamed x22, local copies, waits for them, and re-layouts  12.5 us
    pallas_call x12, Pallas kernels, kernel_call(): pl.pallas_call(body, out_shape=[jax.ShapeDtypeStruct(shape, dtype) for sh...  9.22 us
    ppermute x8, starting transfers between devices, to_narrow(): lax.ppermute(values, 'narrow', [(i, i ^ k) for i in range(narrow_count)])  9.04 us
    ppermute x12, waiting for transfers between devices, swap(): return lax.ppermute(values, 'wide', [(i, i ^ 1) for i in range(wide_count)])  5.56 us
  transfers between devices with their start and end apart: 35, of which 22 were waited for; matrix products, arithmetic and copies ran while one was open for 3% of the time, Pallas kernels for 0%

profile of v1, /device:TPU:0, one launch (start us, length us, event | category | flops | bytes accessed | tf_op | source)
XLA Modules:
  0.0 134.5 jit_solution(13793572985117086664)
XLA Ops:
  0.6 3.0 %collective-permute-start.1 = (bf16[16,4096]{1,0:T(8,128)(2,1)}, bf16[16,4096]{1,0:T(8,128)(2,1)S(1)}, u32[]{:S(2)}, u32[]{:S(2)}) collective-permute-start(bf16[16,4096]{1,0:T(8,128)(2,1)} %hidden.1), channel_id=1, source_target_pairs={{0,8},{4,12},{8,0},{12,4},{16,24},{20,28},{24,16},{28,20},{1,9},{5... | collective-permute-start | bytes 393224 | tf_op jit(solution)/shard_map/ppermute | solution.py:274
  3.6 1.5 %collective-permute-start.3 = (bf16[16,4096]{1,0:T(8,128)(2,1)}, bf16[16,4096]{1,0:T(8,128)(2,1)S(1)}, u32[]{:S(2)}, u32[]{:S(2)}) collective-permute-start(bf16[16,4096]{1,0:T(8,128)(2,1)} %hidden.1), channel_id=1, source_target_pairs={{0,16},{4,20},{8,24},{12,28},{16,0},{20,4},{24,8},{28,12},{1,17},{... | collective-permute-start | bytes 393224 | tf_op jit(solution)/shard_map/ppermute | solution.py:274
  5.2 2.7 %collective-permute-done.1.refs_2_ = bf16[16,4096]{1,0:T(8,128)(2,1)S(1)} collective-permute-done((bf16[16,4096]{1,0:T(8,128)(2,1)}, bf16[16,4096]{1,0:T(8,128)(2,1)S(1)}, u32[]{:S(2)}, u32[]{:S(2)}) %collective-permute-start.1) | collective-permute-done | bytes 131104 | tf_op jit(solution)/shard_map/ppermute | solution.py:274
  7.9 3.8 %collective-permute-done.3.refs_4_ = bf16[16,4096]{1,0:T(8,128)(2,1)S(1)} collective-permute-done((bf16[16,4096]{1,0:T(8,128)(2,1)}, bf16[16,4096]{1,0:T(8,128)(2,1)S(1)}, u32[]{:S(2)}, u32[]{:S(2)}) %collective-permute-start.3) | collective-permute-done | bytes 131104 | tf_op jit(solution)/shard_map/ppermute | solution.py:274
  13.2 2.2 %copy-done = bf16[2,256,4096]{2,1,0:T(8,128)(2,1)S(1)} copy-done((bf16[2,256,4096]{2,1,0:T(8,128)(2,1)S(1)}, bf16[2,256,4096]{2,1,0:T(8,128)(2,1)}, u32[]{:S(2)}) %copy-start) | copy-done | bytes 4194328
  15.3 0.9 copy-done.3
  16.3 0.9 copy-done.5
  17.2 0.9 copy-done.6
  18.8 3.6 %shard_map.203 = (f32[256,128]{1,0:T(8,128)S(1)}, f32[256,128]{1,0:T(8,128)S(1)}, bf16[144,128]{1,0:T(8,128)(2,1)S(1)}, bf16[144,128]{1,0:T(8,128)(2,1)S(1)}) custom-call(s32[2]{0:T(128)S(1)} %pad_add_fusion.place, bf16[16,4096]{1,0:T(8,128)(2,1)S(1)} %copy-done.3, bf16[16,4096]{1,0:T(8,128)(2,1)S(1)} %collective-permute-done.refs_1_, ...), custom_call_target="tpu_custom_call" | custom-call | tf_op jit(solution)/shard_map/pallas_call | solution.py:25
  22.8 0.9 collective-permute-done.7.refs_1_
  23.7 1.5 %collective-permute-start.10 = (bf16[144,128]{1,0:T(8,128)(2,1)S(1)}, bf16[144,128]{1,0:T(8,128)(2,1)S(1)}, u32[]{:S(2)}, u32[]{:S(2)}) collective-permute-start(bf16[144,128]{1,0:T(8,128)(2,1)S(1)} %shard_map.204.refs_0_), channel_id=1, source_target_pairs={{0,24},{4,28},{8,16},{12,20},{16,8},{20,12},{24,0},{28,4},{1,25},{... | collective-permute-start | bytes 110600 | tf_op jit(solution)/shard_map/ppermute | solution.py:274
  25.3 1.5 %collective-permute-start.8 = (bf16[144,128]{1,0:T(8,128)(2,1)S(1)}, bf16[144,128]{1,0:T(8,128)(2,1)S(1)}, u32[]{:S(2)}, u32[]{:S(2)}) collective-permute-start(bf16[144,128]{1,0:T(8,128)(2,1)S(1)} %shard_map.204.refs_0_), channel_id=1, source_target_pairs={{0,8},{4,12},{8,0},{12,4},{16,24},{20,28},{24,16},{28,20},{1,9},{5... | collective-permute-start | bytes 110600 | tf_op jit(solution)/shard_map/ppermute | solution.py:274
  27.3 1.7 %collective-permute-done.10.refs_3_ = bf16[144,128]{1,0:T(8,128)(2,1)S(1)} collective-permute-done((bf16[144,128]{1,0:T(8,128)(2,1)S(1)}, bf16[144,128]{1,0:T(8,128)(2,1)S(1)}, u32[]{:S(2)}, u32[]{:S(2)}) %collective-permute-start.10) | collective-permute-done | bytes 36896 | tf_op jit(solution)/shard_map/ppermute | solution.py:274
  29.2 1.5 %collective-permute-done.9.refs_2_ = bf16[144,128]{1,0:T(8,128)(2,1)S(1)} collective-permute-done((bf16[144,128]{1,0:T(8,128)(2,1)S(1)}, bf16[144,128]{1,0:T(8,128)(2,1)S(1)}, u32[]{:S(2)}, u32[]{:S(2)}) %collective-permute-start.9) | collective-permute-done | bytes 36896 | tf_op jit(solution)/shard_map/ppermute | solution.py:274
  30.8 1.6 %collective-permute-start.11 = (bf16[144,128]{1,0:T(8,128)(2,1)S(1)}, bf16[144,128]{1,0:T(8,128)(2,1)S(1)}, u32[]{:S(2)}, u32[]{:S(2)}) collective-permute-start(bf16[144,128]{1,0:T(8,128)(2,1)S(1)} %shard_map.205.refs_0_), channel_id=1, source_target_pairs={{0,1},{1,0},{2,3},{3,2},{4,5},{5,4},{6,7},{7,6},{8,9},{9,8},{10,11... | collective-permute-start | bytes 110600 | tf_op jit(solution)/shard_map/ppermute | solution.py:277
  32.4 2.6 %collective-permute-start.12 = (bf16[144,128]{1,0:T(8,128)(2,1)S(1)}, bf16[144,128]{1,0:T(8,128)(2,1)S(1)}, u32[]{:S(2)}, u32[]{:S(2)}) collective-permute-start(bf16[144,128]{1,0:T(8,128)(2,1)S(1)} %shard_map.205.refs_0_), channel_id=1, source_target_pairs={{0,2},{1,3},{2,0},{3,1},{4,6},{5,7},{6,4},{7,5},{8,10},{9,11},{10,... | collective-permute-start | bytes 110600 | tf_op jit(solution)/shard_map/ppermute | solution.py:277
  35.2 2.8 %collective-permute-done.12.refs_2_ = bf16[144,128]{1,0:T(8,128)(2,1)S(1)} collective-permute-done((bf16[144,128]{1,0:T(8,128)(2,1)S(1)}, bf16[144,128]{1,0:T(8,128)(2,1)S(1)}, u32[]{:S(2)}, u32[]{:S(2)}) %collective-permute-start.12) | collective-permute-done | bytes 36896 | tf_op jit(solution)/shard_map/ppermute | solution.py:277
  38.0 2.8 %collective-permute-done.13.refs_3_ = bf16[144,128]{1,0:T(8,128)(2,1)S(1)} collective-permute-done((bf16[144,128]{1,0:T(8,128)(2,1)S(1)}, bf16[144,128]{1,0:T(8,128)(2,1)S(1)}, u32[]{:S(2)}, u32[]{:S(2)}) %collective-permute-start.13) | collective-permute-done | bytes 36896 | tf_op jit(solution)/shard_map/ppermute | solution.py:277
  41.7 0.8 copy.36.step_gain
  43.1 1.6 %copy-done.1 = bf16[256,4096]{1,0:T(8,128)(2,1)S(1)} copy-done((bf16[256,4096]{1,0:T(8,128)(2,1)S(1)}, bf16[256,4096]{1,0:T(8,128)(2,1)}, u32[]{:S(2)}) %copy-start.1) | copy-done | bytes 2097176
  44.7 1.2 copy-done.2
  45.9 0.9 copy-done.7
  46.8 3.3 %shard_map.207 = (bf16[256,16,128]{2,1,0:T(8,128)(2,1)}, bf16[64,4096]{1,0:T(8,128)(2,1)S(1)}, bf16[64,4096]{1,0:T(8,128)(2,1)S(1)}) custom-call(s32[2]{0:T(128)S(1)} %pad_add_fusion.place, bf16[144,128]{1,0:T(8,128)(2,1)S(1)} %shard_map.206.own_half, bf16[144,128]{1,0:T(8,128)(2,1)S(1)} %collective-permute-done.14.other_half, f32[256,1]{1,0:T(8,128)S(1)} %copy.36.step_gain, ...), custom_call_target="tpu_custom_call" | custom-call | tf_op jit(solution)/shard_map/pallas_call | solution.py:25
  50.6 1.5 %collective-permute-done.15.got = bf16[64,4096]{1,0:T(8,128)(2,1)S(1)} collective-permute-done((bf16[64,4096]{1,0:T(8,128)(2,1)S(1)}, bf16[64,4096]{1,0:T(8,128)(2,1)S(1)}, u32[]{:S(2)}, u32[]{:S(2)}) %collective-permute-start.15) | collective-permute-done | bytes 524320 | tf_op jit(solution)/shard_map/ppermute | solution.py:271
  52.9 1.0 collective-permute-start.17
  53.9 1.9 %collective-permute-start.18 = (bf16[16,4096]{1,0:T(8,128)(2,1)S(1)}, bf16[16,4096]{1,0:T(8,128)(2,1)S(1)}, u32[]{:S(2)}, u32[]{:S(2)}) collective-permute-start(bf16[16,4096]{1,0:T(8,128)(2,1)S(1)} %get-tuple-element.32), channel_id=1, source_target_pairs={{0,24},{4,28},{8,16},{12,20},{16,8},{20,12},{24,0},{28,4},{1,25},{... | collective-permute-start | bytes 393224 | tf_op jit(solution)/shard_map/ppermute | solution.py:274
  55.9 2.8 %collective-permute-done.16.refs_1_ = bf16[16,4096]{1,0:T(8,128)(2,1)S(1)} collective-permute-done((bf16[16,4096]{1,0:T(8,128)(2,1)S(1)}, bf16[16,4096]{1,0:T(8,128)(2,1)S(1)}, u32[]{:S(2)}, u32[]{:S(2)}) %collective-permute-start.16) | collective-permute-done | bytes 131104 | tf_op jit(solution)/shard_map/ppermute | solution.py:274
  58.7 2.5 %collective-permute-done.17.refs_2_ = bf16[16,4096]{1,0:T(8,128)(2,1)S(1)} collective-permute-done((bf16[16,4096]{1,0:T(8,128)(2,1)S(1)}, bf16[16,4096]{1,0:T(8,128)(2,1)S(1)}, u32[]{:S(2)}, u32[]{:S(2)}) %collective-permute-start.17) | collective-permute-done | bytes 131104 | tf_op jit(solution)/shard_map/ppermute | solution.py:274
  61.4 5.0 %collective-permute-done.19.refs_1_ = bf16[16,4096]{1,0:T(8,128)(2,1)S(1)} collective-permute-done((bf16[16,4096]{1,0:T(8,128)(2,1)S(1)}, bf16[16,4096]{1,0:T(8,128)(2,1)S(1)}, u32[]{:S(2)}, u32[]{:S(2)}) %collective-permute-start.19) | collective-permute-done | bytes 131104 | tf_op jit(solution)/shard_map/ppermute | solution.py:277
  67.9 5.5 %collective-permute-done.20.got = bf16[16,4096]{1,0:T(8,128)(2,1)S(1)} collective-permute-done((bf16[16,4096]{1,0:T(8,128)(2,1)S(1)}, bf16[16,4096]{1,0:T(8,128)(2,1)S(1)}, u32[]{:S(2)}, u32[]{:S(2)}) %collective-permute-start.20) | collective-permute-done | bytes 131104 | tf_op jit(solution)/shard_map/ppermute | solution.py:277
  73.4 0.9 copy-done.4
  74.4 1.3 collective-permute-start.21
  76.3 1.7 %collective-permute-start.23 = (bf16[16,4224]{1,0:T(8,128)(2,1)S(1)}, bf16[16,4224]{1,0:T(8,128)(2,1)S(1)}, u32[]{:S(2)}, u32[]{:S(2)}) collective-permute-start(bf16[16,4224]{1,0:T(8,128)(2,1)S(1)} %shard_map.211.refs_0_.residual), channel_id=1, source_target_pairs={{0,24},{4,28},{8,16},{12,20},{16,8},{20,12},{24,0},{28,4},{1,25},{... | collective-permute-start | bytes 405512 | tf_op jit(solution)/shard_map/ppermute | solution.py:274
  78.0 2.5 %collective-permute-done.21.refs_1_ = bf16[16,4224]{1,0:T(8,128)(2,1)S(1)} collective-permute-done((bf16[16,4224]{1,0:T(8,128)(2,1)S(1)}, bf16[16,4224]{1,0:T(8,128)(2,1)S(1)}, u32[]{:S(2)}, u32[]{:S(2)}) %collective-permute-start.21) | collective-permute-done | bytes 135200 | tf_op jit(solution)/shard_map/ppermute | solution.py:274
  80.5 1.2 collective-permute-done.22.refs_2_
  81.7 1.4 %collective-permute-done.23.refs_3_ = bf16[16,4224]{1,0:T(8,128)(2,1)S(1)} collective-permute-done((bf16[16,4224]{1,0:T(8,128)(2,1)S(1)}, bf16[16,4224]{1,0:T(8,128)(2,1)S(1)}, u32[]{:S(2)}, u32[]{:S(2)}) %collective-permute-start.23) | collective-permute-done | bytes 135200 | tf_op jit(solution)/shard_map/ppermute | solution.py:274
  83.1 1.3 collective-permute-done.27.refs_7_
  85.2 28.6 %shard_map.212 = (bf16[64,4096]{1,0:T(8,128)(2,1)S(1)}, bf16[64,4096]{1,0:T(8,128)(2,1)S(1)}) custom-call(s32[2]{0:T(128)S(1)} %pad_add_fusion.place, bf16[16,4224]{1,0:T(8,128)(2,1)S(1)} %shard_map.211.refs_0_.residual, bf16[16,4224]{1,0:T(8,128)(2,1)S(1)} %collective-permute-done.21.refs_1_, bf16[16,4224]{1,0:T(8,128)(2,1)S(1)} %collective-permute-done.22.refs_2_, ...), custom_call_target="tpu_custom_call" | custom-call | tf_op jit(solution)/shard_map/pallas_call | solution.py:357
  114.0 1.8 %collective-permute-done.28.got = bf16[64,4096]{1,0:T(8,128)(2,1)S(1)} collective-permute-done((bf16[64,4096]{1,0:T(8,128)(2,1)S(1)}, bf16[64,4096]{1,0:T(8,128)(2,1)S(1)}, u32[]{:S(2)}, u32[]{:S(2)}) %collective-permute-start.28) | collective-permute-done | bytes 524320 | tf_op jit(solution)/shard_map/ppermute | solution.py:271
  115.9 1.6 %collective-permute-start.29 = (bf16[16,4096]{1,0:T(8,128)(2,1)S(1)}, bf16[16,4096]{1,0:T(8,128)(2,1)S(1)}, u32[]{:S(2)}, u32[]{:S(2)}) collective-permute-start(bf16[16,4096]{1,0:T(8,128)(2,1)S(1)} %get-tuple-element.36), channel_id=1, source_target_pairs={{0,8},{4,12},{8,0},{12,4},{16,24},{20,28},{24,16},{28,20},{1,9},{5... | collective-permute-start | bytes 393224 | tf_op jit(solution)/shard_map/ppermute | solution.py:274
  117.4 1.0 collective-permute-start.30
  118.4 1.0 collective-permute-start.31
  119.4 2.2 %collective-permute-done.29.refs_1_ = bf16[16,4096]{1,0:T(8,128)(2,1)S(1)} collective-permute-done((bf16[16,4096]{1,0:T(8,128)(2,1)S(1)}, bf16[16,4096]{1,0:T(8,128)(2,1)S(1)}, u32[]{:S(2)}, u32[]{:S(2)}) %collective-permute-start.29) | collective-permute-done | bytes 131104 | tf_op jit(solution)/shard_map/ppermute | solution.py:274
  121.7 4.0 %collective-permute-done.30.refs_2_ = bf16[16,4096]{1,0:T(8,128)(2,1)S(1)} collective-permute-done((bf16[16,4096]{1,0:T(8,128)(2,1)S(1)}, bf16[16,4096]{1,0:T(8,128)(2,1)S(1)}, u32[]{:S(2)}, u32[]{:S(2)}) %collective-permute-start.30) | collective-permute-done | bytes 131104 | tf_op jit(solution)/shard_map/ppermute | solution.py:274
  126.4 1.2 collective-permute-start.33
  127.6 3.1 %collective-permute-start.34 = (bf16[16,1024]{1,0:T(8,128)(2,1)S(1)}, bf16[16,1024]{1,0:T(8,128)(2,1)S(1)}, u32[]{:S(2)}, u32[]{:S(2)}) collective-permute-start(bf16[16,1024]{1,0:T(8,128)(2,1)S(1)} %get-tuple-element.42), channel_id=1, source_target_pairs={{0,3},{1,2},{2,1},{3,0},{4,7},{5,6},{6,5},{7,4},{8,11},{9,10},{10,... | collective-permute-start | bytes 98312 | tf_op jit(solution)/shard_map/ppermute | solution.py:277
  131.3 2.0 %collective-permute-done.34.refs_3_ = bf16[16,1024]{1,0:T(8,128)(2,1)S(1)} collective-permute-done((bf16[16,1024]{1,0:T(8,128)(2,1)S(1)}, bf16[16,1024]{1,0:T(8,128)(2,1)S(1)}, u32[]{:S(2)}, u32[]{:S(2)}) %collective-permute-start.34) | collective-permute-done | bytes 32800 | tf_op jit(solution)/shard_map/ppermute | solution.py:277
  133.3 1.2 shard_map.215
  (64 shorter events, 11.2 us)
Async XLA Ops:
  0.6 7.2 %collective-permute-start.1 = (bf16[16,4096]{1,0:T(8,128)(2,1)}, bf16[16,4096]{1,0:T(8,128)(2,1)S(1)}, u32[]{:S(2)}, u32[]{:S(2)}) collective-permute-start(bf16[16,4096]{1,0:T(8,128)(2,1)} %hidden.1), channel_id=1, source_target_pairs={{0,8},{4,12},{8,0},{12,4},{16,24},{20,28},{24,16},{28,20},{1,9},{5... | collective-permute-start | bytes 393224 | tf_op jit(solution)/shard_map/ppermute | solution.py:274
  3.6 8.0 %collective-permute-start.3 = (bf16[16,4096]{1,0:T(8,128)(2,1)}, bf16[16,4096]{1,0:T(8,128)(2,1)S(1)}, u32[]{:S(2)}, u32[]{:S(2)}) collective-permute-start(bf16[16,4096]{1,0:T(8,128)(2,1)} %hidden.1), channel_id=1, source_target_pairs={{0,16},{4,20},{8,24},{12,28},{16,0},{20,4},{24,8},{28,12},{1,17},{... | collective-permute-start | bytes 393224 | tf_op jit(solution)/shard_map/ppermute | solution.py:274
  5.2 6.5 %collective-permute-start.5 = (bf16[16,4096]{1,0:T(8,128)(2,1)}, bf16[16,4096]{1,0:T(8,128)(2,1)S(1)}, u32[]{:S(2)}, u32[]{:S(2)}) collective-permute-start(bf16[16,4096]{1,0:T(8,128)(2,1)} %hidden.1), channel_id=1, source_target_pairs={{0,24},{4,28},{8,16},{12,20},{16,8},{20,12},{24,0},{28,4},{1,25},{... | collective-permute-start | bytes 393224 | tf_op jit(solution)/shard_map/ppermute | solution.py:274
  5.2 7.9 %collective-permute-start = (bf16[16,4096]{1,0:T(8,128)(2,1)}, bf16[16,4096]{1,0:T(8,128)(2,1)S(1)}, u32[]{:S(2)}, u32[]{:S(2)}) collective-permute-start(bf16[16,4096]{1,0:T(8,128)(2,1)} %hidden.1), channel_id=1, source_target_pairs={{0,4},{4,0},{8,12},{12,8},{16,20},{20,16},{24,28},{28,24},{1,5},{5... | collective-permute-start | bytes 393224 | tf_op jit(solution)/shard_map/ppermute | solution.py:271
  7.9 5.3 %collective-permute-start.2 = (bf16[16,4096]{1,0:T(8,128)(2,1)S(1)}, bf16[16,4096]{1,0:T(8,128)(2,1)S(1)}, u32[]{:S(2)}, u32[]{:S(2)}) collective-permute-start(bf16[16,4096]{1,0:T(8,128)(2,1)S(1)} %collective-permute-done.1.refs_2_), channel_id=1, source_target_pairs={{0,4},{4,0},{8,12},{12,8},{16,20},{20,16},{24,28},{28,24},{1,5},{5... | collective-permute-start | bytes 393224 | tf_op jit(solution)/shard_map/ppermute | solution.py:271
  11.6 1.5 %collective-permute-start.4 = (bf16[16,4096]{1,0:T(8,128)(2,1)S(1)}, bf16[16,4096]{1,0:T(8,128)(2,1)S(1)}, u32[]{:S(2)}, u32[]{:S(2)}) collective-permute-start(bf16[16,4096]{1,0:T(8,128)(2,1)S(1)} %collective-permute-done.3.refs_4_), channel_id=1, source_target_pairs={{0,4},{4,0},{8,12},{12,8},{16,20},{20,16},{24,28},{28,24},{1,5},{5... | collective-permute-start | bytes 393224 | tf_op jit(solution)/shard_map/ppermute | solution.py:271
  11.6 1.5 %collective-permute-start.6 = (bf16[16,4096]{1,0:T(8,128)(2,1)S(1)}, bf16[16,4096]{1,0:T(8,128)(2,1)S(1)}, u32[]{:S(2)}, u32[]{:S(2)}) collective-permute-start(bf16[16,4096]{1,0:T(8,128)(2,1)S(1)} %collective-permute-done.5.refs_6_), channel_id=1, source_target_pairs={{0,4},{4,0},{8,12},{12,8},{16,20},{20,16},{24,28},{28,24},{1,5},{5... | collective-permute-start | bytes 393224 | tf_op jit(solution)/shard_map/ppermute | solution.py:271
  13.2 2.2 %copy-start = (bf16[2,256,4096]{2,1,0:T(8,128)(2,1)S(1)}, bf16[2,256,4096]{2,1,0:T(8,128)(2,1)}, u32[]{:S(2)}) copy-start(bf16[2,256,4096]{2,1,0:T(8,128)(2,1)} %refs_9_.2) | copy-start | bytes 12582916
  15.3 0.9 copy-start.3
  16.3 0.9 copy-start.5
  17.2 0.9 copy-start.6
  18.1 0.7 copy-start.8
  22.4 1.3 collective-permute-start.7
  23.7 5.3 %collective-permute-start.10 = (bf16[144,128]{1,0:T(8,128)(2,1)S(1)}, bf16[144,128]{1,0:T(8,128)(2,1)S(1)}, u32[]{:S(2)}, u32[]{:S(2)}) collective-permute-start(bf16[144,128]{1,0:T(8,128)(2,1)S(1)} %shard_map.204.refs_0_), channel_id=1, source_target_pairs={{0,24},{4,28},{8,16},{12,20},{16,8},{20,12},{24,0},{28,4},{1,25},{... | collective-permute-start | bytes 110600 | tf_op jit(solution)/shard_map/ppermute | solution.py:274
  25.3 4.0 %collective-permute-start.8 = (bf16[144,128]{1,0:T(8,128)(2,1)S(1)}, bf16[144,128]{1,0:T(8,128)(2,1)S(1)}, u32[]{:S(2)}, u32[]{:S(2)}) collective-permute-start(bf16[144,128]{1,0:T(8,128)(2,1)S(1)} %shard_map.204.refs_0_), channel_id=1, source_target_pairs={{0,8},{4,12},{8,0},{12,4},{16,24},{20,28},{24,16},{28,20},{1,9},{5... | collective-permute-start | bytes 110600 | tf_op jit(solution)/shard_map/ppermute | solution.py:274
  26.8 4.0 %collective-permute-start.9 = (bf16[144,128]{1,0:T(8,128)(2,1)S(1)}, bf16[144,128]{1,0:T(8,128)(2,1)S(1)}, u32[]{:S(2)}, u32[]{:S(2)}) collective-permute-start(bf16[144,128]{1,0:T(8,128)(2,1)S(1)} %shard_map.204.refs_0_), channel_id=1, source_target_pairs={{0,16},{4,20},{8,24},{12,28},{16,0},{20,4},{24,8},{28,12},{1,17},{... | collective-permute-start | bytes 110600 | tf_op jit(solution)/shard_map/ppermute | solution.py:274
  30.8 4.5 %collective-permute-start.11 = (bf16[144,128]{1,0:T(8,128)(2,1)S(1)}, bf16[144,128]{1,0:T(8,128)(2,1)S(1)}, u32[]{:S(2)}, u32[]{:S(2)}) collective-permute-start(bf16[144,128]{1,0:T(8,128)(2,1)S(1)} %shard_map.205.refs_0_), channel_id=1, source_target_pairs={{0,1},{1,0},{2,3},{3,2},{4,5},{5,4},{6,7},{7,6},{8,9},{9,8},{10,11... | collective-permute-start | bytes 110600 | tf_op jit(solution)/shard_map/ppermute | solution.py:277
  32.4 5.6 %collective-permute-start.12 = (bf16[144,128]{1,0:T(8,128)(2,1)S(1)}, bf16[144,128]{1,0:T(8,128)(2,1)S(1)}, u32[]{:S(2)}, u32[]{:S(2)}) collective-permute-start(bf16[144,128]{1,0:T(8,128)(2,1)S(1)} %shard_map.205.refs_0_), channel_id=1, source_target_pairs={{0,2},{1,3},{2,0},{3,1},{4,6},{5,7},{6,4},{7,5},{8,10},{9,11},{10,... | collective-permute-start | bytes 110600 | tf_op jit(solution)/shard_map/ppermute | solution.py:277
  35.0 5.8 %collective-permute-start.13 = (bf16[144,128]{1,0:T(8,128)(2,1)S(1)}, bf16[144,128]{1,0:T(8,128)(2,1)S(1)}, u32[]{:S(2)}, u32[]{:S(2)}) collective-permute-start(bf16[144,128]{1,0:T(8,128)(2,1)S(1)} %shard_map.205.refs_0_), channel_id=1, source_target_pairs={{0,3},{1,2},{2,1},{3,0},{4,7},{5,6},{6,5},{7,4},{8,11},{9,10},{10,... | collective-permute-start | bytes 110600 | tf_op jit(solution)/shard_map/ppermute | solution.py:277
  40.8 1.7 %collective-permute-start.14 = (bf16[144,128]{1,0:T(8,128)(2,1)S(1)}, bf16[144,128]{1,0:T(8,128)(2,1)S(1)}, u32[]{:S(2)}, u32[]{:S(2)}) collective-permute-start(bf16[144,128]{1,0:T(8,128)(2,1)S(1)} %shard_map.206.own_half), channel_id=1, source_target_pairs={{0,4},{4,0},{8,12},{12,8},{16,20},{20,16},{24,28},{28,24},{1,5},{5... | collective-permute-start | bytes 110600 | tf_op jit(solution)/shard_map/ppermute | solution.py:271
  43.1 1.6 %copy-start.1 = (bf16[256,4096]{1,0:T(8,128)(2,1)S(1)}, bf16[256,4096]{1,0:T(8,128)(2,1)}, u32[]{:S(2)}) copy-start(bf16[256,4096]{1,0:T(8,128)(2,1)} %out_weight.1) | copy-start | bytes 6291460
  44.7 1.2 copy-start.2
  45.9 0.9 copy-start.7
  50.1 2.0 %collective-permute-start.15 = (bf16[64,4096]{1,0:T(8,128)(2,1)S(1)}, bf16[64,4096]{1,0:T(8,128)(2,1)S(1)}, u32[]{:S(2)}, u32[]{:S(2)}) collective-permute-start(bf16[64,4096]{1,0:T(8,128)(2,1)S(1)} %get-tuple-element.28), channel_id=1, source_target_pairs={{0,4},{4,0},{8,12},{12,8},{16,20},{20,16},{24,28},{28,24},{1,5},{5... | collective-permute-start | bytes 1572872 | tf_op jit(solution)/shard_map/ppermute | solution.py:271
  52.3 6.4 %collective-permute-start.16 = (bf16[16,4096]{1,0:T(8,128)(2,1)S(1)}, bf16[16,4096]{1,0:T(8,128)(2,1)S(1)}, u32[]{:S(2)}, u32[]{:S(2)}) collective-permute-start(bf16[16,4096]{1,0:T(8,128)(2,1)S(1)} %get-tuple-element.30), channel_id=1, source_target_pairs={{0,8},{4,12},{8,0},{12,4},{16,24},{20,28},{24,16},{28,20},{1,9},{5... | collective-permute-start | bytes 393224 | tf_op jit(solution)/shard_map/ppermute | solution.py:274
  52.9 8.3 %collective-permute-start.17 = (bf16[16,4096]{1,0:T(8,128)(2,1)S(1)}, bf16[16,4096]{1,0:T(8,128)(2,1)S(1)}, u32[]{:S(2)}, u32[]{:S(2)}) collective-permute-start(bf16[16,4096]{1,0:T(8,128)(2,1)S(1)} %get-tuple-element.31), channel_id=1, source_target_pairs={{0,16},{4,20},{8,24},{12,28},{16,0},{20,4},{24,8},{28,12},{1,17},{... | collective-permute-start | bytes 393224 | tf_op jit(solution)/shard_map/ppermute | solution.py:274
  53.9 7.3 %collective-permute-start.18 = (bf16[16,4096]{1,0:T(8,128)(2,1)S(1)}, bf16[16,4096]{1,0:T(8,128)(2,1)S(1)}, u32[]{:S(2)}, u32[]{:S(2)}) collective-permute-start(bf16[16,4096]{1,0:T(8,128)(2,1)S(1)} %get-tuple-element.32), channel_id=1, source_target_pairs={{0,24},{4,28},{8,16},{12,20},{16,8},{20,12},{24,0},{28,4},{1,25},{... | collective-permute-start | bytes 393224 | tf_op jit(solution)/shard_map/ppermute | solution.py:274
  61.3 5.0 %collective-permute-start.19 = (bf16[16,4096]{1,0:T(8,128)(2,1)S(1)}, bf16[16,4096]{1,0:T(8,128)(2,1)S(1)}, u32[]{:S(2)}, u32[]{:S(2)}) collective-permute-start(bf16[16,4096]{1,0:T(8,128)(2,1)S(1)} %shard_map.209.refs_0_), channel_id=1, source_target_pairs={{0,1},{1,0},{2,3},{3,2},{4,5},{5,4},{6,7},{7,6},{8,9},{9,8},{10,11... | collective-permute-start | bytes 393224 | tf_op jit(solution)/shard_map/ppermute | solution.py:277
  66.4 7.0 %collective-permute-start.20 = (bf16[16,4096]{1,0:T(8,128)(2,1)S(1)}, bf16[16,4096]{1,0:T(8,128)(2,1)S(1)}, u32[]{:S(2)}, u32[]{:S(2)}) collective-permute-start(bf16[16,4096]{1,0:T(8,128)(2,1)S(1)} %shard_map.210.mine), channel_id=1, source_target_pairs={{0,2},{1,3},{2,0},{3,1},{4,6},{5,7},{6,4},{7,5},{8,10},{9,11},{10,... | collective-permute-start | bytes 393224 | tf_op jit(solution)/shard_map/ppermute | solution.py:277
  73.4 0.9 copy-start.4
  74.4 6.1 %collective-permute-start.21 = (bf16[16,4224]{1,0:T(8,128)(2,1)S(1)}, bf16[16,4224]{1,0:T(8,128)(2,1)S(1)}, u32[]{:S(2)}, u32[]{:S(2)}) collective-permute-start(bf16[16,4224]{1,0:T(8,128)(2,1)S(1)} %shard_map.211.refs_0_.residual), channel_id=1, source_target_pairs={{0,8},{4,12},{8,0},{12,4},{16,24},{20,28},{24,16},{28,20},{1,9},{5... | collective-permute-start | bytes 405512 | tf_op jit(solution)/shard_map/ppermute | solution.py:274
  75.7 6.0 %collective-permute-start.22 = (bf16[16,4224]{1,0:T(8,128)(2,1)S(1)}, bf16[16,4224]{1,0:T(8,128)(2,1)S(1)}, u32[]{:S(2)}, u32[]{:S(2)}) collective-permute-start(bf16[16,4224]{1,0:T(8,128)(2,1)S(1)} %shard_map.211.refs_0_.residual), channel_id=1, source_target_pairs={{0,16},{4,20},{8,24},{12,28},{16,0},{20,4},{24,8},{28,12},{1,17},{... | collective-permute-start | bytes 405512 | tf_op jit(solution)/shard_map/ppermute | solution.py:274
  76.3 6.8 %collective-permute-start.23 = (bf16[16,4224]{1,0:T(8,128)(2,1)S(1)}, bf16[16,4224]{1,0:T(8,128)(2,1)S(1)}, u32[]{:S(2)}, u32[]{:S(2)}) collective-permute-start(bf16[16,4224]{1,0:T(8,128)(2,1)S(1)} %shard_map.211.refs_0_.residual), channel_id=1, source_target_pairs={{0,24},{4,28},{8,16},{12,20},{16,8},{20,12},{24,0},{28,4},{1,25},{... | collective-permute-start | bytes 405512 | tf_op jit(solution)/shard_map/ppermute | solution.py:274
  77.9 5.2 %collective-permute-start.24 = (bf16[16,4224]{1,0:T(8,128)(2,1)S(1)}, bf16[16,4224]{1,0:T(8,128)(2,1)S(1)}, u32[]{:S(2)}, u32[]{:S(2)}) collective-permute-start(bf16[16,4224]{1,0:T(8,128)(2,1)S(1)} %shard_map.211.refs_0_.residual), channel_id=1, source_target_pairs={{0,4},{4,0},{8,12},{12,8},{16,20},{20,16},{24,28},{28,24},{1,5},{5... | collective-permute-start | bytes 405512 | tf_op jit(solution)/shard_map/ppermute | solution.py:271
  80.5 2.6 %collective-permute-start.25 = (bf16[16,4224]{1,0:T(8,128)(2,1)S(1)}, bf16[16,4224]{1,0:T(8,128)(2,1)S(1)}, u32[]{:S(2)}, u32[]{:S(2)}) collective-permute-start(bf16[16,4224]{1,0:T(8,128)(2,1)S(1)} %collective-permute-done.21.refs_1_), channel_id=1, source_target_pairs={{0,4},{4,0},{8,12},{12,8},{16,20},{20,16},{24,28},{28,24},{1,5},{5... | collective-permute-start | bytes 405512 | tf_op jit(solution)/shard_map/ppermute | solution.py:271
  81.7 1.5 %collective-permute-start.26 = (bf16[16,4224]{1,0:T(8,128)(2,1)S(1)}, bf16[16,4224]{1,0:T(8,128)(2,1)S(1)}, u32[]{:S(2)}, u32[]{:S(2)}) collective-permute-start(bf16[16,4224]{1,0:T(8,128)(2,1)S(1)} %collective-permute-done.22.refs_2_), channel_id=1, source_target_pairs={{0,4},{4,0},{8,12},{12,8},{16,20},{20,16},{24,28},{28,24},{1,5},{5... | collective-permute-start | bytes 405512 | tf_op jit(solution)/shard_map/ppermute | solution.py:271
  83.1 1.4 %collective-permute-start.27 = (bf16[16,4224]{1,0:T(8,128)(2,1)S(1)}, bf16[16,4224]{1,0:T(8,128)(2,1)S(1)}, u32[]{:S(2)}, u32[]{:S(2)}) collective-permute-start(bf16[16,4224]{1,0:T(8,128)(2,1)S(1)} %collective-permute-done.23.refs_3_), channel_id=1, source_target_pairs={{0,4},{4,0},{8,12},{12,8},{16,20},{20,16},{24,28},{28,24},{1,5},{5... | collective-permute-start | bytes 405512 | tf_op jit(solution)/shard_map/ppermute | solution.py:271
  84.5 0.7 copy-start.9
  113.8 2.0 %collective-permute-start.28 = (bf16[64,4096]{1,0:T(8,128)(2,1)S(1)}, bf16[64,4096]{1,0:T(8,128)(2,1)S(1)}, u32[]{:S(2)}, u32[]{:S(2)}) collective-permute-start(bf16[64,4096]{1,0:T(8,128)(2,1)S(1)} %get-tuple-element.34), channel_id=1, source_target_pairs={{0,4},{4,0},{8,12},{12,8},{16,20},{20,16},{24,28},{28,24},{1,5},{5... | collective-permute-start | bytes 1572872 | tf_op jit(solution)/shard_map/ppermute | solution.py:271
  115.9 5.8 %collective-permute-start.29 = (bf16[16,4096]{1,0:T(8,128)(2,1)S(1)}, bf16[16,4096]{1,0:T(8,128)(2,1)S(1)}, u32[]{:S(2)}, u32[]{:S(2)}) collective-permute-start(bf16[16,4096]{1,0:T(8,128)(2,1)S(1)} %get-tuple-element.36), channel_id=1, source_target_pairs={{0,8},{4,12},{8,0},{12,4},{16,24},{20,28},{24,16},{28,20},{1,9},{5... | collective-permute-start | bytes 393224 | tf_op jit(solution)/shard_map/ppermute | solution.py:274
  117.4 8.3 %collective-permute-start.30 = (bf16[16,4096]{1,0:T(8,128)(2,1)S(1)}, bf16[16,4096]{1,0:T(8,128)(2,1)S(1)}, u32[]{:S(2)}, u32[]{:S(2)}) collective-permute-start(bf16[16,4096]{1,0:T(8,128)(2,1)S(1)} %get-tuple-element.37), channel_id=1, source_target_pairs={{0,16},{4,20},{8,24},{12,28},{16,0},{20,4},{24,8},{28,12},{1,17},{... | collective-permute-start | bytes 393224 | tf_op jit(solution)/shard_map/ppermute | solution.py:274
  118.4 7.2 %collective-permute-start.31 = (bf16[16,4096]{1,0:T(8,128)(2,1)S(1)}, bf16[16,4096]{1,0:T(8,128)(2,1)S(1)}, u32[]{:S(2)}, u32[]{:S(2)}) collective-permute-start(bf16[16,4096]{1,0:T(8,128)(2,1)S(1)} %get-tuple-element.38), channel_id=1, source_target_pairs={{0,24},{4,28},{8,16},{12,20},{16,8},{20,12},{24,0},{28,4},{1,25},{... | collective-permute-start | bytes 393224 | tf_op jit(solution)/shard_map/ppermute | solution.py:274
  126.3 4.5 %collective-permute-start.32 = (bf16[16,1024]{1,0:T(8,128)(2,1)S(1)}, bf16[16,1024]{1,0:T(8,128)(2,1)S(1)}, u32[]{:S(2)}, u32[]{:S(2)}) collective-permute-start(bf16[16,1024]{1,0:T(8,128)(2,1)S(1)} %get-tuple-element.40), channel_id=1, source_target_pairs={{0,1},{1,0},{2,3},{3,2},{4,5},{5,4},{6,7},{7,6},{8,9},{9,8},{10,11... | collective-permute-start | bytes 98312 | tf_op jit(solution)/shard_map/ppermute | solution.py:277
  126.4 5.0 %collective-permute-start.33 = (bf16[16,1024]{1,0:T(8,128)(2,1)S(1)}, bf16[16,1024]{1,0:T(8,128)(2,1)S(1)}, u32[]{:S(2)}, u32[]{:S(2)}) collective-permute-start(bf16[16,1024]{1,0:T(8,128)(2,1)S(1)} %get-tuple-element.41), channel_id=1, source_target_pairs={{0,2},{1,3},{2,0},{3,1},{4,6},{5,7},{6,4},{7,5},{8,10},{9,11},{10,... | collective-permute-start | bytes 98312 | tf_op jit(solution)/shard_map/ppermute | solution.py:277
  127.6 5.7 %collective-permute-start.34 = (bf16[16,1024]{1,0:T(8,128)(2,1)S(1)}, bf16[16,1024]{1,0:T(8,128)(2,1)S(1)}, u32[]{:S(2)}, u32[]{:S(2)}) collective-permute-start(bf16[16,1024]{1,0:T(8,128)(2,1)S(1)} %get-tuple-element.42), channel_id=1, source_target_pairs={{0,3},{1,2},{2,1},{3,0},{4,7},{5,6},{6,5},{7,4},{8,11},{9,10},{10,... | collective-permute-start | bytes 98312 | tf_op jit(solution)/shard_map/ppermute | solution.py:277

commit v2 on v1

--- a/solution.py
+++ b/solution.py
@@ -11,6 +11,7 @@
 EPS = 1e-06
 MIB = 1 << 20
 LANES = 128
+PIECES = 4
 F32 = jnp.float32
 BF16 = jnp.bfloat16
 
@@ -19,17 +20,48 @@
     return values.astype(F32)
 
 
-def kernel_call(body, outs, args, scalars=1, scratch=(), limit=32):
+def kernel_call(body, outs, args, scalars=1, far=0, scratch=(), limit=16, cost=None):
     smem = pl.BlockSpec(memory_space=pltpu.SMEM)
     vmem = pl.BlockSpec(memory_space=pltpu.VMEM)
+    hbm = pl.BlockSpec(memory_space=pltpu.HBM)
+    near = len(args) - far
+    stay = [pltpu.with_memory_space_constraint(item, pltpu.HBM) for item in args[near:]]
+    args = (*args[:near], *stay)
     return pl.pallas_call(
         body,
         out_shape=[jax.ShapeDtypeStruct(shape, dtype) for shape, dtype in outs],
-        in_specs=[smem] * scalars + [vmem] * (len(args) - scalars),
+        in_specs=[smem] * scalars + [vmem] * (len(args) - scalars - far) + [hbm] * far,
         out_specs=[vmem] * len(outs),
         scratch_shapes=scratch,
         compiler_params=pltpu.CompilerParams(vmem_limit_bytes=limit * MIB),
+        cost_estimate=cost,
     )(*args)
+
+
+def start_copies(pairs, sems):
+    copies = [pltpu.make_async_copy(src, dst, sems.at[i]) for i, (src, dst) in enumerate(pairs)]
+    for copy in copies:
+        copy.start()
+    return copies
+
+
+def finish(copies):
+    for copy in copies:
+        copy.wait()
+
+
+def pieces(source, target, start):
+    size = target.shape[0] // PIECES
+    return [
+        (source.at[pl.ds(start + i * size, size), :], target.at[pl.ds(i * size, size), :])
+        for i in range(PIECES)
+    ]
+
+
+def fetch_rows_kernel(start, after, source, out, token, sems):
+    copies = start_copies(pieces(source, out, start), sems)
+    token[...] = jnp.zeros(token.shape, F32)
+    finish(copies)
 
 
 def normalized(block, gain):
@@ -42,15 +74,123 @@
     return values / (1.0 + jnp.exp(-values))
 
 
-def project_kernel(
-    blocks,
+def stage_kernel(
     place,
-    *refs,
+    in_weight,
+    cache,
+    select,
+    hidden,
+    gain,
+    ffn_gain,
+    conv_weight,
+    conv_bias,
+    step_bias,
+    skip_gain,
+    step_gain,
+    decay,
+    experts,
+    share,
+    in_weight_out,
+    cache_out,
+    select_out,
+    hidden_out,
+    gain_out,
+    ffn_gain_out,
+    columns,
+    step_gain_out,
+    rates,
+    weights,
+    conv_weight_in,
+    conv_bias_in,
+    step_bias_in,
+    skip_gain_in,
+    step_gain_in,
+    decay_in,
+    experts_in,
+    share_in,
+    packed,
+    sems,
 ):
+    small = start_copies(
+        (
+            (conv_weight, conv_weight_in),
+            (conv_bias, conv_bias_in),
+            (step_bias, step_bias_in),
+            (skip_gain, skip_gain_in),
+            (step_gain, step_gain_in),
+            (decay, decay_in),
+            (experts, experts_in),
+            (share, share_in),
+        ),
+        sems,
+    )
+    large = start_copies(
+        (
+            (in_weight, in_weight_out),
+            (cache, cache_out),
+            (select, select_out),
+            (hidden, hidden_out),
+            (gain, gain_out),
+            (ffn_gain, ffn_gain_out),
+        ),
+        sems.at[pl.ds(len(small), 6)],
+    )
+    finish(small)
+    taps, channels = conv_weight.shape
+    packed[...] = jnp.zeros(packed.shape, F32)
+    packed[:taps, :channels] = conv_weight_in[...]
+    packed[taps : taps + 1, :channels] = conv_bias_in[...]
+    packed[taps + 1 : taps + 2, :channels] = step_bias_in[...]
+    packed[taps + 2 : taps + 3, :channels] = skip_gain_in[...]
+    columns[...] = packed[...].T[:channels, :]
+    rank = step_gain.shape[1]
+    packed[:1, :rank] = step_gain_in[...]
+    step_gain_out[...] = packed[...].T[:rank, :]
+    topk, count = experts.shape
+    packed[:topk, :count] = f32(experts_in[...])
+    packed[topk : 2 * topk, :count] = share_in[...]
+    turned = packed[:, :LANES].T[:count, :]
+    lane = lax.broadcasted_iota(jnp.int32, (count, LANES), 1)
+    first = lane < LANES // 2
+    number = f32(jnp.where(first, lane, lane - LANES // 2))
+    dense = jnp.zeros(lane.shape, F32)
+    for k in range(topk):
+        hit = number == turned[:, k : k + 1]
+        dense = dense + jnp.where(hit, turned[:, topk + k : topk + k + 1], 0.0)
+    upper = dense.astype(BF16)
+    lower = (dense - f32(upper)).astype(BF16)
+    weights[...] = jnp.where(first, f32(upper), f32(lower)).astype(BF16)
+    rate = -jnp.exp(decay_in[...])
+    for c in range(channels):
+        rates[c] = jnp.broadcast_to(rate[:, c : c + 1], rates.shape[1:])
+    finish(large)
+
+
+def project_kernel(blocks, place, *refs):
     rows = refs[:blocks]
-    gain, weight, cache, columns, select, conved_out, gate_out, keep, send, normed, selected = refs[
-        blocks:
+    gain, weight, cache, columns, select, out_weight, step_weight, states = refs[
+        blocks : blocks + 8
     ]
+    (
+        conved_out,
+        gate_out,
+        keep,
+        send,
+        out_weight_out,
+        step_weight_out,
+        states_out,
+        normed,
+        selected,
+        sems,
+    ) = refs[blocks + 8 :]
+    copies = start_copies(
+        (
+            (out_weight, out_weight_out),
+            (step_weight, step_weight_out),
+            (states, states_out),
+        ),
+        sems,
+    )
     me = place[0]
     count = rows[0].shape[0]
     for j in range(blocks):
@@ -70,6 +210,7 @@
     send[...] = selected[pl.ds(pl.multiple_of((1 - side) * half, 16), half), :].astype(BF16)
     z_gate = lax.dot_general(weight[1], normed[...], dims, preferred_element_type=F32)
     gate_out[...] = sigmoid_times(z_gate)
+    finish(copies)
 
 
 def state_kernel(
@@ -104,7 +245,7 @@
     selected[pl.ds(pl.multiple_of((1 - side) * half, 16), half), :] = f32(other_half[...])
     low = selected[:rank, :]
     mean_square = jnp.mean(low * low, axis=0, keepdims=True)
-    step_low = (low * lax.rsqrt(mean_square + EPS) * step_gain[...]).astype(BF16)
+    step_low = (low * lax.rsqrt(mean_square + EPS) * step_gain[:, :1]).astype(BF16)
     raw = jnp.dot(step_weight[...], step_low, preferred_element_type=F32) + columns[:, 5:6]
     sizes = jnp.maximum(raw, 0.0) + jnp.log1p(jnp.exp(-jnp.abs(raw)))
     step[...] = sizes
@@ -145,68 +286,87 @@
         out[...] = (f32(keep[span, :]) + f32(got[span, :])).astype(BF16)
 
 
-def add_kernel(*refs):
+def add_kernel(count, *refs):
     total = f32(refs[0][...])
-    for ref in refs[1:-1]:
+    for ref in refs[1:count]:
         total = total + f32(ref[...])
     refs[-1][...] = total.astype(refs[-1].dtype)
 
 
-def residual_kernel(mine, got, hidden, experts, share, out):
+def residual_kernel(mine, got, hidden, weights, token, out):
     width = hidden.shape[1]
     residual = f32(hidden[...]) + (f32(mine[...]) + f32(got[...]))
     out[:, :width] = residual.astype(BF16)
-    lane = lax.broadcasted_iota(jnp.int32, (hidden.shape[0], LANES), 1)
-    first = lane < LANES // 2
-    number = jnp.where(first, lane, lane - LANES // 2)
-    dense = jnp.zeros(lane.shape, F32)
-    for k in range(experts.shape[1]):
-        dense = dense + jnp.where(number == experts[:, k : k + 1], share[:, k : k + 1], 0.0)
-    upper = dense.astype(BF16)
-    lower = (dense - f32(upper)).astype(BF16)
-    out[:, width:] = jnp.where(first, f32(upper), f32(lower)).astype(BF16)
+    out[:, width:] = weights[...]
 
 
 def expert_kernel(blocks, group, place, *refs):
     rows = refs[:blocks]
-    gain, gate_proj, up_proj, down_proj, keep, send, normed, share, total = refs[blocks:]
-    index = pl.program_id(0)
+    gain, *downs = refs[blocks : blocks + 4]
+    gate_proj, up_proj = refs[blocks + 4 : blocks + 6]
+    keep, send, normed, share, total, gates, ups, sems = refs[blocks + 6 :]
     count = rows[0].shape[0]
     width = gain.shape[1]
-
-    @pl.when(index == 0)
-    def _():
-        expert = place[0] // group
-        lane = lax.broadcasted_iota(jnp.int32, (count, LANES), 1)
-        wanted = (lane == expert) | (lane == expert + LANES // 2)
-        for j in range(blocks):
-            span = slice(j * count, (j + 1) * count)
-            normed[span, :] = normalized(rows[j][:, :width], gain[...])
-            shares = jnp.where(wanted, f32(rows[j][:, width:]), 0.0)
-            share[span, :] = jnp.broadcast_to(
-                jnp.sum(shares, axis=1, keepdims=True), (count, LANES)
-            )
-
-    inputs = normed[...]
-    gate_act = jnp.dot(inputs, gate_proj[...], preferred_element_type=F32)
-    up_act = jnp.dot(inputs, up_proj[...], preferred_element_type=F32)
-    inner = (sigmoid_times(gate_act) * up_act).astype(BF16)
-    added = jnp.dot(inner, down_proj[...], preferred_element_type=F32)
-
-    @pl.when(index == 0)
-    def _():
-        total[...] = added
-
-    @pl.when(index > 0)
-    def _():
-        total[...] += added
-
-    @pl.when(index == pl.num_programs(0) - 1)
-    def _():
-        weighted = (total[...] * share[:, :1]).astype(BF16)
-        kept = keep.shape[0]
-        keep[...] = weighted[:kept]
-        send[...] = weighted[kept:]
+    size = gates.shape[2]
+    steps = gate_proj.shape[1] // size
+
+    def copies(i, slot):
+        span = pl.ds(pl.multiple_of(i * size, size), size)
+        return (
+            pltpu.make_async_copy(gate_proj.at[:, span], gates.at[slot], sems.at[slot, 0]),
+            pltpu.make_async_copy(up_proj.at[:, span], ups.at[slot], sems.at[slot, 1]),
+        )
+
+    def begin(i, slot):
+        for copy in copies(i, slot):
+            copy.start()
+
+    for i in range(min(2, steps)):
+        begin(i, i)
+    expert = place[0] // group
+    lane = lax.broadcasted_iota(jnp.int32, (count, LANES), 1)
+    wanted = (lane == expert) | (lane == expert + LANES // 2)
+    for j in range(blocks):
+        span = slice(j * count, (j + 1) * count)
+        normed[span, :] = normalized(rows[j][:, :width], gain[...])
+        shares = jnp.where(wanted, f32(rows[j][:, width:]), 0.0)
+        share[span, :] = jnp.broadcast_to(jnp.sum(shares, axis=1, keepdims=True), (count, LANES))
+
+    def inner_of(gate_block, up_block):
+        inputs = normed[...]
+        gate_act = jnp.dot(inputs, gate_block, preferred_element_type=F32)
+        up_act = jnp.dot(inputs, up_block, preferred_element_type=F32)
+        return (sigmoid_times(gate_act) * up_act).astype(BF16)
+
+    total[...] = jnp.zeros(total.shape, F32)
+    group = 2 if all(down.shape[0] % (2 * size) == 0 for down in downs) else 1
+    first = 0
+    for down in downs:
+        last = first + down.shape[0] // size
+
+        def step(j, carry, down=down, first=first):
+            parts = []
+            for part in range(group):
+                i = first + j * group + part
+                slot = part if group == 2 else lax.rem(i, 2)
+                finish(copies(i, slot))
+                parts.append(inner_of(gates[slot], ups[slot]))
+
+                @pl.when(i + 2 < steps)
+                def _(i=i, slot=slot):
+                    begin(i + 2, slot)
+
+            inner = jnp.concatenate(parts, axis=1)
+            span = pl.ds(pl.multiple_of(j * group * size, size), group * size)
+            total[...] += jnp.dot(inner, down[span, :], preferred_element_type=F32)
+            return carry
+
+        lax.fori_loop(0, (last - first) // group, step, 0)
+        first = last
+    weighted = (total[...] * share[:, :1]).astype(BF16)
+    kept = keep.shape[0]
+    keep[...] = weighted[:kept]
+    send[...] = weighted[kept:]
 
 
 def columns_kernel(place, *refs):
@@ -276,37 +436,134 @@
     def to_narrow(values, k):
         return lax.ppermute(values, "narrow", [(i, i ^ k) for i in range(narrow_count)])
 
-    def plane_gather(block):
-        same = [block] + [to_chip(block, k) for k in range(1, chips)]
+    def fetch_rows(start, size, after):
+        return kernel_call(
+            functools.partial(fetch_rows_kernel, start),
+            [((size, width), BF16), ((8, LANES), F32)],
+            (after, down_proj),
+            scalars=0,
+            far=1,
+            scratch=[pltpu.SemaphoreType.DMA((PIECES,))],
+            cost=pl.CostEstimate(flops=0, bytes_accessed=4 * size * width, transcendentals=0),
+        )
+
+    def plane_gather(block, near):
+        same = [near, *[to_chip(block, k) for k in range(1, chips)]]
         other = [swap(item) for item in same]
         return same, other
 
     def plane_scatter(keep, got):
-        parts = kernel_call(split_kernel, [((count, width), BF16)] * chips, (keep, got), scalars=0)
-        return [parts[0]] + [to_chip(parts[k], k) for k in range(1, chips)]
-
-    def add(*items):
-        return kernel_call(add_kernel, [(items[0].shape, BF16)], items, scalars=0)[0]
+        return kernel_call(split_kernel, [((count, width), BF16)] * chips, (keep, got), scalars=0)
+
+    def to_chips(parts):
+        return [to_chip(parts[k], k) for k in range(1, chips)]
+
+    def add(*items, token=None):
+        args = items if token is None else (*items, token)
+        body = functools.partial(add_kernel, len(items))
+        return kernel_call(body, [(items[0].shape, BF16)], args, scalars=0)[0]
 
     place = jnp.stack([lax.axis_index("wide"), lax.axis_index("narrow")]).astype(jnp.int32)
-    columns = jnp.concatenate(
-        [conv_weight.T, jnp.stack([conv_bias, step_bias, skip_gain], axis=1)], axis=1
-    )
-    rates = jnp.broadcast_to(-jnp.exp(decay_log)[:, :, None], (channels, states, rows))
-
-    same, other = plane_gather(hidden)
+    block = next(size for size in (256, 128, hidden_units) if hidden_units % size == 0)
+    steps = hidden_units // block
+    third = max(1, steps // 3) * block
+    rank = step_weight.shape[1]
+    topk = route_experts.shape[1]
+    padded = max(LANES, channels, rank)
+    (
+        in_weight_near,
+        conv_cache_near,
+        select_near,
+        hidden_near,
+        mixer_gain_near,
+        ffn_gain_near,
+        columns,
+        step_gain_column,
+        rates,
+        weights,
+    ) = kernel_call(
+        stage_kernel,
+        [
+            (in_weight.shape, BF16),
+            (conv_cache.shape, BF16),
+            ((chosen, channels), BF16),
+            (hidden.shape, BF16),
+            ((1, width), F32),
+            ((1, width), F32),
+            ((channels, LANES), F32),
+            ((rank, LANES), F32),
+            ((channels, states, rows), F32),
+            ((count, LANES), BF16),
+        ],
+        (
+            place,
+            in_weight,
+            conv_cache,
+            select_weight.T,
+            hidden,
+            mixer_gain[None, :],
+            ffn_gain[None, :],
+            conv_weight,
+            conv_bias[None, :],
+            step_bias[None, :],
+            skip_gain[None, :],
+            step_gain[None, :],
+            decay_log.T,
+            route_experts.T,
+            route_share.T,
+        ),
+        far=14,
+        scratch=[
+            pltpu.VMEM(conv_weight.shape, F32),
+            pltpu.VMEM((1, channels), F32),
+            pltpu.VMEM((1, channels), F32),
+            pltpu.VMEM((1, channels), F32),
+            pltpu.VMEM((1, rank), F32),
+            pltpu.VMEM((states, channels), F32),
+            pltpu.VMEM((topk, count), jnp.int32),
+            pltpu.VMEM((topk, count), F32),
+            pltpu.VMEM((LANES, padded), F32),
+            pltpu.SemaphoreType.DMA((14,)),
+        ],
+        cost=pl.CostEstimate(
+            flops=0,
+            bytes_accessed=4 * in_weight.size,
+            transcendentals=decay_log.size,
+        ),
+    )
+
+    same, other = plane_gather(hidden, hidden_near)
     interleaved = [item for pair in zip(same, other) for item in pair]
     half = chosen // 2
-    conved, gate, keep, send = kernel_call(
+    conved, gate, keep, send, out_weight_near, step_weight_near, states_near = kernel_call(
         functools.partial(project_kernel, wide_count),
         [
             ((channels, rows), F32),
             ((channels, rows), F32),
             ((half, rows), BF16),
             ((half, rows), BF16),
+            (out_weight.shape, BF16),
+            (step_weight.shape, BF16),
+            (ssm_cache.shape, BF16),
         ],
-        (place, *interleaved, mixer_gain[None, :], in_weight, conv_cache, columns, select_weight.T),
-        scratch=[pltpu.VMEM((rows, width), BF16), pltpu.VMEM((chosen, rows), F32)],
+        (
+            place,
+            *interleaved,
+            mixer_gain_near,
+            in_weight_near,
+            conv_cache_near,
+            columns,
+            select_near,
+            out_weight,
+            step_weight,
+            ssm_cache,
+        ),
+        far=3,
+        scratch=[
+            pltpu.VMEM((rows, width), BF16),
+            pltpu.VMEM((chosen, rows), F32),
+            pltpu.SemaphoreType.DMA((3,)),
+        ],
     )
     part = add(keep, swap(send))
     part = add(part, *[to_chip(part, k) for k in range(1, chips)])
@@ -322,14 +579,14 @@
             place,
             part,
             swap(part),
-            step_gain[:, None],
-            step_weight,
+            step_gain_column,
+            step_weight_near,
             columns,
             conved,
             gate,
-            ssm_cache,
+            states_near,
             rates,
-            out_weight,
+            out_weight_near,
         ),
         scratch=[
             pltpu.VMEM((chosen, rows), F32),
@@ -340,37 +597,48 @@
         ],
     )
     parts = plane_scatter(keep, swap(send))
-    mine = add(*parts)
+    down_first, token = fetch_rows(0, third, parts[0])
+    mine = add(parts[0], *to_chips(parts), token=token)
+    down_second, token = fetch_rows(third, third, mine)
     step = 1
     while 2 * step < narrow_count:
-        mine = add(mine, to_narrow(mine, step))
+        mine = add(mine, to_narrow(mine, step), token=token)
         step *= 2
+    down_third, token = fetch_rows(2 * third, hidden_units - 2 * third, mine)
     (residual,) = kernel_call(
         residual_kernel,
         [((count, width + LANES), BF16)],
-        (mine, to_narrow(mine, step), hidden, route_experts, route_share),
+        (mine, to_narrow(mine, step), hidden_near, weights, token),
         scalars=0,
     )
-    same, other = plane_gather(residual)
-    block = next(size for size in (256, 128, hidden_units) if hidden_units % size == 0)
-    whole = pl.BlockSpec(memory_space=pltpu.VMEM)
-    keep, send = pl.pallas_call(
+    same, other = plane_gather(residual, residual)
+    keep, send = kernel_call(
         functools.partial(expert_kernel, wide_count, wide_count // EXPERTS),
-        grid=(hidden_units // block,),
-        out_shape=[jax.ShapeDtypeStruct((rows // 2, width), BF16)] * 2,
-        in_specs=[pl.BlockSpec(memory_space=pltpu.SMEM)]
-        + [whole] * (wide_count + 1)
-        + [pl.BlockSpec((width, block), lambda i: (0, i))] * 2
-        + [pl.BlockSpec((block, width), lambda i: (i, 0))],
-        out_specs=[whole] * 2,
-        scratch_shapes=[
+        [((rows // 2, width), BF16)] * 2,
+        (
+            place,
+            *same,
+            *other,
+            ffn_gain_near,
+            down_first,
+            down_second,
+            down_third,
+            gate_proj,
+            up_proj,
+        ),
+        far=2,
+        scratch=[
             pltpu.VMEM((rows, width), BF16),
             pltpu.VMEM((rows, LANES), F32),
             pltpu.VMEM((rows, width), F32),
+            pltpu.VMEM((2, width, block), BF16),
+            pltpu.VMEM((2, width, block), BF16),
+            pltpu.SemaphoreType.DMA((2, 2)),
         ],
-        compiler_params=pltpu.CompilerParams(vmem_limit_bytes=48 * MIB),
-    )(place, *same, *other, ffn_gain[None, :], gate_proj, up_proj, down_proj)
+        limit=20,
+    )
     parts = plane_scatter(keep, swap(send))
+    parts = [parts[0], *to_chips(parts)]
     col_share = width // narrow_count
     shares = kernel_call(
         columns_kernel, [((count, col_share), BF16)] * narrow_count, (place, *parts)

time: 135 us -> 116 us (0.86)
  local copies, waits for them, and re-layouts: 14.1 us -> 0 us
  waiting for transfers between devices: 50.7 us -> 40.6 us
  Pallas kernels: 37.8 us -> 43.7 us
  starting transfers between devices: 29.5 us -> 31.1 us
  other arithmetic: 1.55 us -> 0.07 us
    pallas_call x12 -> x17, Pallas kernels: 9.22 us -> 43.7 us  [kernel_call(): pl.pallas_call(body, out_shape=[jax.ShapeDtypeStruct(shape, dtype) for sh...]
    pallas_call x1 -> x0, Pallas kernels: 28.6 us -> none  [on_device(): pl.pallas_call(functools.partial(expert_kernel, wide_count, wide_count //...]
    unnamed x22 -> x0, local copies, waits for them, and re-layouts: 12.5 us -> none
    ppermute x15, waiting for transfers between devices: 26.6 us -> 19.4 us  [to_chip(): lax.ppermute(values, 'wide', [(i, i ^ 2 * k) for i in range(wide_count)])]
    ppermute x8, waiting for transfers between devices: 18.5 us -> 12.8 us  [to_narrow(): lax.ppermute(values, 'narrow', [(i, i ^ k) for i in range(narrow_count)])]
    ppermute x12, waiting for transfers between devices: 5.56 us -> 8.45 us  [swap(): return lax.ppermute(values, 'wide', [(i, i ^ 1) for i in range(wide_count)])]
    ppermute x8, starting transfers between devices: 9.04 us -> 11.1 us  [to_narrow(): lax.ppermute(values, 'narrow', [(i, i ^ k) for i in range(narrow_count)])]
    broadcast_in_dim x2 -> x0, local copies, waits for them, and re-layouts: 1.41 us -> none  [the longest x1 0.81 us: on_device(): step_gain[:, None]]
  transfers between devices with their start and end apart: 35 -> 35, of which waited for: 22 -> 24; matrix products, arithmetic and copies ran while one was open for 3% -> 0% of each run, Pallas kernels for 0% -> 12%
where the time goes in v2:
time: 116 us
  Pallas kernels  43.7 us (38%)
  waiting for transfers between devices  40.6 us (35%)
  starting transfers between devices  31.1 us (27%)
    pallas_call x17, Pallas kernels, kernel_call(): pl.pallas_call(body, out_shape=[jax.ShapeDtypeStruct(shape, dtype) for sh...  43.7 us
    ppermute x15, waiting for transfers between devices, to_chip(): lax.ppermute(values, 'wide', [(i, i ^ 2 * k) for i in range(wide_count)])  19.4 us
    ppermute x15, starting transfers between devices, to_chip(): lax.ppermute(values, 'wide', [(i, i ^ 2 * k) for i in range(wide_count)])  18.8 us
    ppermute x8, waiting for transfers between devices, to_narrow(): lax.ppermute(values, 'narrow', [(i, i ^ k) for i in range(narrow_count)])  12.8 us
    ppermute x8, starting transfers between devices, to_narrow(): lax.ppermute(values, 'narrow', [(i, i ^ k) for i in range(narrow_count)])  11.1 us
    ppermute x12, waiting for transfers between devices, swap(): return lax.ppermute(values, 'wide', [(i, i ^ 1) for i in range(wide_count)])  8.45 us
  transfers between devices with their start and end apart: 35, of which 24 were waited for; matrix products, arithmetic and copies ran while one was open for 0% of the time, Pallas kernels for 12%

profile of v2, /device:TPU:0, one launch (start us, length us, event | category | flops | bytes accessed | tf_op | source)
XLA Modules:
  0.0 116.3 jit_solution(15268348882776970661)
XLA Ops:
  0.6 3.0 %collective-permute-start.1 = (bf16[16,4096]{1,0:T(8,128)(2,1)}, bf16[16,4096]{1,0:T(8,128)(2,1)S(1)}, u32[]{:S(2)}, u32[]{:S(2)}) collective-permute-start(bf16[16,4096]{1,0:T(8,128)(2,1)} %hidden.1), channel_id=1, source_target_pairs={{0,8},{4,12},{8,0},{12,4},{16,24},{20,28},{24,16},{28,20},{1,9},{5... | collective-permute-start | bytes 393224 | tf_op jit(solution)/shard_map/ppermute | solution.py:434
  3.6 1.5 %collective-permute-start.5 = (bf16[16,4096]{1,0:T(8,128)(2,1)}, bf16[16,4096]{1,0:T(8,128)(2,1)S(1)}, u32[]{:S(2)}, u32[]{:S(2)}) collective-permute-start(bf16[16,4096]{1,0:T(8,128)(2,1)} %hidden.1), channel_id=1, source_target_pairs={{0,24},{4,28},{8,16},{12,20},{16,8},{20,12},{24,0},{28,4},{1,25},{... | collective-permute-start | bytes 393224 | tf_op jit(solution)/shard_map/ppermute | solution.py:434
  5.3 3.1 %shard_map.203 = (bf16[2,256,4096]{2,1,0:T(8,128)(2,1)S(1)}, bf16[3,256,128]{2,1,0:T(8,128)(2,1)S(1)}, bf16[288,256]{1,0:T(8,128)(2,1)S(1)}, bf16[16,4096]{1,0:T...) custom-call(s32[2]{0:T(128)S(1)} %pad_add_fusion.place, ...), custom_call_target="tpu_custom_call" | custom-call | bytes 8388608 | tf_op jit(solution)/shard_map/pallas_call | solution.py:30
  8.9 2.6 %collective-permute-done.5.refs_6_ = bf16[16,4096]{1,0:T(8,128)(2,1)S(1)} collective-permute-done((bf16[16,4096]{1,0:T(8,128)(2,1)}, bf16[16,4096]{1,0:T(8,128)(2,1)S(1)}, u32[]{:S(2)}, u32[]{:S(2)}) %collective-permute-start.5) | collective-permute-done | bytes 131104 | tf_op jit(solution)/shard_map/ppermute | solution.py:434
  11.5 1.4 %collective-permute-done.3.refs_4_ = bf16[16,4096]{1,0:T(8,128)(2,1)S(1)} collective-permute-done((bf16[16,4096]{1,0:T(8,128)(2,1)}, bf16[16,4096]{1,0:T(8,128)(2,1)S(1)}, u32[]{:S(2)}, u32[]{:S(2)}) %collective-permute-start.3) | collective-permute-done | bytes 131104 | tf_op jit(solution)/shard_map/ppermute | solution.py:434
  12.8 1.3 %collective-permute-done.4.refs_5_ = bf16[16,4096]{1,0:T(8,128)(2,1)S(1)} collective-permute-done((bf16[16,4096]{1,0:T(8,128)(2,1)S(1)}, bf16[16,4096]{1,0:T(8,128)(2,1)S(1)}, u32[]{:S(2)}, u32[]{:S(2)}) %collective-permute-start.4) | collective-permute-done | bytes 131104 | tf_op jit(solution)/shard_map/ppermute | solution.py:431
  14.2 3.7 %shard_map.204 = (f32[256,128]{1,0:T(8,128)S(1)}, f32[256,128]{1,0:T(8,128)S(1)}, bf16[144,128]{1,0:T(8,128)(2,1)S(1)}, bf16[144,128]{1,0:T(8,128)(2,1)S(1)}, bf...) custom-call(s32[2]{0:T(128)S(1)} %pad_add_fusion.place, ...), custom_call_target="tpu_custom_call" | custom-call | tf_op jit(solution)/shard_map/pallas_call | solution.py:30
  18.1 1.1 collective-permute-done.7.refs_1_
  19.2 1.5 %collective-permute-start.10 = (bf16[144,128]{1,0:T(8,128)(2,1)S(1)}, bf16[144,128]{1,0:T(8,128)(2,1)S(1)}, u32[]{:S(2)}, u32[]{:S(2)}) collective-permute-start(bf16[144,128]{1,0:T(8,128)(2,1)S(1)} %shard_map.205.refs_0_), channel_id=1, source_target_pairs={{0,24},{4,28},{8,16},{12,20},{16,8},{20,12},{24,0},{28,4},{1,25},{... | collective-permute-start | bytes 110600 | tf_op jit(solution)/shard_map/ppermute | solution.py:434
  20.7 1.5 %collective-permute-start.9 = (bf16[144,128]{1,0:T(8,128)(2,1)S(1)}, bf16[144,128]{1,0:T(8,128)(2,1)S(1)}, u32[]{:S(2)}, u32[]{:S(2)}) collective-permute-start(bf16[144,128]{1,0:T(8,128)(2,1)S(1)} %shard_map.205.refs_0_), channel_id=1, source_target_pairs={{0,16},{4,20},{8,24},{12,28},{16,0},{20,4},{24,8},{28,12},{1,17},{... | collective-permute-start | bytes 110600 | tf_op jit(solution)/shard_map/ppermute | solution.py:434
  22.7 1.4 %collective-permute-done.10.refs_3_ = bf16[144,128]{1,0:T(8,128)(2,1)S(1)} collective-permute-done((bf16[144,128]{1,0:T(8,128)(2,1)S(1)}, bf16[144,128]{1,0:T(8,128)(2,1)S(1)}, u32[]{:S(2)}, u32[]{:S(2)}) %collective-permute-start.10) | collective-permute-done | bytes 36896 | tf_op jit(solution)/shard_map/ppermute | solution.py:434
  24.1 0.5 collective-permute-done.9.refs_2_
  24.6 1.5 %collective-permute-done.8.refs_1_ = bf16[144,128]{1,0:T(8,128)(2,1)S(1)} collective-permute-done((bf16[144,128]{1,0:T(8,128)(2,1)S(1)}, bf16[144,128]{1,0:T(8,128)(2,1)S(1)}, u32[]{:S(2)}, u32[]{:S(2)}) %collective-permute-start.8) | collective-permute-done | bytes 36896 | tf_op jit(solution)/shard_map/ppermute | solution.py:434
  26.2 3.7 %collective-permute-start.13 = (bf16[144,128]{1,0:T(8,128)(2,1)S(1)}, bf16[144,128]{1,0:T(8,128)(2,1)S(1)}, u32[]{:S(2)}, u32[]{:S(2)}) collective-permute-start(bf16[144,128]{1,0:T(8,128)(2,1)S(1)} %shard_map.206.refs_0_), channel_id=1, source_target_pairs={{0,3},{1,2},{2,1},{3,0},{4,7},{5,6},{6,5},{7,4},{8,11},{9,10},{10,... | collective-permute-start | bytes 110600 | tf_op jit(solution)/shard_map/ppermute | solution.py:437
  29.8 0.8 collective-permute-start.11
  30.6 1.4 %collective-permute-done.13.refs_3_ = bf16[144,128]{1,0:T(8,128)(2,1)S(1)} collective-permute-done((bf16[144,128]{1,0:T(8,128)(2,1)S(1)}, bf16[144,128]{1,0:T(8,128)(2,1)S(1)}, u32[]{:S(2)}, u32[]{:S(2)}) %collective-permute-start.13) | collective-permute-done | bytes 36896 | tf_op jit(solution)/shard_map/ppermute | solution.py:437
  32.0 2.7 %collective-permute-done.12.refs_2_ = bf16[144,128]{1,0:T(8,128)(2,1)S(1)} collective-permute-done((bf16[144,128]{1,0:T(8,128)(2,1)S(1)}, bf16[144,128]{1,0:T(8,128)(2,1)S(1)}, u32[]{:S(2)}, u32[]{:S(2)}) %collective-permute-start.12) | collective-permute-done | bytes 36896 | tf_op jit(solution)/shard_map/ppermute | solution.py:437
  34.8 1.2 %collective-permute-done.14.other_half = bf16[144,128]{1,0:T(8,128)(2,1)S(1)} collective-permute-done((bf16[144,128]{1,0:T(8,128)(2,1)S(1)}, bf16[144,128]{1,0:T(8,128)(2,1)S(1)}, u32[]{:S(2)}, u32[]{:S(2)}) %collective-permute-start.14) | collective-permute-done | bytes 36896 | tf_op jit(solution)/shard_map/ppermute | solution.py:431
  36.0 3.5 %shard_map.208 = (bf16[256,16,128]{2,1,0:T(8,128)(2,1)}, bf16[64,4096]{1,0:T(8,128)(2,1)S(1)}, bf16[64,4096]{1,0:T(8,128)(2,1)S(1)}) custom-call(s32[2]{0:T(128)S(1)} %pad_add_fusion.place, bf16[144,128]{1,0:T(8,128)(2,1)S(1)} %shard_map.207.own_half, bf16[144,128]{1,0:T(8,128)(2,1)S(1)} %collective-permute-done.14.other_half, ...), custom_call_target="tpu_custom_call" | custom-call | tf_op jit(solution)/shard_map/pallas_call | solution.py:30
  39.6 1.7 %collective-permute-done.15.got = bf16[64,4096]{1,0:T(8,128)(2,1)S(1)} collective-permute-done((bf16[64,4096]{1,0:T(8,128)(2,1)S(1)}, bf16[64,4096]{1,0:T(8,128)(2,1)S(1)}, u32[]{:S(2)}, u32[]{:S(2)}) %collective-permute-start.15) | collective-permute-done | bytes 524320 | tf_op jit(solution)/shard_map/ppermute | solution.py:431
  41.5 0.6 collective-permute-start.16
  42.6 2.4 %collective-permute-start.18 = (bf16[16,4096]{1,0:T(8,128)(2,1)S(1)}, bf16[16,4096]{1,0:T(8,128)(2,1)S(1)}, u32[]{:S(2)}, u32[]{:S(2)}) collective-permute-start(bf16[16,4096]{1,0:T(8,128)(2,1)S(1)} %get-tuple-element.62), channel_id=1, source_target_pairs={{0,24},{4,28},{8,16},{12,20},{16,8},{20,12},{24,0},{28,4},{1,25},{... | collective-permute-start | bytes 393224 | tf_op jit(solution)/shard_map/ppermute | solution.py:434
  45.1 3.5 %shard_map.210 = (bf16[1024,4096]{1,0:T(8,128)(2,1)S(1)}, f32[8,128]{1,0:T(8,128)S(1)}) custom-call(bf16[16,4096]{1,0:T(8,128)(2,1)S(1)} %get-tuple-element.59.after.refs_0_, bf16[3072,4096]{1,0:T(8,128)(2,1)} %source.5), custom_call_target="tpu_custom_call" | custom-call | bytes 16777216 | tf_op jit(solution)/shard_map/pallas_call | solution.py:30
  48.6 1.6 %collective-permute-done.17.refs_2_ = bf16[16,4096]{1,0:T(8,128)(2,1)S(1)} collective-permute-done((bf16[16,4096]{1,0:T(8,128)(2,1)S(1)}, bf16[16,4096]{1,0:T(8,128)(2,1)S(1)}, u32[]{:S(2)}, u32[]{:S(2)}) %collective-permute-start.17) | collective-permute-done | bytes 131104 | tf_op jit(solution)/shard_map/ppermute | solution.py:434
  50.4 3.5 %shard_map.212 = (bf16[1024,4096]{1,0:T(8,128)(2,1)S(1)}, f32[8,128]{1,0:T(8,128)S(1)}) custom-call(bf16[16,4096]{1,0:T(8,128)(2,1)S(1)} %shard_map.211.after.refs_0_, bf16[3072,4096]{1,0:T(8,128)(2,1)} %source.5), custom_call_target="tpu_custom_call" | custom-call | bytes 16777216 | tf_op jit(solution)/shard_map/pallas_call | solution.py:30
  53.9 1.4 %collective-permute-done.19.refs_1_ = bf16[16,4096]{1,0:T(8,128)(2,1)S(1)} collective-permute-done((bf16[16,4096]{1,0:T(8,128)(2,1)S(1)}, bf16[16,4096]{1,0:T(8,128)(2,1)S(1)}, u32[]{:S(2)}, u32[]{:S(2)}) %collective-permute-start.19) | collective-permute-done | bytes 131104 | tf_op jit(solution)/shard_map/ppermute | solution.py:437
  55.4 2.1 %collective-permute-start.20 = (bf16[16,4096]{1,0:T(8,128)(2,1)S(1)}, bf16[16,4096]{1,0:T(8,128)(2,1)S(1)}, u32[]{:S(2)}, u32[]{:S(2)}) collective-permute-start(bf16[16,4096]{1,0:T(8,128)(2,1)S(1)} %shard_map.213.after.mine), channel_id=1, source_target_pairs={{0,2},{1,3},{2,0},{3,1},{4,6},{5,7},{6,4},{7,5},{8,10},{9,11},{10,... | collective-permute-start | bytes 393224 | tf_op jit(solution)/shard_map/ppermute | solution.py:437
  57.5 3.5 %shard_map.214 = (bf16[1024,4096]{1,0:T(8,128)(2,1)S(1)}, f32[8,128]{1,0:T(8,128)S(1)}) custom-call(bf16[16,4096]{1,0:T(8,128)(2,1)S(1)} %shard_map.213.after.mine, bf16[3072,4096]{1,0:T(8,128)(2,1)} %source.5), custom_call_target="tpu_custom_call" | custom-call | bytes 16777216 | tf_op jit(solution)/shard_map/pallas_call | solution.py:30
  61.0 1.7 %collective-permute-done.20.got = bf16[16,4096]{1,0:T(8,128)(2,1)S(1)} collective-permute-done((bf16[16,4096]{1,0:T(8,128)(2,1)S(1)}, bf16[16,4096]{1,0:T(8,128)(2,1)S(1)}, u32[]{:S(2)}, u32[]{:S(2)}) %collective-permute-start.20) | collective-permute-done | bytes 131104 | tf_op jit(solution)/shard_map/ppermute | solution.py:437
  62.8 1.5 %collective-permute-start.23 = (bf16[16,4224]{1,0:T(8,128)(2,1)S(1)}, bf16[16,4224]{1,0:T(8,128)(2,1)S(1)}, u32[]{:S(2)}, u32[]{:S(2)}) collective-permute-start(bf16[16,4224]{1,0:T(8,128)(2,1)S(1)} %shard_map.215.refs_0_.residual), channel_id=1, source_target_pairs={{0,24},{4,28},{8,16},{12,20},{16,8},{20,12},{24,0},{28,4},{1,25},{... | collective-permute-start | bytes 405512 | tf_op jit(solution)/shard_map/ppermute | solution.py:434
  64.3 1.5 %collective-permute-start.22 = (bf16[16,4224]{1,0:T(8,128)(2,1)S(1)}, bf16[16,4224]{1,0:T(8,128)(2,1)S(1)}, u32[]{:S(2)}, u32[]{:S(2)}) collective-permute-start(bf16[16,4224]{1,0:T(8,128)(2,1)S(1)} %shard_map.215.refs_0_.residual), channel_id=1, source_target_pairs={{0,16},{4,20},{8,24},{12,28},{16,0},{20,4},{24,8},{28,12},{1,17},{... | collective-permute-start | bytes 405512 | tf_op jit(solution)/shard_map/ppermute | solution.py:434
  66.3 2.5 %collective-permute-done.23.refs_3_ = bf16[16,4224]{1,0:T(8,128)(2,1)S(1)} collective-permute-done((bf16[16,4224]{1,0:T(8,128)(2,1)S(1)}, bf16[16,4224]{1,0:T(8,128)(2,1)S(1)}, u32[]{:S(2)}, u32[]{:S(2)}) %collective-permute-start.23) | collective-permute-done | bytes 135200 | tf_op jit(solution)/shard_map/ppermute | solution.py:434
  68.8 1.3 %collective-permute-done.22.refs_2_ = bf16[16,4224]{1,0:T(8,128)(2,1)S(1)} collective-permute-done((bf16[16,4224]{1,0:T(8,128)(2,1)S(1)}, bf16[16,4224]{1,0:T(8,128)(2,1)S(1)}, u32[]{:S(2)}, u32[]{:S(2)}) %collective-permute-start.22) | collective-permute-done | bytes 135200 | tf_op jit(solution)/shard_map/ppermute | solution.py:434
  70.2 0.6 collective-permute-done.21.refs_1_
  70.8 0.7 collective-permute-done.26.refs_6_
  71.5 0.6 collective-permute-done.25.refs_5_
  72.2 20.7 %shard_map.216 = (bf16[64,4096]{1,0:T(8,128)(2,1)S(1)}, bf16[64,4096]{1,0:T(8,128)(2,1)S(1)}) custom-call(s32[2]{0:T(128)S(1)} %pad_add_fusion.place, bf16[16,4224]{1,0:T(8,128)(2,1)S(1)} %shard_map.215.refs_0_.residual, bf16[16,4224]{1,0:T(8,128)(2,1)S(1)} %collective-permute-done.21.refs_1_, bf16[16,4224]{1,0:T(8,128)(2,1)S(1)} %collective-permute-done.22.refs_2_, ...), custom_call_target="tpu_custom_call" | custom-call | tf_op jit(solution)/shard_map/pallas_call | solution.py:30
  93.1 1.8 %collective-permute-done.28.got = bf16[64,4096]{1,0:T(8,128)(2,1)S(1)} collective-permute-done((bf16[64,4096]{1,0:T(8,128)(2,1)S(1)}, bf16[64,4096]{1,0:T(8,128)(2,1)S(1)}, u32[]{:S(2)}, u32[]{:S(2)}) %collective-permute-start.28) | collective-permute-done | bytes 524320 | tf_op jit(solution)/shard_map/ppermute | solution.py:431
  95.0 1.2 %collective-permute-start.29 = (bf16[16,4096]{1,0:T(8,128)(2,1)S(1)}, bf16[16,4096]{1,0:T(8,128)(2,1)S(1)}, u32[]{:S(2)}, u32[]{:S(2)}) collective-permute-start(bf16[16,4096]{1,0:T(8,128)(2,1)S(1)} %get-tuple-element.74), channel_id=1, source_target_pairs={{0,8},{4,12},{8,0},{12,4},{16,24},{20,28},{24,16},{28,20},{1,9},{5... | collective-permute-start | bytes 393224 | tf_op jit(solution)/shard_map/ppermute | solution.py:434
  96.2 0.6 collective-permute-start.30
  96.8 1.7 %collective-permute-start.31 = (bf16[16,4096]{1,0:T(8,128)(2,1)S(1)}, bf16[16,4096]{1,0:T(8,128)(2,1)S(1)}, u32[]{:S(2)}, u32[]{:S(2)}) collective-permute-start(bf16[16,4096]{1,0:T(8,128)(2,1)S(1)} %get-tuple-element.76), channel_id=1, source_target_pairs={{0,24},{4,28},{8,16},{12,20},{16,8},{20,12},{24,0},{28,4},{1,25},{... | collective-permute-start | bytes 393224 | tf_op jit(solution)/shard_map/ppermute | solution.py:434
  98.5 2.6 %collective-permute-done.29.refs_1_ = bf16[16,4096]{1,0:T(8,128)(2,1)S(1)} collective-permute-done((bf16[16,4096]{1,0:T(8,128)(2,1)S(1)}, bf16[16,4096]{1,0:T(8,128)(2,1)S(1)}, u32[]{:S(2)}, u32[]{:S(2)}) %collective-permute-start.29) | collective-permute-done | bytes 131104 | tf_op jit(solution)/shard_map/ppermute | solution.py:434
  101.1 3.4 %collective-permute-done.30.refs_2_ = bf16[16,4096]{1,0:T(8,128)(2,1)S(1)} collective-permute-done((bf16[16,4096]{1,0:T(8,128)(2,1)S(1)}, bf16[16,4096]{1,0:T(8,128)(2,1)S(1)}, u32[]{:S(2)}, u32[]{:S(2)}) %collective-permute-start.30) | collective-permute-done | bytes 131104 | tf_op jit(solution)/shard_map/ppermute | solution.py:434
  104.5 0.6 shard_map.218
  105.2 4.2 %collective-permute-start.33 = (bf16[16,1024]{1,0:T(8,128)(2,1)S(1)}, bf16[16,1024]{1,0:T(8,128)(2,1)S(1)}, u32[]{:S(2)}, u32[]{:S(2)}) collective-permute-start(bf16[16,1024]{1,0:T(8,128)(2,1)S(1)} %get-tuple-element.79), channel_id=1, source_target_pairs={{0,2},{1,3},{2,0},{3,1},{4,6},{5,7},{6,4},{7,5},{8,10},{9,11},{10,... | collective-permute-start | bytes 98312 | tf_op jit(solution)/shard_map/ppermute | solution.py:437
  109.6 2.2 %collective-permute-done.33.refs_2_ = bf16[16,1024]{1,0:T(8,128)(2,1)S(1)} collective-permute-done((bf16[16,1024]{1,0:T(8,128)(2,1)S(1)}, bf16[16,1024]{1,0:T(8,128)(2,1)S(1)}, u32[]{:S(2)}, u32[]{:S(2)}) %collective-permute-start.33) | collective-permute-done | bytes 32800 | tf_op jit(solution)/shard_map/ppermute | solution.py:437
  111.8 3.3 %collective-permute-done.34.refs_3_ = bf16[16,1024]{1,0:T(8,128)(2,1)S(1)} collective-permute-done((bf16[16,1024]{1,0:T(8,128)(2,1)S(1)}, bf16[16,1024]{1,0:T(8,128)(2,1)S(1)}, u32[]{:S(2)}, u32[]{:S(2)}) %collective-permute-start.34) | collective-permute-done | bytes 32800 | tf_op jit(solution)/shard_map/ppermute | solution.py:437
  115.1 1.2 %shard_map.219 = bf16[16,1024]{1,0:T(8,128)(2,1)} custom-call(s32[2]{0:T(128)S(1)} %pad_add_fusion.place, bf16[16,4224]{1,0:T(8,128)(2,1)S(1)} %shard_map.215.refs_0_.residual, bf16[16,1024]{1,0:T(8,128)(2,1)S(1)} %get-tuple-element.77.refs_0_, bf16[16,1024]{1,0:T(8,128)(2,1)S(1)} %collective-permute-done.32.refs_1_, ...), custom_call_target="tpu_custom_call" | custom-call | tf_op jit(solution)/shard_map/pallas_call | solution.py:30
  (40 shorter events, 3.8 us)
Async XLA Ops:
  0.6 7.8 %collective-permute-start.1 = (bf16[16,4096]{1,0:T(8,128)(2,1)}, bf16[16,4096]{1,0:T(8,128)(2,1)S(1)}, u32[]{:S(2)}, u32[]{:S(2)}) collective-permute-start(bf16[16,4096]{1,0:T(8,128)(2,1)} %hidden.1), channel_id=1, source_target_pairs={{0,8},{4,12},{8,0},{12,4},{16,24},{20,28},{24,16},{28,20},{1,9},{5... | collective-permute-start | bytes 393224 | tf_op jit(solution)/shard_map/ppermute | solution.py:434
  3.6 7.8 %collective-permute-start.5 = (bf16[16,4096]{1,0:T(8,128)(2,1)}, bf16[16,4096]{1,0:T(8,128)(2,1)S(1)}, u32[]{:S(2)}, u32[]{:S(2)}) collective-permute-start(bf16[16,4096]{1,0:T(8,128)(2,1)} %hidden.1), channel_id=1, source_target_pairs={{0,24},{4,28},{8,16},{12,20},{16,8},{20,12},{24,0},{28,4},{1,25},{... | collective-permute-start | bytes 393224 | tf_op jit(solution)/shard_map/ppermute | solution.py:434
  5.1 7.7 %collective-permute-start.3 = (bf16[16,4096]{1,0:T(8,128)(2,1)}, bf16[16,4096]{1,0:T(8,128)(2,1)S(1)}, u32[]{:S(2)}, u32[]{:S(2)}) collective-permute-start(bf16[16,4096]{1,0:T(8,128)(2,1)} %hidden.1), channel_id=1, source_target_pairs={{0,16},{4,20},{8,24},{12,28},{16,0},{20,4},{24,8},{28,12},{1,17},{... | collective-permute-start | bytes 393224 | tf_op jit(solution)/shard_map/ppermute | solution.py:434
  8.3 4.5 %collective-permute-start = (bf16[16,4096]{1,0:T(8,128)(2,1)S(1)}, bf16[16,4096]{1,0:T(8,128)(2,1)S(1)}, u32[]{:S(2)}, u32[]{:S(2)}) collective-permute-start(bf16[16,4096]{1,0:T(8,128)(2,1)S(1)} %get-tuple-element.42.refs_0_.hidden), channel_id=1, source_target_pairs={{0,4},{4,0},{8,12},{12,8},{16,20},{20,16},{24,28},{28,24},{1,5},{5... | collective-permute-start | bytes 393224 | tf_op jit(solution)/shard_map/ppermute | solution.py:431
  8.4 4.4 %collective-permute-start.2 = (bf16[16,4096]{1,0:T(8,128)(2,1)S(1)}, bf16[16,4096]{1,0:T(8,128)(2,1)S(1)}, u32[]{:S(2)}, u32[]{:S(2)}) collective-permute-start(bf16[16,4096]{1,0:T(8,128)(2,1)S(1)} %collective-permute-done.1.refs_2_), channel_id=1, source_target_pairs={{0,4},{4,0},{8,12},{12,8},{16,20},{20,16},{24,28},{28,24},{1,5},{5... | collective-permute-start | bytes 393224 | tf_op jit(solution)/shard_map/ppermute | solution.py:431
  11.5 1.4 %collective-permute-start.6 = (bf16[16,4096]{1,0:T(8,128)(2,1)S(1)}, bf16[16,4096]{1,0:T(8,128)(2,1)S(1)}, u32[]{:S(2)}, u32[]{:S(2)}) collective-permute-start(bf16[16,4096]{1,0:T(8,128)(2,1)S(1)} %collective-permute-done.5.refs_6_), channel_id=1, source_target_pairs={{0,4},{4,0},{8,12},{12,8},{16,20},{20,16},{24,28},{28,24},{1,5},{5... | collective-permute-start | bytes 393224 | tf_op jit(solution)/shard_map/ppermute | solution.py:431
  12.8 1.3 %collective-permute-start.4 = (bf16[16,4096]{1,0:T(8,128)(2,1)S(1)}, bf16[16,4096]{1,0:T(8,128)(2,1)S(1)}, u32[]{:S(2)}, u32[]{:S(2)}) collective-permute-start(bf16[16,4096]{1,0:T(8,128)(2,1)S(1)} %collective-permute-done.3.refs_4_), channel_id=1, source_target_pairs={{0,4},{4,0},{8,12},{12,8},{16,20},{20,16},{24,28},{28,24},{1,5},{5... | collective-permute-start | bytes 393224 | tf_op jit(solution)/shard_map/ppermute | solution.py:431
  17.9 1.3 %collective-permute-start.7 = (bf16[144,128]{1,0:T(8,128)(2,1)S(1)}, bf16[144,128]{1,0:T(8,128)(2,1)S(1)}, u32[]{:S(2)}, u32[]{:S(2)}) collective-permute-start(bf16[144,128]{1,0:T(8,128)(2,1)S(1)} %get-tuple-element.49), channel_id=1, source_target_pairs={{0,4},{4,0},{8,12},{12,8},{16,20},{20,16},{24,28},{28,24},{1,5},{5... | collective-permute-start | bytes 110600 | tf_op jit(solution)/shard_map/ppermute | solution.py:431
  19.2 4.9 %collective-permute-start.10 = (bf16[144,128]{1,0:T(8,128)(2,1)S(1)}, bf16[144,128]{1,0:T(8,128)(2,1)S(1)}, u32[]{:S(2)}, u32[]{:S(2)}) collective-permute-start(bf16[144,128]{1,0:T(8,128)(2,1)S(1)} %shard_map.205.refs_0_), channel_id=1, source_target_pairs={{0,24},{4,28},{8,16},{12,20},{16,8},{20,12},{24,0},{28,4},{1,25},{... | collective-permute-start | bytes 110600 | tf_op jit(solution)/shard_map/ppermute | solution.py:434
  20.7 4.0 %collective-permute-start.9 = (bf16[144,128]{1,0:T(8,128)(2,1)S(1)}, bf16[144,128]{1,0:T(8,128)(2,1)S(1)}, u32[]{:S(2)}, u32[]{:S(2)}) collective-permute-start(bf16[144,128]{1,0:T(8,128)(2,1)S(1)} %shard_map.205.refs_0_), channel_id=1, source_target_pairs={{0,16},{4,20},{8,24},{12,28},{16,0},{20,4},{24,8},{28,12},{1,17},{... | collective-permute-start | bytes 110600 | tf_op jit(solution)/shard_map/ppermute | solution.py:434
  22.2 4.0 %collective-permute-start.8 = (bf16[144,128]{1,0:T(8,128)(2,1)S(1)}, bf16[144,128]{1,0:T(8,128)(2,1)S(1)}, u32[]{:S(2)}, u32[]{:S(2)}) collective-permute-start(bf16[144,128]{1,0:T(8,128)(2,1)S(1)} %shard_map.205.refs_0_), channel_id=1, source_target_pairs={{0,8},{4,12},{8,0},{12,4},{16,24},{20,28},{24,16},{28,20},{1,9},{5... | collective-permute-start | bytes 110600 | tf_op jit(solution)/shard_map/ppermute | solution.py:434
  26.2 5.9 %collective-permute-start.13 = (bf16[144,128]{1,0:T(8,128)(2,1)S(1)}, bf16[144,128]{1,0:T(8,128)(2,1)S(1)}, u32[]{:S(2)}, u32[]{:S(2)}) collective-permute-start(bf16[144,128]{1,0:T(8,128)(2,1)S(1)} %shard_map.206.refs_0_), channel_id=1, source_target_pairs={{0,3},{1,2},{2,1},{3,0},{4,7},{5,6},{6,5},{7,4},{8,11},{9,10},{10,... | collective-permute-start | bytes 110600 | tf_op jit(solution)/shard_map/ppermute | solution.py:437
  29.8 4.9 %collective-permute-start.12 = (bf16[144,128]{1,0:T(8,128)(2,1)S(1)}, bf16[144,128]{1,0:T(8,128)(2,1)S(1)}, u32[]{:S(2)}, u32[]{:S(2)}) collective-permute-start(bf16[144,128]{1,0:T(8,128)(2,1)S(1)} %shard_map.206.refs_0_), channel_id=1, source_target_pairs={{0,2},{1,3},{2,0},{3,1},{4,6},{5,7},{6,4},{7,5},{8,10},{9,11},{10,... | collective-permute-start | bytes 110600 | tf_op jit(solution)/shard_map/ppermute | solution.py:437
  29.8 4.9 %collective-permute-start.11 = (bf16[144,128]{1,0:T(8,128)(2,1)S(1)}, bf16[144,128]{1,0:T(8,128)(2,1)S(1)}, u32[]{:S(2)}, u32[]{:S(2)}) collective-permute-start(bf16[144,128]{1,0:T(8,128)(2,1)S(1)} %shard_map.206.refs_0_), channel_id=1, source_target_pairs={{0,1},{1,0},{2,3},{3,2},{4,5},{5,4},{6,7},{7,6},{8,9},{9,8},{10,11... | collective-permute-start | bytes 110600 | tf_op jit(solution)/shard_map/ppermute | solution.py:437
  34.7 1.3 %collective-permute-start.14 = (bf16[144,128]{1,0:T(8,128)(2,1)S(1)}, bf16[144,128]{1,0:T(8,128)(2,1)S(1)}, u32[]{:S(2)}, u32[]{:S(2)}) collective-permute-start(bf16[144,128]{1,0:T(8,128)(2,1)S(1)} %shard_map.207.own_half), channel_id=1, source_target_pairs={{0,4},{4,0},{8,12},{12,8},{16,20},{20,16},{24,28},{28,24},{1,5},{5... | collective-permute-start | bytes 110600 | tf_op jit(solution)/shard_map/ppermute | solution.py:431
  39.5 1.9 %collective-permute-start.15 = (bf16[64,4096]{1,0:T(8,128)(2,1)S(1)}, bf16[64,4096]{1,0:T(8,128)(2,1)S(1)}, u32[]{:S(2)}, u32[]{:S(2)}) collective-permute-start(bf16[64,4096]{1,0:T(8,128)(2,1)S(1)} %get-tuple-element.58), channel_id=1, source_target_pairs={{0,4},{4,0},{8,12},{12,8},{16,20},{20,16},{24,28},{28,24},{1,5},{5... | collective-permute-start | bytes 1572872 | tf_op jit(solution)/shard_map/ppermute | solution.py:431
  41.5 7.1 %collective-permute-start.16 = (bf16[16,4096]{1,0:T(8,128)(2,1)S(1)}, bf16[16,4096]{1,0:T(8,128)(2,1)S(1)}, u32[]{:S(2)}, u32[]{:S(2)}) collective-permute-start(bf16[16,4096]{1,0:T(8,128)(2,1)S(1)} %get-tuple-element.60), channel_id=1, source_target_pairs={{0,8},{4,12},{8,0},{12,4},{16,24},{20,28},{24,16},{28,20},{1,9},{5... | collective-permute-start | bytes 393224 | tf_op jit(solution)/shard_map/ppermute | solution.py:434
  42.1 8.1 %collective-permute-start.17 = (bf16[16,4096]{1,0:T(8,128)(2,1)S(1)}, bf16[16,4096]{1,0:T(8,128)(2,1)S(1)}, u32[]{:S(2)}, u32[]{:S(2)}) collective-permute-start(bf16[16,4096]{1,0:T(8,128)(2,1)S(1)} %get-tuple-element.61), channel_id=1, source_target_pairs={{0,16},{4,20},{8,24},{12,28},{16,0},{20,4},{24,8},{28,12},{1,17},{... | collective-permute-start | bytes 393224 | tf_op jit(solution)/shard_map/ppermute | solution.py:434
  42.6 7.6 %collective-permute-start.18 = (bf16[16,4096]{1,0:T(8,128)(2,1)S(1)}, bf16[16,4096]{1,0:T(8,128)(2,1)S(1)}, u32[]{:S(2)}, u32[]{:S(2)}) collective-permute-start(bf16[16,4096]{1,0:T(8,128)(2,1)S(1)} %get-tuple-element.62), channel_id=1, source_target_pairs={{0,24},{4,28},{8,16},{12,20},{16,8},{20,12},{24,0},{28,4},{1,25},{... | collective-permute-start | bytes 393224 | tf_op jit(solution)/shard_map/ppermute | solution.py:434
  50.3 5.0 %collective-permute-start.19 = (bf16[16,4096]{1,0:T(8,128)(2,1)S(1)}, bf16[16,4096]{1,0:T(8,128)(2,1)S(1)}, u32[]{:S(2)}, u32[]{:S(2)}) collective-permute-start(bf16[16,4096]{1,0:T(8,128)(2,1)S(1)} %shard_map.211.after.refs_0_), channel_id=1, source_target_pairs={{0,1},{1,0},{2,3},{3,2},{4,5},{5,4},{6,7},{7,6},{8,9},{9,8},{10,11... | collective-permute-start | bytes 393224 | tf_op jit(solution)/shard_map/ppermute | solution.py:437
  55.4 7.3 %collective-permute-start.20 = (bf16[16,4096]{1,0:T(8,128)(2,1)S(1)}, bf16[16,4096]{1,0:T(8,128)(2,1)S(1)}, u32[]{:S(2)}, u32[]{:S(2)}) collective-permute-start(bf16[16,4096]{1,0:T(8,128)(2,1)S(1)} %shard_map.213.after.mine), channel_id=1, source_target_pairs={{0,2},{1,3},{2,0},{3,1},{4,6},{5,7},{6,4},{7,5},{8,10},{9,11},{10,... | collective-permute-start | bytes 393224 | tf_op jit(solution)/shard_map/ppermute | solution.py:437
  62.8 6.1 %collective-permute-start.23 = (bf16[16,4224]{1,0:T(8,128)(2,1)S(1)}, bf16[16,4224]{1,0:T(8,128)(2,1)S(1)}, u32[]{:S(2)}, u32[]{:S(2)}) collective-permute-start(bf16[16,4224]{1,0:T(8,128)(2,1)S(1)} %shard_map.215.refs_0_.residual), channel_id=1, source_target_pairs={{0,24},{4,28},{8,16},{12,20},{16,8},{20,12},{24,0},{28,4},{1,25},{... | collective-permute-start | bytes 405512 | tf_op jit(solution)/shard_map/ppermute | solution.py:434
  64.3 5.9 %collective-permute-start.22 = (bf16[16,4224]{1,0:T(8,128)(2,1)S(1)}, bf16[16,4224]{1,0:T(8,128)(2,1)S(1)}, u32[]{:S(2)}, u32[]{:S(2)}) collective-permute-start(bf16[16,4224]{1,0:T(8,128)(2,1)S(1)} %shard_map.215.refs_0_.residual), channel_id=1, source_target_pairs={{0,16},{4,20},{8,24},{12,28},{16,0},{20,4},{24,8},{28,12},{1,17},{... | collective-permute-start | bytes 405512 | tf_op jit(solution)/shard_map/ppermute | solution.py:434
  65.8 5.0 %collective-permute-start.21 = (bf16[16,4224]{1,0:T(8,128)(2,1)S(1)}, bf16[16,4224]{1,0:T(8,128)(2,1)S(1)}, u32[]{:S(2)}, u32[]{:S(2)}) collective-permute-start(bf16[16,4224]{1,0:T(8,128)(2,1)S(1)} %shard_map.215.refs_0_.residual), channel_id=1, source_target_pairs={{0,8},{4,12},{8,0},{12,4},{16,24},{20,28},{24,16},{28,20},{1,9},{5... | collective-permute-start | bytes 405512 | tf_op jit(solution)/shard_map/ppermute | solution.py:434
  66.3 4.5 %collective-permute-start.24 = (bf16[16,4224]{1,0:T(8,128)(2,1)S(1)}, bf16[16,4224]{1,0:T(8,128)(2,1)S(1)}, u32[]{:S(2)}, u32[]{:S(2)}) collective-permute-start(bf16[16,4224]{1,0:T(8,128)(2,1)S(1)} %shard_map.215.refs_0_.residual), channel_id=1, source_target_pairs={{0,4},{4,0},{8,12},{12,8},{16,20},{20,16},{24,28},{28,24},{1,5},{5... | collective-permute-start | bytes 405512 | tf_op jit(solution)/shard_map/ppermute | solution.py:431
  68.8 2.0 %collective-permute-start.27 = (bf16[16,4224]{1,0:T(8,128)(2,1)S(1)}, bf16[16,4224]{1,0:T(8,128)(2,1)S(1)}, u32[]{:S(2)}, u32[]{:S(2)}) collective-permute-start(bf16[16,4224]{1,0:T(8,128)(2,1)S(1)} %collective-permute-done.23.refs_3_), channel_id=1, source_target_pairs={{0,4},{4,0},{8,12},{12,8},{16,20},{20,16},{24,28},{28,24},{1,5},{5... | collective-permute-start | bytes 405512 | tf_op jit(solution)/shard_map/ppermute | solution.py:431
  70.2 1.4 %collective-permute-start.26 = (bf16[16,4224]{1,0:T(8,128)(2,1)S(1)}, bf16[16,4224]{1,0:T(8,128)(2,1)S(1)}, u32[]{:S(2)}, u32[]{:S(2)}) collective-permute-start(bf16[16,4224]{1,0:T(8,128)(2,1)S(1)} %collective-permute-done.22.refs_2_), channel_id=1, source_target_pairs={{0,4},{4,0},{8,12},{12,8},{16,20},{20,16},{24,28},{28,24},{1,5},{5... | collective-permute-start | bytes 405512 | tf_op jit(solution)/shard_map/ppermute | solution.py:431
  70.8 1.4 %collective-permute-start.25 = (bf16[16,4224]{1,0:T(8,128)(2,1)S(1)}, bf16[16,4224]{1,0:T(8,128)(2,1)S(1)}, u32[]{:S(2)}, u32[]{:S(2)}) collective-permute-start(bf16[16,4224]{1,0:T(8,128)(2,1)S(1)} %collective-permute-done.21.refs_1_), channel_id=1, source_target_pairs={{0,4},{4,0},{8,12},{12,8},{16,20},{20,16},{24,28},{28,24},{1,5},{5... | collective-permute-start | bytes 405512 | tf_op jit(solution)/shard_map/ppermute | solution.py:431
  92.9 2.0 %collective-permute-start.28 = (bf16[64,4096]{1,0:T(8,128)(2,1)S(1)}, bf16[64,4096]{1,0:T(8,128)(2,1)S(1)}, u32[]{:S(2)}, u32[]{:S(2)}) collective-permute-start(bf16[64,4096]{1,0:T(8,128)(2,1)S(1)} %get-tuple-element.72), channel_id=1, source_target_pairs={{0,4},{4,0},{8,12},{12,8},{16,20},{20,16},{24,28},{28,24},{1,5},{5... | collective-permute-start | bytes 1572872 | tf_op jit(solution)/shard_map/ppermute | solution.py:431
  95.0 6.1 %collective-permute-start.29 = (bf16[16,4096]{1,0:T(8,128)(2,1)S(1)}, bf16[16,4096]{1,0:T(8,128)(2,1)S(1)}, u32[]{:S(2)}, u32[]{:S(2)}) collective-permute-start(bf16[16,4096]{1,0:T(8,128)(2,1)S(1)} %get-tuple-element.74), channel_id=1, source_target_pairs={{0,8},{4,12},{8,0},{12,4},{16,24},{20,28},{24,16},{28,20},{1,9},{5... | collective-permute-start | bytes 393224 | tf_op jit(solution)/shard_map/ppermute | solution.py:434
  96.2 8.2 %collective-permute-start.30 = (bf16[16,4096]{1,0:T(8,128)(2,1)S(1)}, bf16[16,4096]{1,0:T(8,128)(2,1)S(1)}, u32[]{:S(2)}, u32[]{:S(2)}) collective-permute-start(bf16[16,4096]{1,0:T(8,128)(2,1)S(1)} %get-tuple-element.75), channel_id=1, source_target_pairs={{0,16},{4,20},{8,24},{12,28},{16,0},{20,4},{24,8},{28,12},{1,17},{... | collective-permute-start | bytes 393224 | tf_op jit(solution)/shard_map/ppermute | solution.py:434
  96.8 7.7 %collective-permute-start.31 = (bf16[16,4096]{1,0:T(8,128)(2,1)S(1)}, bf16[16,4096]{1,0:T(8,128)(2,1)S(1)}, u32[]{:S(2)}, u32[]{:S(2)}) collective-permute-start(bf16[16,4096]{1,0:T(8,128)(2,1)S(1)} %get-tuple-element.76), channel_id=1, source_target_pairs={{0,24},{4,28},{8,16},{12,20},{16,8},{20,12},{24,0},{28,4},{1,25},{... | collective-permute-start | bytes 393224 | tf_op jit(solution)/shard_map/ppermute | solution.py:434
  105.1 4.5 %collective-permute-start.32 = (bf16[16,1024]{1,0:T(8,128)(2,1)S(1)}, bf16[16,1024]{1,0:T(8,128)(2,1)S(1)}, u32[]{:S(2)}, u32[]{:S(2)}) collective-permute-start(bf16[16,1024]{1,0:T(8,128)(2,1)S(1)} %get-tuple-element.78), channel_id=1, source_target_pairs={{0,1},{1,0},{2,3},{3,2},{4,5},{5,4},{6,7},{7,6},{8,9},{9,8},{10,11... | collective-permute-start | bytes 98312 | tf_op jit(solution)/shard_map/ppermute | solution.py:437
  105.2 6.6 %collective-permute-start.33 = (bf16[16,1024]{1,0:T(8,128)(2,1)S(1)}, bf16[16,1024]{1,0:T(8,128)(2,1)S(1)}, u32[]{:S(2)}, u32[]{:S(2)}) collective-permute-start(bf16[16,1024]{1,0:T(8,128)(2,1)S(1)} %get-tuple-element.79), channel_id=1, source_target_pairs={{0,2},{1,3},{2,0},{3,1},{4,6},{5,7},{6,4},{7,5},{8,10},{9,11},{10,... | collective-permute-start | bytes 98312 | tf_op jit(solution)/shard_map/ppermute | solution.py:437
  109.4 5.7 %collective-permute-start.34 = (bf16[16,1024]{1,0:T(8,128)(2,1)S(1)}, bf16[16,1024]{1,0:T(8,128)(2,1)S(1)}, u32[]{:S(2)}, u32[]{:S(2)}) collective-permute-start(bf16[16,1024]{1,0:T(8,128)(2,1)S(1)} %get-tuple-element.80), channel_id=1, source_target_pairs={{0,3},{1,2},{2,1},{3,0},{4,7},{5,6},{6,5},{7,4},{8,11},{9,10},{10,... | collective-permute-start | bytes 98312 | tf_op jit(solution)/shard_map/ppermute | solution.py:437

commit v3 on v2

--- a/solution.py
+++ b/solution.py
@@ -11,7 +11,7 @@
 EPS = 1e-06
 MIB = 1 << 20
 LANES = 128
-PIECES = 4
+PIECES = 2
 F32 = jnp.float32
 BF16 = jnp.bfloat16
 
@@ -20,8 +20,7 @@
     return values.astype(F32)
 
 
-def kernel_call(body, outs, args, scalars=1, far=0, scratch=(), limit=16, cost=None):
-    smem = pl.BlockSpec(memory_space=pltpu.SMEM)
+def kernel_call(body, outs, args, far=0, scratch=(), limit=16, cost=None, pinned=0):
     vmem = pl.BlockSpec(memory_space=pltpu.VMEM)
     hbm = pl.BlockSpec(memory_space=pltpu.HBM)
     near = len(args) - far
@@ -29,8 +28,11 @@
     args = (*args[:near], *stay)
     return pl.pallas_call(
         body,
-        out_shape=[jax.ShapeDtypeStruct(shape, dtype) for shape, dtype in outs],
-        in_specs=[smem] * scalars + [vmem] * (len(args) - scalars - far) + [hbm] * far,
+        out_shape=[
+            pltpu.VMEM(*out) if i < pinned else jax.ShapeDtypeStruct(*out)
+            for i, out in enumerate(outs)
+        ],
+        in_specs=[vmem] * near + [hbm] * far,
         out_specs=[vmem] * len(outs),
         scratch_shapes=scratch,
         compiler_params=pltpu.CompilerParams(vmem_limit_bytes=limit * MIB),
@@ -50,17 +52,32 @@
         copy.wait()
 
 
-def pieces(source, target, start):
-    size = target.shape[0] // PIECES
-    return [
-        (source.at[pl.ds(start + i * size, size), :], target.at[pl.ds(i * size, size), :])
-        for i in range(PIECES)
-    ]
-
-
-def fetch_rows_kernel(start, after, source, out, token, sems):
-    copies = start_copies(pieces(source, out, start), sems)
+def fetch_rows_kernel(start, after, source, *refs):
+    *outs, token, sems = refs
+    size = outs[0].shape[0] // PIECES
+    pairs = []
+    for i, out in enumerate(outs):
+        for j in range(PIECES):
+            first = start + (i * PIECES + j) * size
+            pairs.append((source.at[pl.ds(first, size), :], out.at[pl.ds(j * size, size), :]))
+    copies = start_copies(pairs, sems)
     token[...] = jnp.zeros(token.shape, F32)
+    finish(copies)
+
+
+def fetch_kernel(after, first, second, third, first_out, second_out, third_out, token, sems):
+    copies = start_copies(((first, first_out), (second, second_out), (third, third_out)), sems)
+    token[...] = jnp.zeros(token.shape, F32)
+    finish(copies)
+
+
+def fetch_columns_kernel(block, first, second, first_out, second_out, block_out, sems):
+    size = first_out.shape[1]
+    copies = start_copies(
+        ((first.at[:, pl.ds(0, size)], first_out), (second.at[:, pl.ds(0, size)], second_out)),
+        sems,
+    )
+    block_out[...] = block[...]
     finish(copies)
 
 
@@ -75,7 +92,6 @@
 
 
 def stage_kernel(
-    place,
     in_weight,
     cache,
     select,
@@ -166,32 +182,11 @@
     finish(large)
 
 
-def project_kernel(blocks, place, *refs):
+def project_kernel(blocks, *refs):
     rows = refs[:blocks]
-    gain, weight, cache, columns, select, out_weight, step_weight, states = refs[
-        blocks : blocks + 8
-    ]
-    (
-        conved_out,
-        gate_out,
-        keep,
-        send,
-        out_weight_out,
-        step_weight_out,
-        states_out,
-        normed,
-        selected,
-        sems,
-    ) = refs[blocks + 8 :]
-    copies = start_copies(
-        (
-            (out_weight, out_weight_out),
-            (step_weight, step_weight_out),
-            (states, states_out),
-        ),
-        sems,
-    )
-    me = place[0]
+    gain, weight, cache, columns, select = refs[blocks : blocks + 5]
+    conved_out, gate_out, keep, send, normed, selected = refs[blocks + 5 :]
+    me = lax.axis_index("wide")
     count = rows[0].shape[0]
     for j in range(blocks):
         start = pl.multiple_of((me ^ j) * count, count)
@@ -210,12 +205,10 @@
     send[...] = selected[pl.ds(pl.multiple_of((1 - side) * half, 16), half), :].astype(BF16)
     z_gate = lax.dot_general(weight[1], normed[...], dims, preferred_element_type=F32)
     gate_out[...] = sigmoid_times(z_gate)
-    finish(copies)
 
 
 def state_kernel(
     blocks,
-    place,
     own_half,
     other_half,
     step_gain,
@@ -235,7 +228,7 @@
     mixed,
     turned,
 ):
-    me = place[0]
+    me = lax.axis_index("wide")
     side = me & 1
     half = own_half.shape[0]
     channels, states, rows = cache.shape
@@ -300,18 +293,17 @@
     out[:, width:] = weights[...]
 
 
-def expert_kernel(blocks, group, place, *refs):
+def expert_kernel(blocks, steps, group, *refs):
     rows = refs[:blocks]
-    gain, *downs = refs[blocks : blocks + 4]
-    gate_proj, up_proj = refs[blocks + 4 : blocks + 6]
-    keep, send, normed, share, total, gates, ups, sems = refs[blocks + 6 :]
+    gain, *downs = refs[blocks : blocks + 1 + steps]
+    gate_first, up_first, gate_proj, up_proj = refs[blocks + 1 + steps : blocks + 5 + steps]
+    keep, send, normed, share, total, gates, ups, sems = refs[blocks + 5 + steps :]
     count = rows[0].shape[0]
     width = gain.shape[1]
     size = gates.shape[2]
-    steps = gate_proj.shape[1] // size
 
     def copies(i, slot):
-        span = pl.ds(pl.multiple_of(i * size, size), size)
+        span = pl.ds(i * size, size)
         return (
             pltpu.make_async_copy(gate_proj.at[:, span], gates.at[slot], sems.at[slot, 0]),
             pltpu.make_async_copy(up_proj.at[:, span], ups.at[slot], sems.at[slot, 1]),
@@ -321,9 +313,21 @@
         for copy in copies(i, slot):
             copy.start()
 
-    for i in range(min(2, steps)):
-        begin(i, i)
-    expert = place[0] // group
+    near = gate_first.shape[1]
+    rest = size - near
+    ahead = []
+    if rest:
+        span = pl.ds(near, rest)
+        ahead = start_copies(
+            (
+                (gate_proj.at[:, span], gates.at[0, :, pl.ds(0, rest)]),
+                (up_proj.at[:, span], ups.at[0, :, pl.ds(0, rest)]),
+            ),
+            sems.at[0],
+        )
+    for i in range(1, min(2 if rest else 3, steps)):
+        begin(i, i % 2)
+    expert = lax.axis_index("wide") // group
     lane = lax.broadcasted_iota(jnp.int32, (count, LANES), 1)
     wanted = (lane == expert) | (lane == expert + LANES // 2)
     for j in range(blocks):
@@ -338,62 +342,54 @@
         up_act = jnp.dot(inputs, up_block, preferred_element_type=F32)
         return (sigmoid_times(gate_act) * up_act).astype(BF16)
 
-    total[...] = jnp.zeros(total.shape, F32)
-    group = 2 if all(down.shape[0] % (2 * size) == 0 for down in downs) else 1
-    first = 0
-    for down in downs:
-        last = first + down.shape[0] // size
-
-        def step(j, carry, down=down, first=first):
-            parts = []
-            for part in range(group):
-                i = first + j * group + part
-                slot = part if group == 2 else lax.rem(i, 2)
-                finish(copies(i, slot))
-                parts.append(inner_of(gates[slot], ups[slot]))
-
-                @pl.when(i + 2 < steps)
-                def _(i=i, slot=slot):
-                    begin(i + 2, slot)
-
-            inner = jnp.concatenate(parts, axis=1)
-            span = pl.ds(pl.multiple_of(j * group * size, size), group * size)
-            total[...] += jnp.dot(inner, down[span, :], preferred_element_type=F32)
-            return carry
-
-        lax.fori_loop(0, (last - first) // group, step, 0)
-        first = last
+    inner = inner_of(gate_first[...], up_first[...])
+    if rest:
+        finish(ahead)
+        more = inner_of(gates[0, :, :rest], ups[0, :, :rest])
+        if steps > 2:
+            begin(2, 0)
+        inner = jnp.concatenate([inner, more], axis=1)
+    total[...] = jnp.dot(inner, downs[0][...], preferred_element_type=F32)
+    for i in range(1, steps):
+        slot = i % 2
+        finish(copies(i, slot))
+        inner = inner_of(gates[slot], ups[slot])
+        if i + 2 < steps:
+            begin(i + 2, slot)
+        total[...] += jnp.dot(inner, downs[i][...], preferred_element_type=F32)
     weighted = (total[...] * share[:, :1]).astype(BF16)
     kept = keep.shape[0]
     keep[...] = weighted[:kept]
     send[...] = weighted[kept:]
 
 
-def columns_kernel(place, *refs):
-    outs = refs[-place_count(refs) :]
-    ins = refs[: -len(outs)]
+def columns_kernel(narrow_count, *refs):
+    ins, outs = refs[:-narrow_count], refs[-narrow_count:]
     size = outs[0].shape[1]
-    me = place[1]
-    for k, out in enumerate(outs):
-        span = pl.ds(pl.multiple_of((me ^ k) * size, size), size)
-        total = f32(ins[0][:, span])
-        for ref in ins[1:]:
-            total = total + f32(ref[:, span])
-        out[...] = total.astype(BF16)
-
-
-def place_count(refs):
-    return refs[0].shape[1] // refs[-1].shape[1]
-
-
-def final_kernel(place, residual, *refs):
-    out = refs[-1]
+    for me in range(narrow_count):
+
+        @pl.when(lax.axis_index("narrow") == me)
+        def _(me=me):
+            for k, out in enumerate(outs):
+                first = (me ^ k) * size
+                span = slice(first, first + size)
+                total = f32(ins[0][:, span])
+                for ref in ins[1:]:
+                    total = total + f32(ref[:, span])
+                out[...] = total.astype(BF16)
+
+
+def final_kernel(narrow_count, residual, *refs):
+    *ins, out = refs
     size = out.shape[1]
-    span = pl.ds(pl.multiple_of(place[1] * size, size), size)
-    total = f32(refs[0][...])
-    for ref in refs[1:-1]:
-        total = total + f32(ref[...])
-    out[...] = (f32(residual[:, span]) + total).astype(BF16)
+    for me in range(narrow_count):
+
+        @pl.when(lax.axis_index("narrow") == me)
+        def _(me=me):
+            total = f32(ins[0][...])
+            for ref in ins[1:]:
+                total = total + f32(ref[...])
+            out[...] = (f32(residual[:, me * size : (me + 1) * size]) + total).astype(BF16)
 
 
 def on_device(
@@ -436,15 +432,28 @@
     def to_narrow(values, k):
         return lax.ppermute(values, "narrow", [(i, i ^ k) for i in range(narrow_count)])
 
-    def fetch_rows(start, size, after):
+    def fetch_rows(start, number, after):
+        *blocks, token = kernel_call(
+            functools.partial(fetch_rows_kernel, start * block),
+            [((block, width), BF16)] * number + [((8, LANES), F32)],
+            (after, down_proj),
+                far=1,
+            scratch=[pltpu.SemaphoreType.DMA((number * PIECES,))],
+            cost=pl.CostEstimate(
+                flops=0, bytes_accessed=4 * number * block * width, transcendentals=0
+            ),
+        )
+        return blocks, token
+
+    def fetch_columns(size, after):
         return kernel_call(
-            functools.partial(fetch_rows_kernel, start),
-            [((size, width), BF16), ((8, LANES), F32)],
-            (after, down_proj),
-            scalars=0,
-            far=1,
-            scratch=[pltpu.SemaphoreType.DMA((PIECES,))],
-            cost=pl.CostEstimate(flops=0, bytes_accessed=4 * size * width, transcendentals=0),
+            fetch_columns_kernel,
+            [((width, size), BF16), ((width, size), BF16), (after.shape, BF16)],
+            (after, gate_proj, up_proj),
+                far=2,
+            scratch=[pltpu.SemaphoreType.DMA((2,))],
+            cost=pl.CostEstimate(flops=0, bytes_accessed=8 * size * width, transcendentals=0),
+            pinned=2,
         )
 
     def plane_gather(block, near):
@@ -453,7 +462,7 @@
         return same, other
 
     def plane_scatter(keep, got):
-        return kernel_call(split_kernel, [((count, width), BF16)] * chips, (keep, got), scalars=0)
+        return kernel_call(split_kernel, [((count, width), BF16)] * chips, (keep, got))
 
     def to_chips(parts):
         return [to_chip(parts[k], k) for k in range(1, chips)]
@@ -461,12 +470,12 @@
     def add(*items, token=None):
         args = items if token is None else (*items, token)
         body = functools.partial(add_kernel, len(items))
-        return kernel_call(body, [(items[0].shape, BF16)], args, scalars=0)[0]
-
-    place = jnp.stack([lax.axis_index("wide"), lax.axis_index("narrow")]).astype(jnp.int32)
-    block = next(size for size in (256, 128, hidden_units) if hidden_units % size == 0)
+        return kernel_call(body, [(items[0].shape, BF16)], args)[0]
+
+    block = next(size for size in (512, 256, 128, hidden_units) if hidden_units % size == 0)
     steps = hidden_units // block
-    third = max(1, steps // 3) * block
+    third = max(1, steps // 3)
+    near = block // 2 if block % (2 * LANES) == 0 else block
     rank = step_weight.shape[1]
     topk = route_experts.shape[1]
     padded = max(LANES, channels, rank)
@@ -496,7 +505,6 @@
             ((count, LANES), BF16),
         ],
         (
-            place,
             in_weight,
             conv_cache,
             select_weight.T,
@@ -535,38 +543,44 @@
     same, other = plane_gather(hidden, hidden_near)
     interleaved = [item for pair in zip(same, other) for item in pair]
     half = chosen // 2
-    conved, gate, keep, send, out_weight_near, step_weight_near, states_near = kernel_call(
+    conved, gate, keep, send = kernel_call(
         functools.partial(project_kernel, wide_count),
         [
             ((channels, rows), F32),
             ((channels, rows), F32),
             ((half, rows), BF16),
             ((half, rows), BF16),
-            (out_weight.shape, BF16),
-            (step_weight.shape, BF16),
-            (ssm_cache.shape, BF16),
         ],
         (
-            place,
             *interleaved,
             mixer_gain_near,
             in_weight_near,
             conv_cache_near,
             columns,
             select_near,
-            out_weight,
-            step_weight,
-            ssm_cache,
-        ),
-        far=3,
+        ),
         scratch=[
             pltpu.VMEM((rows, width), BF16),
             pltpu.VMEM((chosen, rows), F32),
-            pltpu.SemaphoreType.DMA((3,)),
         ],
     )
     part = add(keep, swap(send))
-    part = add(part, *[to_chip(part, k) for k in range(1, chips)])
+    out_weight_near, step_weight_near, states_near, token = kernel_call(
+        fetch_kernel,
+        [
+            (out_weight.shape, BF16),
+            (step_weight.shape, BF16),
+            (ssm_cache.shape, BF16),
+            ((8, LANES), F32),
+        ],
+        (part, out_weight, step_weight, ssm_cache),
+        far=3,
+        scratch=[pltpu.SemaphoreType.DMA((3,))],
+        cost=pl.CostEstimate(
+            flops=0, bytes_accessed=4 * (out_weight.size + ssm_cache.size), transcendentals=0
+        ),
+    )
+    part = add(part, *[to_chip(part, k) for k in range(1, chips)], token=token)
     part = add(part, *[to_narrow(part, k) for k in range(1, narrow_count)])
     new_state, keep, send = kernel_call(
         functools.partial(state_kernel, wide_count),
@@ -576,7 +590,6 @@
             ((rows // 2, width), BF16),
         ],
         (
-            place,
             part,
             swap(part),
             step_gain_column,
@@ -604,25 +617,26 @@
     while 2 * step < narrow_count:
         mine = add(mine, to_narrow(mine, step), token=token)
         step *= 2
-    down_third, token = fetch_rows(2 * third, hidden_units - 2 * third, mine)
+    down_third, token = fetch_rows(2 * third, steps - 2 * third, mine)
     (residual,) = kernel_call(
         residual_kernel,
         [((count, width + LANES), BF16)],
         (mine, to_narrow(mine, step), hidden_near, weights, token),
-        scalars=0,
-    )
-    same, other = plane_gather(residual, residual)
+    )
+    gate_first, up_first, residual_near = fetch_columns(near, residual)
+    same, other = plane_gather(residual, residual_near)
     keep, send = kernel_call(
-        functools.partial(expert_kernel, wide_count, wide_count // EXPERTS),
+        functools.partial(expert_kernel, wide_count, steps, wide_count // EXPERTS),
         [((rows // 2, width), BF16)] * 2,
         (
-            place,
             *same,
             *other,
             ffn_gain_near,
-            down_first,
-            down_second,
-            down_third,
+            *down_first,
+            *down_second,
+            *down_third,
+            gate_first,
+            up_first,
             gate_proj,
             up_proj,
         ),
@@ -635,19 +649,19 @@
             pltpu.VMEM((2, width, block), BF16),
             pltpu.SemaphoreType.DMA((2, 2)),
         ],
-        limit=20,
+        limit=22,
     )
     parts = plane_scatter(keep, swap(send))
     parts = [parts[0], *to_chips(parts)]
     col_share = width // narrow_count
     shares = kernel_call(
-        columns_kernel, [((count, col_share), BF16)] * narrow_count, (place, *parts)
+        functools.partial(columns_kernel, narrow_count),
+        [((count, col_share), BF16)] * narrow_count, parts
     )
     (layer_out,) = kernel_call(
-        final_kernel,
+        functools.partial(final_kernel, narrow_count),
         [((count, col_share), BF16)],
         (
-            place,
             residual,
             shares[0],
             *[to_narrow(shares[k], k) for k in range(1, narrow_count)],

time: 116 us -> 111 us (0.957)
  waiting for transfers between devices: 40.6 us -> 36.7 us
  Pallas kernels: 43.7 us -> 41.9 us
    ppermute x15, waiting for transfers between devices: 19.4 us -> 15.4 us  [to_chip(): lax.ppermute(values, 'wide', [(i, i ^ 2 * k) for i in range(wide_count)])]
    pallas_call x17 -> x19, Pallas kernels: 43.7 us -> 41.9 us  [kernel_call(): pl.pallas_call(body, out_shape=[pltpu.VMEM(*out) if i < pinned else jax.S...]
  transfers between devices with their start and end apart: 35 -> 35, of which waited for: 24 -> 23; matrix products, arithmetic and copies ran while one was open for 0% -> 0% of each run, Pallas kernels for 12% -> 16%
where the time goes in v3:
time: 111 us
  Pallas kernels  41.9 us (38%)
  waiting for transfers between devices  36.7 us (33%)
  starting transfers between devices  31.4 us (28%)
    pallas_call x19, Pallas kernels, kernel_call(): pl.pallas_call(body, out_shape=[pltpu.VMEM(*out) if i < pinned else jax.S...  41.9 us
    ppermute x15, starting transfers between devices, to_chip(): lax.ppermute(values, 'wide', [(i, i ^ 2 * k) for i in range(wide_count)])  18.8 us
    ppermute x15, waiting for transfers between devices, to_chip(): lax.ppermute(values, 'wide', [(i, i ^ 2 * k) for i in range(wide_count)])  15.4 us
    ppermute x8, waiting for transfers between devices, to_narrow(): lax.ppermute(values, 'narrow', [(i, i ^ k) for i in range(narrow_count)])  12.8 us
    ppermute x8, starting transfers between devices, to_narrow(): lax.ppermute(values, 'narrow', [(i, i ^ k) for i in range(narrow_count)])  11.1 us
    ppermute x12, waiting for transfers between devices, swap(): return lax.ppermute(values, 'wide', [(i, i ^ 1) for i in range(wide_count)])  8.45 us
  transfers between devices with their start and end apart: 35, of which 23 were waited for; matrix products, arithmetic and copies ran while one was open for 0% of the time, Pallas kernels for 16%

profile of v3, /device:TPU:0, one launch (start us, length us, event | category | flops | bytes accessed | tf_op | source)
XLA Modules:
  0.0 110.8 jit_solution(11286198270786806184)
XLA Ops:
  0.6 3.0 %collective-permute-start.1 = (bf16[16,4096]{1,0:T(8,128)(2,1)}, bf16[16,4096]{1,0:T(8,128)(2,1)S(1)}, u32[]{:S(2)}, u32[]{:S(2)}) collective-permute-start(bf16[16,4096]{1,0:T(8,128)(2,1)} %hidden.1), channel_id=1, source_target_pairs={{0,8},{4,12},{8,0},{12,4},{16,24},{20,28},{24,16},{28,20},{1,9},{5... | collective-permute-start | bytes 393224 | tf_op jit(solution)/shard_map/ppermute | solution.py:430
  3.6 1.5 %collective-permute-start.5 = (bf16[16,4096]{1,0:T(8,128)(2,1)}, bf16[16,4096]{1,0:T(8,128)(2,1)S(1)}, u32[]{:S(2)}, u32[]{:S(2)}) collective-permute-start(bf16[16,4096]{1,0:T(8,128)(2,1)} %hidden.1), channel_id=1, source_target_pairs={{0,24},{4,28},{8,16},{12,20},{16,8},{20,12},{24,0},{28,4},{1,25},{... | collective-permute-start | bytes 393224 | tf_op jit(solution)/shard_map/ppermute | solution.py:430
  5.2 2.5 %shard_map.203 = (bf16[2,256,4096]{2,1,0:T(8,128)(2,1)S(1)}, bf16[3,256,128]{2,1,0:T(8,128)(2,1)S(1)}, bf16[288,256]{1,0:T(8,128)(2,1)S(1)}, bf16[16,4096]{1,0:T...) custom-call(bf16[2,256,4096]{2,1,0:T(8,128)(2,1)} %in_weight.1, ...), custom_call_target="tpu_custom_call" | custom-call | bytes 8388608 | tf_op jit(solution)/shard_map/pallas_call | solution.py:29
  8.3 3.2 %collective-permute-done.5.refs_6_ = bf16[16,4096]{1,0:T(8,128)(2,1)S(1)} collective-permute-done((bf16[16,4096]{1,0:T(8,128)(2,1)}, bf16[16,4096]{1,0:T(8,128)(2,1)S(1)}, u32[]{:S(2)}, u32[]{:S(2)}) %collective-permute-start.5) | collective-permute-done | bytes 131104 | tf_op jit(solution)/shard_map/ppermute | solution.py:430
  11.5 1.4 %collective-permute-done.3.refs_4_ = bf16[16,4096]{1,0:T(8,128)(2,1)S(1)} collective-permute-done((bf16[16,4096]{1,0:T(8,128)(2,1)}, bf16[16,4096]{1,0:T(8,128)(2,1)S(1)}, u32[]{:S(2)}, u32[]{:S(2)}) %collective-permute-start.3) | collective-permute-done | bytes 131104 | tf_op jit(solution)/shard_map/ppermute | solution.py:430
  12.8 1.3 %collective-permute-done.4.refs_5_ = bf16[16,4096]{1,0:T(8,128)(2,1)S(1)} collective-permute-done((bf16[16,4096]{1,0:T(8,128)(2,1)S(1)}, bf16[16,4096]{1,0:T(8,128)(2,1)S(1)}, u32[]{:S(2)}, u32[]{:S(2)}) %collective-permute-start.4) | collective-permute-done | bytes 131104 | tf_op jit(solution)/shard_map/ppermute | solution.py:427
  14.2 3.1 %shard_map.204 = (f32[256,128]{1,0:T(8,128)S(1)}, f32[256,128]{1,0:T(8,128)S(1)}, bf16[144,128]{1,0:T(8,128)(2,1)S(1)}, bf16[144,128]{1,0:T(8,128)(2,1)S(1)}) custom-call(bf16[16,4096]{1,0:T(8,128)(2,1)S(1)} %get-tuple-element.49.refs_0_.hidden, bf16[16,4096]{1,0:T(8,128)(2,1)S(1)} %collective-permute-done.refs_1_, ...), custom_call_target="tpu_custom_call" | custom-call | tf_op jit(solution)/shard_map/pallas_call | solution.py:29
  17.5 1.1 collective-permute-done.7.refs_1_
  18.5 1.5 %collective-permute-start.10 = (bf16[144,128]{1,0:T(8,128)(2,1)S(1)}, bf16[144,128]{1,0:T(8,128)(2,1)S(1)}, u32[]{:S(2)}, u32[]{:S(2)}) collective-permute-start(bf16[144,128]{1,0:T(8,128)(2,1)S(1)} %shard_map.205.after.refs_0_), channel_id=1, source_target_pairs={{0,24},{4,28},{8,16},{12,20},{16,8},{20,12},{24,0},{28,4},{1,25},{... | collective-permute-start | bytes 110600 | tf_op jit(solution)/shard_map/ppermute | solution.py:430
  20.0 1.5 %collective-permute-start.9 = (bf16[144,128]{1,0:T(8,128)(2,1)S(1)}, bf16[144,128]{1,0:T(8,128)(2,1)S(1)}, u32[]{:S(2)}, u32[]{:S(2)}) collective-permute-start(bf16[144,128]{1,0:T(8,128)(2,1)S(1)} %shard_map.205.after.refs_0_), channel_id=1, source_target_pairs={{0,16},{4,20},{8,24},{12,28},{16,0},{20,4},{24,8},{28,12},{1,17},{... | collective-permute-start | bytes 110600 | tf_op jit(solution)/shard_map/ppermute | solution.py:430
  21.6 0.5 collective-permute-start.8
  22.1 1.9 %shard_map.206 = (bf16[256,4096]{1,0:T(8,128)(2,1)S(1)}, bf16[256,256]{1,0:T(8,128)(2,1)S(1)}, bf16[256,16,128]{2,1,0:T(8,128)(2,1)S(1)}, f32[8,128]{1,0:T(8,128)S(1)}) custom-call(bf16[144,128]{1,0:T(8,128)(2,1)S(1)} %shard_map.205.after.refs_0_, bf16[256,4096]{1,0:T(8,128)(2,1)} %first.2, bf16[256,256]{1,0:T(8,128)(2,1)} %second.2, bf16[256,16,128]{2,1,0:T(8,128)(2,1)} %third.1), custom_call_target="tpu_custom_call" | custom-call | bytes 6291456 | tf_op jit(solution)/shard_map/pallas_call | solution.py:29
  24.0 1.5 %collective-permute-done.8.refs_1_ = bf16[144,128]{1,0:T(8,128)(2,1)S(1)} collective-permute-done((bf16[144,128]{1,0:T(8,128)(2,1)S(1)}, bf16[144,128]{1,0:T(8,128)(2,1)S(1)}, u32[]{:S(2)}, u32[]{:S(2)}) %collective-permute-start.8) | collective-permute-done | bytes 36896 | tf_op jit(solution)/shard_map/ppermute | solution.py:430
  25.5 3.7 %collective-permute-start.13 = (bf16[144,128]{1,0:T(8,128)(2,1)S(1)}, bf16[144,128]{1,0:T(8,128)(2,1)S(1)}, u32[]{:S(2)}, u32[]{:S(2)}) collective-permute-start(bf16[144,128]{1,0:T(8,128)(2,1)S(1)} %shard_map.207.refs_0_), channel_id=1, source_target_pairs={{0,3},{1,2},{2,1},{3,0},{4,7},{5,6},{6,5},{7,4},{8,11},{9,10},{10,... | collective-permute-start | bytes 110600 | tf_op jit(solution)/shard_map/ppermute | solution.py:433
  29.2 0.8 collective-permute-start.11
  30.0 1.4 %collective-permute-done.13.refs_3_ = bf16[144,128]{1,0:T(8,128)(2,1)S(1)} collective-permute-done((bf16[144,128]{1,0:T(8,128)(2,1)S(1)}, bf16[144,128]{1,0:T(8,128)(2,1)S(1)}, u32[]{:S(2)}, u32[]{:S(2)}) %collective-permute-start.13) | collective-permute-done | bytes 36896 | tf_op jit(solution)/shard_map/ppermute | solution.py:433
  31.4 2.7 %collective-permute-done.12.refs_2_ = bf16[144,128]{1,0:T(8,128)(2,1)S(1)} collective-permute-done((bf16[144,128]{1,0:T(8,128)(2,1)S(1)}, bf16[144,128]{1,0:T(8,128)(2,1)S(1)}, u32[]{:S(2)}, u32[]{:S(2)}) %collective-permute-start.12) | collective-permute-done | bytes 36896 | tf_op jit(solution)/shard_map/ppermute | solution.py:433
  34.2 1.2 %collective-permute-done.14.other_half = bf16[144,128]{1,0:T(8,128)(2,1)S(1)} collective-permute-done((bf16[144,128]{1,0:T(8,128)(2,1)S(1)}, bf16[144,128]{1,0:T(8,128)(2,1)S(1)}, u32[]{:S(2)}, u32[]{:S(2)}) %collective-permute-start.14) | collective-permute-done | bytes 36896 | tf_op jit(solution)/shard_map/ppermute | solution.py:427
  35.4 3.0 %shard_map.209 = (bf16[256,16,128]{2,1,0:T(8,128)(2,1)}, bf16[64,4096]{1,0:T(8,128)(2,1)S(1)}, bf16[64,4096]{1,0:T(8,128)(2,1)S(1)}) custom-call(bf16[144,128]{1,0:T(8,128)(2,1)S(1)} %shard_map.208.own_half, bf16[144,128]{1,0:T(8,128)(2,1)S(1)} %collective-permute-done.14.other_half, f32[256,128]{1,0:T(8,128)S(1)} %get-tuple-element.58.step_gain, ...), custom_call_target="tpu_custom_call" | custom-call | tf_op jit(solution)/shard_map/pallas_call | solution.py:29
  38.5 1.7 %collective-permute-done.15.got = bf16[64,4096]{1,0:T(8,128)(2,1)S(1)} collective-permute-done((bf16[64,4096]{1,0:T(8,128)(2,1)S(1)}, bf16[64,4096]{1,0:T(8,128)(2,1)S(1)}, u32[]{:S(2)}, u32[]{:S(2)}) %collective-permute-start.15) | collective-permute-done | bytes 524320 | tf_op jit(solution)/shard_map/ppermute | solution.py:427
  40.4 0.6 collective-permute-start.16
  41.5 2.4 %collective-permute-start.18 = (bf16[16,4096]{1,0:T(8,128)(2,1)S(1)}, bf16[16,4096]{1,0:T(8,128)(2,1)S(1)}, u32[]{:S(2)}, u32[]{:S(2)}) collective-permute-start(bf16[16,4096]{1,0:T(8,128)(2,1)S(1)} %get-tuple-element.70), channel_id=1, source_target_pairs={{0,24},{4,28},{8,16},{12,20},{16,8},{20,12},{24,0},{28,4},{1,25},{... | collective-permute-start | bytes 393224 | tf_op jit(solution)/shard_map/ppermute | solution.py:430
  43.9 3.5 %shard_map.211 = (bf16[512,4096]{1,0:T(8,128)(2,1)S(1)}, bf16[512,4096]{1,0:T(8,128)(2,1)S(1)}, f32[8,128]{1,0:T(8,128)S(1)}) custom-call(bf16[16,4096]{1,0:T(8,128)(2,1)S(1)} %get-tuple-element.67.after.refs_0_, bf16[3072,4096]{1,0:T(8,128)(2,1)} %source.5), custom_call_target="tpu_custom_call" | custom-call | bytes 16777216 | tf_op jit(solution)/shard_map/pallas_call | solution.py:29
  47.5 1.6 %collective-permute-done.17.refs_2_ = bf16[16,4096]{1,0:T(8,128)(2,1)S(1)} collective-permute-done((bf16[16,4096]{1,0:T(8,128)(2,1)S(1)}, bf16[16,4096]{1,0:T(8,128)(2,1)S(1)}, u32[]{:S(2)}, u32[]{:S(2)}) %collective-permute-start.17) | collective-permute-done | bytes 131104 | tf_op jit(solution)/shard_map/ppermute | solution.py:430
  49.2 3.5 %shard_map.213 = (bf16[512,4096]{1,0:T(8,128)(2,1)S(1)}, bf16[512,4096]{1,0:T(8,128)(2,1)S(1)}, f32[8,128]{1,0:T(8,128)S(1)}) custom-call(bf16[16,4096]{1,0:T(8,128)(2,1)S(1)} %shard_map.212.after.refs_0_, bf16[3072,4096]{1,0:T(8,128)(2,1)} %source.5), custom_call_target="tpu_custom_call" | custom-call | bytes 16777216 | tf_op jit(solution)/shard_map/pallas_call | solution.py:29
  52.7 1.4 %collective-permute-done.19.refs_1_ = bf16[16,4096]{1,0:T(8,128)(2,1)S(1)} collective-permute-done((bf16[16,4096]{1,0:T(8,128)(2,1)S(1)}, bf16[16,4096]{1,0:T(8,128)(2,1)S(1)}, u32[]{:S(2)}, u32[]{:S(2)}) %collective-permute-start.19) | collective-permute-done | bytes 131104 | tf_op jit(solution)/shard_map/ppermute | solution.py:433
  54.2 2.1 %collective-permute-start.20 = (bf16[16,4096]{1,0:T(8,128)(2,1)S(1)}, bf16[16,4096]{1,0:T(8,128)(2,1)S(1)}, u32[]{:S(2)}, u32[]{:S(2)}) collective-permute-start(bf16[16,4096]{1,0:T(8,128)(2,1)S(1)} %shard_map.214.after.mine), channel_id=1, source_target_pairs={{0,2},{1,3},{2,0},{3,1},{4,6},{5,7},{6,4},{7,5},{8,10},{9,11},{10,... | collective-permute-start | bytes 393224 | tf_op jit(solution)/shard_map/ppermute | solution.py:433
  56.3 3.5 %shard_map.215 = (bf16[512,4096]{1,0:T(8,128)(2,1)S(1)}, bf16[512,4096]{1,0:T(8,128)(2,1)S(1)}, f32[8,128]{1,0:T(8,128)S(1)}) custom-call(bf16[16,4096]{1,0:T(8,128)(2,1)S(1)} %shard_map.214.after.mine, bf16[3072,4096]{1,0:T(8,128)(2,1)} %source.5), custom_call_target="tpu_custom_call" | custom-call | bytes 16777216 | tf_op jit(solution)/shard_map/pallas_call | solution.py:29
  59.8 1.7 %collective-permute-done.20.got = bf16[16,4096]{1,0:T(8,128)(2,1)S(1)} collective-permute-done((bf16[16,4096]{1,0:T(8,128)(2,1)S(1)}, bf16[16,4096]{1,0:T(8,128)(2,1)S(1)}, u32[]{:S(2)}, u32[]{:S(2)}) %collective-permute-start.20) | collective-permute-done | bytes 131104 | tf_op jit(solution)/shard_map/ppermute | solution.py:433
  61.6 1.5 %collective-permute-start.23 = (bf16[16,4224]{1,0:T(8,128)(2,1)S(1)}, bf16[16,4224]{1,0:T(8,128)(2,1)S(1)}, u32[]{:S(2)}, u32[]{:S(2)}) collective-permute-start(bf16[16,4224]{1,0:T(8,128)(2,1)S(1)} %shard_map.216.block.residual), channel_id=1, source_target_pairs={{0,24},{4,28},{8,16},{12,20},{16,8},{20,12},{24,0},{28,4},{1,25},{... | collective-permute-start | bytes 405512 | tf_op jit(solution)/shard_map/ppermute | solution.py:430
  63.1 1.5 %collective-permute-start.22 = (bf16[16,4224]{1,0:T(8,128)(2,1)S(1)}, bf16[16,4224]{1,0:T(8,128)(2,1)S(1)}, u32[]{:S(2)}, u32[]{:S(2)}) collective-permute-start(bf16[16,4224]{1,0:T(8,128)(2,1)S(1)} %shard_map.216.block.residual), channel_id=1, source_target_pairs={{0,16},{4,20},{8,24},{12,28},{16,0},{20,4},{24,8},{28,12},{1,17},{... | collective-permute-start | bytes 405512 | tf_op jit(solution)/shard_map/ppermute | solution.py:430
  64.6 0.5 collective-permute-start.21
  65.2 2.3 %shard_map.217 = (bf16[4096,256]{1,0:T(8,128)(2,1)S(1)}, bf16[4096,256]{1,0:T(8,128)(2,1)S(1)}, bf16[16,4224]{1,0:T(8,128)(2,1)S(1)}) custom-call(bf16[16,4224]{1,0:T(8,128)(2,1)S(1)} %shard_map.216.block.residual, bf16[4096,3072]{1,0:T(8,128)(2,1)} %refs_17_.1, bf16[4096,3072]{1,0:T(8,128)(2,1)} %refs_18_.1), custom_call_target="tpu_custom_call" | custom-call | bytes 8388608 | tf_op jit(solution)/shard_map/pallas_call | solution.py:29
  68.0 1.0 collective-permute-done.22.refs_2_
  69.0 0.6 collective-permute-done.21.refs_1_
  69.7 0.7 collective-permute-done.26.refs_6_
  70.4 0.6 collective-permute-done.25.refs_5_
  71.0 17.5 %shard_map.218 = (bf16[64,4096]{1,0:T(8,128)(2,1)S(1)}, bf16[64,4096]{1,0:T(8,128)(2,1)S(1)}) custom-call(bf16[16,4224]{1,0:T(8,128)(2,1)S(1)} %get-tuple-element.75.refs_0_, bf16[16,4224]{1,0:T(8,128)(2,1)S(1)} %collective-permute-done.21.refs_1_, bf16[16,4224]{1,0:T(8,128)(2,1)S(1)} %collective-permute-done.22.refs_2_, ...), custom_call_target="tpu_custom_call" | custom-call | tf_op jit(solution)/shard_map/pallas_call | solution.py:29
  88.7 1.8 %collective-permute-done.28.got = bf16[64,4096]{1,0:T(8,128)(2,1)S(1)} collective-permute-done((bf16[64,4096]{1,0:T(8,128)(2,1)S(1)}, bf16[64,4096]{1,0:T(8,128)(2,1)S(1)}, u32[]{:S(2)}, u32[]{:S(2)}) %collective-permute-start.28) | collective-permute-done | bytes 524320 | tf_op jit(solution)/shard_map/ppermute | solution.py:427
  90.6 1.2 %collective-permute-start.29 = (bf16[16,4096]{1,0:T(8,128)(2,1)S(1)}, bf16[16,4096]{1,0:T(8,128)(2,1)S(1)}, u32[]{:S(2)}, u32[]{:S(2)}) collective-permute-start(bf16[16,4096]{1,0:T(8,128)(2,1)S(1)} %get-tuple-element.88), channel_id=1, source_target_pairs={{0,8},{4,12},{8,0},{12,4},{16,24},{20,28},{24,16},{28,20},{1,9},{5... | collective-permute-start | bytes 393224 | tf_op jit(solution)/shard_map/ppermute | solution.py:430
  91.8 0.6 collective-permute-start.30
  92.4 1.7 %collective-permute-start.31 = (bf16[16,4096]{1,0:T(8,128)(2,1)S(1)}, bf16[16,4096]{1,0:T(8,128)(2,1)S(1)}, u32[]{:S(2)}, u32[]{:S(2)}) collective-permute-start(bf16[16,4096]{1,0:T(8,128)(2,1)S(1)} %get-tuple-element.90), channel_id=1, source_target_pairs={{0,24},{4,28},{8,16},{12,20},{16,8},{20,12},{24,0},{28,4},{1,25},{... | collective-permute-start | bytes 393224 | tf_op jit(solution)/shard_map/ppermute | solution.py:430
  94.1 2.6 %collective-permute-done.29.refs_1_ = bf16[16,4096]{1,0:T(8,128)(2,1)S(1)} collective-permute-done((bf16[16,4096]{1,0:T(8,128)(2,1)S(1)}, bf16[16,4096]{1,0:T(8,128)(2,1)S(1)}, u32[]{:S(2)}, u32[]{:S(2)}) %collective-permute-start.29) | collective-permute-done | bytes 131104 | tf_op jit(solution)/shard_map/ppermute | solution.py:430
  96.7 3.4 %collective-permute-done.30.refs_2_ = bf16[16,4096]{1,0:T(8,128)(2,1)S(1)} collective-permute-done((bf16[16,4096]{1,0:T(8,128)(2,1)S(1)}, bf16[16,4096]{1,0:T(8,128)(2,1)S(1)}, u32[]{:S(2)}, u32[]{:S(2)}) %collective-permute-start.30) | collective-permute-done | bytes 131104 | tf_op jit(solution)/shard_map/ppermute | solution.py:430
  100.2 4.2 %collective-permute-start.33 = (bf16[16,1024]{1,0:T(8,128)(2,1)S(1)}, bf16[16,1024]{1,0:T(8,128)(2,1)S(1)}, u32[]{:S(2)}, u32[]{:S(2)}) collective-permute-start(bf16[16,1024]{1,0:T(8,128)(2,1)S(1)} %get-tuple-element.93), channel_id=1, source_target_pairs={{0,2},{1,3},{2,0},{3,1},{4,6},{5,7},{6,4},{7,5},{8,10},{9,11},{10,... | collective-permute-start | bytes 98312 | tf_op jit(solution)/shard_map/ppermute | solution.py:433
  104.6 2.2 %collective-permute-done.33.refs_2_ = bf16[16,1024]{1,0:T(8,128)(2,1)S(1)} collective-permute-done((bf16[16,1024]{1,0:T(8,128)(2,1)S(1)}, bf16[16,1024]{1,0:T(8,128)(2,1)S(1)}, u32[]{:S(2)}, u32[]{:S(2)}) %collective-permute-start.33) | collective-permute-done | bytes 32800 | tf_op jit(solution)/shard_map/ppermute | solution.py:433
  106.8 3.3 %collective-permute-done.34.refs_3_ = bf16[16,1024]{1,0:T(8,128)(2,1)S(1)} collective-permute-done((bf16[16,1024]{1,0:T(8,128)(2,1)S(1)}, bf16[16,1024]{1,0:T(8,128)(2,1)S(1)}, u32[]{:S(2)}, u32[]{:S(2)}) %collective-permute-start.34) | collective-permute-done | bytes 32800 | tf_op jit(solution)/shard_map/ppermute | solution.py:433
  110.1 0.6 shard_map.221
  (41 shorter events, 3.3 us)
Async XLA Ops:
  0.6 7.2 %collective-permute-start.1 = (bf16[16,4096]{1,0:T(8,128)(2,1)}, bf16[16,4096]{1,0:T(8,128)(2,1)S(1)}, u32[]{:S(2)}, u32[]{:S(2)}) collective-permute-start(bf16[16,4096]{1,0:T(8,128)(2,1)} %hidden.1), channel_id=1, source_target_pairs={{0,8},{4,12},{8,0},{12,4},{16,24},{20,28},{24,16},{28,20},{1,9},{5... | collective-permute-start | bytes 393224 | tf_op jit(solution)/shard_map/ppermute | solution.py:430
  3.6 7.8 %collective-permute-start.5 = (bf16[16,4096]{1,0:T(8,128)(2,1)}, bf16[16,4096]{1,0:T(8,128)(2,1)S(1)}, u32[]{:S(2)}, u32[]{:S(2)}) collective-permute-start(bf16[16,4096]{1,0:T(8,128)(2,1)} %hidden.1), channel_id=1, source_target_pairs={{0,24},{4,28},{8,16},{12,20},{16,8},{20,12},{24,0},{28,4},{1,25},{... | collective-permute-start | bytes 393224 | tf_op jit(solution)/shard_map/ppermute | solution.py:430
  5.1 7.7 %collective-permute-start.3 = (bf16[16,4096]{1,0:T(8,128)(2,1)}, bf16[16,4096]{1,0:T(8,128)(2,1)S(1)}, u32[]{:S(2)}, u32[]{:S(2)}) collective-permute-start(bf16[16,4096]{1,0:T(8,128)(2,1)} %hidden.1), channel_id=1, source_target_pairs={{0,16},{4,20},{8,24},{12,28},{16,0},{20,4},{24,8},{28,12},{1,17},{... | collective-permute-start | bytes 393224 | tf_op jit(solution)/shard_map/ppermute | solution.py:430
  7.7 5.1 %collective-permute-start = (bf16[16,4096]{1,0:T(8,128)(2,1)S(1)}, bf16[16,4096]{1,0:T(8,128)(2,1)S(1)}, u32[]{:S(2)}, u32[]{:S(2)}) collective-permute-start(bf16[16,4096]{1,0:T(8,128)(2,1)S(1)} %get-tuple-element.49.refs_0_.hidden), channel_id=1, source_target_pairs={{0,4},{4,0},{8,12},{12,8},{16,20},{20,16},{24,28},{28,24},{1,5},{5... | collective-permute-start | bytes 393224 | tf_op jit(solution)/shard_map/ppermute | solution.py:427
  7.9 5.0 %collective-permute-start.2 = (bf16[16,4096]{1,0:T(8,128)(2,1)S(1)}, bf16[16,4096]{1,0:T(8,128)(2,1)S(1)}, u32[]{:S(2)}, u32[]{:S(2)}) collective-permute-start(bf16[16,4096]{1,0:T(8,128)(2,1)S(1)} %collective-permute-done.1.refs_2_), channel_id=1, source_target_pairs={{0,4},{4,0},{8,12},{12,8},{16,20},{20,16},{24,28},{28,24},{1,5},{5... | collective-permute-start | bytes 393224 | tf_op jit(solution)/shard_map/ppermute | solution.py:427
  11.5 1.4 %collective-permute-start.6 = (bf16[16,4096]{1,0:T(8,128)(2,1)S(1)}, bf16[16,4096]{1,0:T(8,128)(2,1)S(1)}, u32[]{:S(2)}, u32[]{:S(2)}) collective-permute-start(bf16[16,4096]{1,0:T(8,128)(2,1)S(1)} %collective-permute-done.5.refs_6_), channel_id=1, source_target_pairs={{0,4},{4,0},{8,12},{12,8},{16,20},{20,16},{24,28},{28,24},{1,5},{5... | collective-permute-start | bytes 393224 | tf_op jit(solution)/shard_map/ppermute | solution.py:427
  12.8 1.3 %collective-permute-start.4 = (bf16[16,4096]{1,0:T(8,128)(2,1)S(1)}, bf16[16,4096]{1,0:T(8,128)(2,1)S(1)}, u32[]{:S(2)}, u32[]{:S(2)}) collective-permute-start(bf16[16,4096]{1,0:T(8,128)(2,1)S(1)} %collective-permute-done.3.refs_4_), channel_id=1, source_target_pairs={{0,4},{4,0},{8,12},{12,8},{16,20},{20,16},{24,28},{28,24},{1,5},{5... | collective-permute-start | bytes 393224 | tf_op jit(solution)/shard_map/ppermute | solution.py:427
  17.2 1.3 %collective-permute-start.7 = (bf16[144,128]{1,0:T(8,128)(2,1)S(1)}, bf16[144,128]{1,0:T(8,128)(2,1)S(1)}, u32[]{:S(2)}, u32[]{:S(2)}) collective-permute-start(bf16[144,128]{1,0:T(8,128)(2,1)S(1)} %get-tuple-element.56), channel_id=1, source_target_pairs={{0,4},{4,0},{8,12},{12,8},{16,20},{20,16},{24,28},{28,24},{1,5},{5... | collective-permute-start | bytes 110600 | tf_op jit(solution)/shard_map/ppermute | solution.py:427
  18.5 5.5 %collective-permute-start.10 = (bf16[144,128]{1,0:T(8,128)(2,1)S(1)}, bf16[144,128]{1,0:T(8,128)(2,1)S(1)}, u32[]{:S(2)}, u32[]{:S(2)}) collective-permute-start(bf16[144,128]{1,0:T(8,128)(2,1)S(1)} %shard_map.205.after.refs_0_), channel_id=1, source_target_pairs={{0,24},{4,28},{8,16},{12,20},{16,8},{20,12},{24,0},{28,4},{1,25},{... | collective-permute-start | bytes 110600 | tf_op jit(solution)/shard_map/ppermute | solution.py:430
  20.0 4.0 %collective-permute-start.9 = (bf16[144,128]{1,0:T(8,128)(2,1)S(1)}, bf16[144,128]{1,0:T(8,128)(2,1)S(1)}, u32[]{:S(2)}, u32[]{:S(2)}) collective-permute-start(bf16[144,128]{1,0:T(8,128)(2,1)S(1)} %shard_map.205.after.refs_0_), channel_id=1, source_target_pairs={{0,16},{4,20},{8,24},{12,28},{16,0},{20,4},{24,8},{28,12},{1,17},{... | collective-permute-start | bytes 110600 | tf_op jit(solution)/shard_map/ppermute | solution.py:430
  21.6 4.0 %collective-permute-start.8 = (bf16[144,128]{1,0:T(8,128)(2,1)S(1)}, bf16[144,128]{1,0:T(8,128)(2,1)S(1)}, u32[]{:S(2)}, u32[]{:S(2)}) collective-permute-start(bf16[144,128]{1,0:T(8,128)(2,1)S(1)} %shard_map.205.after.refs_0_), channel_id=1, source_target_pairs={{0,8},{4,12},{8,0},{12,4},{16,24},{20,28},{24,16},{28,20},{1,9},{5... | collective-permute-start | bytes 110600 | tf_op jit(solution)/shard_map/ppermute | solution.py:430
  25.5 5.9 %collective-permute-start.13 = (bf16[144,128]{1,0:T(8,128)(2,1)S(1)}, bf16[144,128]{1,0:T(8,128)(2,1)S(1)}, u32[]{:S(2)}, u32[]{:S(2)}) collective-permute-start(bf16[144,128]{1,0:T(8,128)(2,1)S(1)} %shard_map.207.refs_0_), channel_id=1, source_target_pairs={{0,3},{1,2},{2,1},{3,0},{4,7},{5,6},{6,5},{7,4},{8,11},{9,10},{10,... | collective-permute-start | bytes 110600 | tf_op jit(solution)/shard_map/ppermute | solution.py:433
  29.2 4.9 %collective-permute-start.12 = (bf16[144,128]{1,0:T(8,128)(2,1)S(1)}, bf16[144,128]{1,0:T(8,128)(2,1)S(1)}, u32[]{:S(2)}, u32[]{:S(2)}) collective-permute-start(bf16[144,128]{1,0:T(8,128)(2,1)S(1)} %shard_map.207.refs_0_), channel_id=1, source_target_pairs={{0,2},{1,3},{2,0},{3,1},{4,6},{5,7},{6,4},{7,5},{8,10},{9,11},{10,... | collective-permute-start | bytes 110600 | tf_op jit(solution)/shard_map/ppermute | solution.py:433
  29.2 4.9 %collective-permute-start.11 = (bf16[144,128]{1,0:T(8,128)(2,1)S(1)}, bf16[144,128]{1,0:T(8,128)(2,1)S(1)}, u32[]{:S(2)}, u32[]{:S(2)}) collective-permute-start(bf16[144,128]{1,0:T(8,128)(2,1)S(1)} %shard_map.207.refs_0_), channel_id=1, source_target_pairs={{0,1},{1,0},{2,3},{3,2},{4,5},{5,4},{6,7},{7,6},{8,9},{9,8},{10,11... | collective-permute-start | bytes 110600 | tf_op jit(solution)/shard_map/ppermute | solution.py:433
  34.1 1.3 %collective-permute-start.14 = (bf16[144,128]{1,0:T(8,128)(2,1)S(1)}, bf16[144,128]{1,0:T(8,128)(2,1)S(1)}, u32[]{:S(2)}, u32[]{:S(2)}) collective-permute-start(bf16[144,128]{1,0:T(8,128)(2,1)S(1)} %shard_map.208.own_half), channel_id=1, source_target_pairs={{0,4},{4,0},{8,12},{12,8},{16,20},{20,16},{24,28},{28,24},{1,5},{5... | collective-permute-start | bytes 110600 | tf_op jit(solution)/shard_map/ppermute | solution.py:427
  38.3 1.9 %collective-permute-start.15 = (bf16[64,4096]{1,0:T(8,128)(2,1)S(1)}, bf16[64,4096]{1,0:T(8,128)(2,1)S(1)}, u32[]{:S(2)}, u32[]{:S(2)}) collective-permute-start(bf16[64,4096]{1,0:T(8,128)(2,1)S(1)} %get-tuple-element.66), channel_id=1, source_target_pairs={{0,4},{4,0},{8,12},{12,8},{16,20},{20,16},{24,28},{28,24},{1,5},{5... | collective-permute-start | bytes 1572872 | tf_op jit(solution)/shard_map/ppermute | solution.py:427
  40.4 7.1 %collective-permute-start.16 = (bf16[16,4096]{1,0:T(8,128)(2,1)S(1)}, bf16[16,4096]{1,0:T(8,128)(2,1)S(1)}, u32[]{:S(2)}, u32[]{:S(2)}) collective-permute-start(bf16[16,4096]{1,0:T(8,128)(2,1)S(1)} %get-tuple-element.68), channel_id=1, source_target_pairs={{0,8},{4,12},{8,0},{12,4},{16,24},{20,28},{24,16},{28,20},{1,9},{5... | collective-permute-start | bytes 393224 | tf_op jit(solution)/shard_map/ppermute | solution.py:430
  41.0 8.1 %collective-permute-start.17 = (bf16[16,4096]{1,0:T(8,128)(2,1)S(1)}, bf16[16,4096]{1,0:T(8,128)(2,1)S(1)}, u32[]{:S(2)}, u32[]{:S(2)}) collective-permute-start(bf16[16,4096]{1,0:T(8,128)(2,1)S(1)} %get-tuple-element.69), channel_id=1, source_target_pairs={{0,16},{4,20},{8,24},{12,28},{16,0},{20,4},{24,8},{28,12},{1,17},{... | collective-permute-start | bytes 393224 | tf_op jit(solution)/shard_map/ppermute | solution.py:430
  41.5 7.6 %collective-permute-start.18 = (bf16[16,4096]{1,0:T(8,128)(2,1)S(1)}, bf16[16,4096]{1,0:T(8,128)(2,1)S(1)}, u32[]{:S(2)}, u32[]{:S(2)}) collective-permute-start(bf16[16,4096]{1,0:T(8,128)(2,1)S(1)} %get-tuple-element.70), channel_id=1, source_target_pairs={{0,24},{4,28},{8,16},{12,20},{16,8},{20,12},{24,0},{28,4},{1,25},{... | collective-permute-start | bytes 393224 | tf_op jit(solution)/shard_map/ppermute | solution.py:430
  49.2 5.0 %collective-permute-start.19 = (bf16[16,4096]{1,0:T(8,128)(2,1)S(1)}, bf16[16,4096]{1,0:T(8,128)(2,1)S(1)}, u32[]{:S(2)}, u32[]{:S(2)}) collective-permute-start(bf16[16,4096]{1,0:T(8,128)(2,1)S(1)} %shard_map.212.after.refs_0_), channel_id=1, source_target_pairs={{0,1},{1,0},{2,3},{3,2},{4,5},{5,4},{6,7},{7,6},{8,9},{9,8},{10,11... | collective-permute-start | bytes 393224 | tf_op jit(solution)/shard_map/ppermute | solution.py:433
  54.2 7.3 %collective-permute-start.20 = (bf16[16,4096]{1,0:T(8,128)(2,1)S(1)}, bf16[16,4096]{1,0:T(8,128)(2,1)S(1)}, u32[]{:S(2)}, u32[]{:S(2)}) collective-permute-start(bf16[16,4096]{1,0:T(8,128)(2,1)S(1)} %shard_map.214.after.mine), channel_id=1, source_target_pairs={{0,2},{1,3},{2,0},{3,1},{4,6},{5,7},{6,4},{7,5},{8,10},{9,11},{10,... | collective-permute-start | bytes 393224 | tf_op jit(solution)/shard_map/ppermute | solution.py:433
  61.6 6.1 %collective-permute-start.23 = (bf16[16,4224]{1,0:T(8,128)(2,1)S(1)}, bf16[16,4224]{1,0:T(8,128)(2,1)S(1)}, u32[]{:S(2)}, u32[]{:S(2)}) collective-permute-start(bf16[16,4224]{1,0:T(8,128)(2,1)S(1)} %shard_map.216.block.residual), channel_id=1, source_target_pairs={{0,24},{4,28},{8,16},{12,20},{16,8},{20,12},{24,0},{28,4},{1,25},{... | collective-permute-start | bytes 405512 | tf_op jit(solution)/shard_map/ppermute | solution.py:430
  63.1 5.9 %collective-permute-start.22 = (bf16[16,4224]{1,0:T(8,128)(2,1)S(1)}, bf16[16,4224]{1,0:T(8,128)(2,1)S(1)}, u32[]{:S(2)}, u32[]{:S(2)}) collective-permute-start(bf16[16,4224]{1,0:T(8,128)(2,1)S(1)} %shard_map.216.block.residual), channel_id=1, source_target_pairs={{0,16},{4,20},{8,24},{12,28},{16,0},{20,4},{24,8},{28,12},{1,17},{... | collective-permute-start | bytes 405512 | tf_op jit(solution)/shard_map/ppermute | solution.py:430
  64.6 5.0 %collective-permute-start.21 = (bf16[16,4224]{1,0:T(8,128)(2,1)S(1)}, bf16[16,4224]{1,0:T(8,128)(2,1)S(1)}, u32[]{:S(2)}, u32[]{:S(2)}) collective-permute-start(bf16[16,4224]{1,0:T(8,128)(2,1)S(1)} %shard_map.216.block.residual), channel_id=1, source_target_pairs={{0,8},{4,12},{8,0},{12,4},{16,24},{20,28},{24,16},{28,20},{1,9},{5... | collective-permute-start | bytes 405512 | tf_op jit(solution)/shard_map/ppermute | solution.py:430
  67.4 2.2 %collective-permute-start.24 = (bf16[16,4224]{1,0:T(8,128)(2,1)S(1)}, bf16[16,4224]{1,0:T(8,128)(2,1)S(1)}, u32[]{:S(2)}, u32[]{:S(2)}) collective-permute-start(bf16[16,4224]{1,0:T(8,128)(2,1)S(1)} %get-tuple-element.75.refs_0_), channel_id=1, source_target_pairs={{0,4},{4,0},{8,12},{12,8},{16,20},{20,16},{24,28},{28,24},{1,5},{5... | collective-permute-start | bytes 405512 | tf_op jit(solution)/shard_map/ppermute | solution.py:427
  67.7 2.0 %collective-permute-start.27 = (bf16[16,4224]{1,0:T(8,128)(2,1)S(1)}, bf16[16,4224]{1,0:T(8,128)(2,1)S(1)}, u32[]{:S(2)}, u32[]{:S(2)}) collective-permute-start(bf16[16,4224]{1,0:T(8,128)(2,1)S(1)} %collective-permute-done.23.refs_3_), channel_id=1, source_target_pairs={{0,4},{4,0},{8,12},{12,8},{16,20},{20,16},{24,28},{28,24},{1,5},{5... | collective-permute-start | bytes 405512 | tf_op jit(solution)/shard_map/ppermute | solution.py:427
  69.0 1.4 %collective-permute-start.26 = (bf16[16,4224]{1,0:T(8,128)(2,1)S(1)}, bf16[16,4224]{1,0:T(8,128)(2,1)S(1)}, u32[]{:S(2)}, u32[]{:S(2)}) collective-permute-start(bf16[16,4224]{1,0:T(8,128)(2,1)S(1)} %collective-permute-done.22.refs_2_), channel_id=1, source_target_pairs={{0,4},{4,0},{8,12},{12,8},{16,20},{20,16},{24,28},{28,24},{1,5},{5... | collective-permute-start | bytes 405512 | tf_op jit(solution)/shard_map/ppermute | solution.py:427
  69.6 1.4 %collective-permute-start.25 = (bf16[16,4224]{1,0:T(8,128)(2,1)S(1)}, bf16[16,4224]{1,0:T(8,128)(2,1)S(1)}, u32[]{:S(2)}, u32[]{:S(2)}) collective-permute-start(bf16[16,4224]{1,0:T(8,128)(2,1)S(1)} %collective-permute-done.21.refs_1_), channel_id=1, source_target_pairs={{0,4},{4,0},{8,12},{12,8},{16,20},{20,16},{24,28},{28,24},{1,5},{5... | collective-permute-start | bytes 405512 | tf_op jit(solution)/shard_map/ppermute | solution.py:427
  88.5 2.0 %collective-permute-start.28 = (bf16[64,4096]{1,0:T(8,128)(2,1)S(1)}, bf16[64,4096]{1,0:T(8,128)(2,1)S(1)}, u32[]{:S(2)}, u32[]{:S(2)}) collective-permute-start(bf16[64,4096]{1,0:T(8,128)(2,1)S(1)} %get-tuple-element.86), channel_id=1, source_target_pairs={{0,4},{4,0},{8,12},{12,8},{16,20},{20,16},{24,28},{28,24},{1,5},{5... | collective-permute-start | bytes 1572872 | tf_op jit(solution)/shard_map/ppermute | solution.py:427
  90.6 6.1 %collective-permute-start.29 = (bf16[16,4096]{1,0:T(8,128)(2,1)S(1)}, bf16[16,4096]{1,0:T(8,128)(2,1)S(1)}, u32[]{:S(2)}, u32[]{:S(2)}) collective-permute-start(bf16[16,4096]{1,0:T(8,128)(2,1)S(1)} %get-tuple-element.88), channel_id=1, source_target_pairs={{0,8},{4,12},{8,0},{12,4},{16,24},{20,28},{24,16},{28,20},{1,9},{5... | collective-permute-start | bytes 393224 | tf_op jit(solution)/shard_map/ppermute | solution.py:430
  91.8 8.2 %collective-permute-start.30 = (bf16[16,4096]{1,0:T(8,128)(2,1)S(1)}, bf16[16,4096]{1,0:T(8,128)(2,1)S(1)}, u32[]{:S(2)}, u32[]{:S(2)}) collective-permute-start(bf16[16,4096]{1,0:T(8,128)(2,1)S(1)} %get-tuple-element.89), channel_id=1, source_target_pairs={{0,16},{4,20},{8,24},{12,28},{16,0},{20,4},{24,8},{28,12},{1,17},{... | collective-permute-start | bytes 393224 | tf_op jit(solution)/shard_map/ppermute | solution.py:430
  92.4 7.7 %collective-permute-start.31 = (bf16[16,4096]{1,0:T(8,128)(2,1)S(1)}, bf16[16,4096]{1,0:T(8,128)(2,1)S(1)}, u32[]{:S(2)}, u32[]{:S(2)}) collective-permute-start(bf16[16,4096]{1,0:T(8,128)(2,1)S(1)} %get-tuple-element.90), channel_id=1, source_target_pairs={{0,24},{4,28},{8,16},{12,20},{16,8},{20,12},{24,0},{28,4},{1,25},{... | collective-permute-start | bytes 393224 | tf_op jit(solution)/shard_map/ppermute | solution.py:430
  100.1 4.5 %collective-permute-start.32 = (bf16[16,1024]{1,0:T(8,128)(2,1)S(1)}, bf16[16,1024]{1,0:T(8,128)(2,1)S(1)}, u32[]{:S(2)}, u32[]{:S(2)}) collective-permute-start(bf16[16,1024]{1,0:T(8,128)(2,1)S(1)} %get-tuple-element.92), channel_id=1, source_target_pairs={{0,1},{1,0},{2,3},{3,2},{4,5},{5,4},{6,7},{7,6},{8,9},{9,8},{10,11... | collective-permute-start | bytes 98312 | tf_op jit(solution)/shard_map/ppermute | solution.py:433
  100.2 6.6 %collective-permute-start.33 = (bf16[16,1024]{1,0:T(8,128)(2,1)S(1)}, bf16[16,1024]{1,0:T(8,128)(2,1)S(1)}, u32[]{:S(2)}, u32[]{:S(2)}) collective-permute-start(bf16[16,1024]{1,0:T(8,128)(2,1)S(1)} %get-tuple-element.93), channel_id=1, source_target_pairs={{0,2},{1,3},{2,0},{3,1},{4,6},{5,7},{6,4},{7,5},{8,10},{9,11},{10,... | collective-permute-start | bytes 98312 | tf_op jit(solution)/shard_map/ppermute | solution.py:433
  104.4 5.7 %collective-permute-start.34 = (bf16[16,1024]{1,0:T(8,128)(2,1)S(1)}, bf16[16,1024]{1,0:T(8,128)(2,1)S(1)}, u32[]{:S(2)}, u32[]{:S(2)}) collective-permute-start(bf16[16,1024]{1,0:T(8,128)(2,1)S(1)} %get-tuple-element.94), channel_id=1, source_target_pairs={{0,3},{1,2},{2,1},{3,0},{4,7},{5,6},{6,5},{7,4},{8,11},{9,10},{10,... | collective-permute-start | bytes 98312 | tf_op jit(solution)/shard_map/ppermute | solution.py:433

commit v4 on v3

--- a/solution.py
+++ b/solution.py
@@ -20,7 +20,7 @@
     return values.astype(F32)
 
 
-def kernel_call(body, outs, args, far=0, scratch=(), limit=16, cost=None, pinned=0):
+def kernel_call(body, outs, args, far=0, scratch=(), limit=2, cost=None, far_outs=()):
     vmem = pl.BlockSpec(memory_space=pltpu.VMEM)
     hbm = pl.BlockSpec(memory_space=pltpu.HBM)
     near = len(args) - far
@@ -28,12 +28,9 @@
     args = (*args[:near], *stay)
     return pl.pallas_call(
         body,
-        out_shape=[
-            pltpu.VMEM(*out) if i < pinned else jax.ShapeDtypeStruct(*out)
-            for i, out in enumerate(outs)
-        ],
+        out_shape=[jax.ShapeDtypeStruct(*out) for out in outs],
         in_specs=[vmem] * near + [hbm] * far,
-        out_specs=[vmem] * len(outs),
+        out_specs=[hbm if i in far_outs else vmem for i in range(len(outs))],
         scratch_shapes=scratch,
         compiler_params=pltpu.CompilerParams(vmem_limit_bytes=limit * MIB),
         cost_estimate=cost,
@@ -52,10 +49,11 @@
         copy.wait()
 
 
-def fetch_rows_kernel(start, after, source, *refs):
-    *outs, token, sems = refs
+def fetch_rows_kernel(start, stores, after, *refs):
+    stored, (source, *outs), (token, sems) = refs[:stores], refs[stores:-2], refs[-2:]
+    stored_out, outs = outs[len(outs) - stores :], outs[: len(outs) - stores]
     size = outs[0].shape[0] // PIECES
-    pairs = []
+    pairs = list(zip(stored, stored_out))
     for i, out in enumerate(outs):
         for j in range(PIECES):
             first = start + (i * PIECES + j) * size
@@ -71,12 +69,15 @@
     finish(copies)
 
 
-def fetch_columns_kernel(block, first, second, first_out, second_out, block_out, sems):
-    size = first_out.shape[1]
-    copies = start_copies(
-        ((first.at[:, pl.ds(0, size)], first_out), (second.at[:, pl.ds(0, size)], second_out)),
-        sems,
-    )
+def fetch_columns_kernel(starts, block, first, second, *refs):
+    *outs, block_out, sems = refs
+    size = outs[0].shape[1] // 2
+    pairs = []
+    for start, out in zip(starts, outs, strict=True):
+        span = pl.ds(start, size)
+        pairs.append((first.at[:, span], out.at[:, pl.ds(0, size)]))
+        pairs.append((second.at[:, span], out.at[:, pl.ds(size, size)]))
+    copies = start_copies(pairs, sems)
     block_out[...] = block[...]
     finish(copies)
 
@@ -185,7 +186,7 @@
 def project_kernel(blocks, *refs):
     rows = refs[:blocks]
     gain, weight, cache, columns, select = refs[blocks : blocks + 5]
-    conved_out, gate_out, keep, send, normed, selected = refs[blocks + 5 :]
+    conved_out, normed, keep, send, selected = refs[blocks + 5 :]
     me = lax.axis_index("wide")
     count = rows[0].shape[0]
     for j in range(blocks):
@@ -203,8 +204,12 @@
     side = me & 1
     keep[...] = selected[pl.ds(pl.multiple_of(side * half, 16), half), :].astype(BF16)
     send[...] = selected[pl.ds(pl.multiple_of((1 - side) * half, 16), half), :].astype(BF16)
+
+
+def gate_kernel(weight, normed, out):
+    dims = (((1,), (1,)), ((), ()))
     z_gate = lax.dot_general(weight[1], normed[...], dims, preferred_element_type=F32)
-    gate_out[...] = sigmoid_times(z_gate)
+    out[...] = sigmoid_times(z_gate)
 
 
 def state_kernel(
@@ -286,47 +291,43 @@
     refs[-1][...] = total.astype(refs[-1].dtype)
 
 
-def residual_kernel(mine, got, hidden, weights, token, out):
+def residual_kernel(mine, got, hidden, weights, out):
     width = hidden.shape[1]
     residual = f32(hidden[...]) + (f32(mine[...]) + f32(got[...]))
     out[:, :width] = residual.astype(BF16)
     out[:, width:] = weights[...]
 
 
-def expert_kernel(blocks, steps, group, *refs):
-    rows = refs[:blocks]
-    gain, *downs = refs[blocks : blocks + 1 + steps]
-    gate_first, up_first, gate_proj, up_proj = refs[blocks + 1 + steps : blocks + 5 + steps]
-    keep, send, normed, share, total, gates, ups, sems = refs[blocks + 5 + steps :]
+def expert_kernel(blocks, steps, near_units, group, *refs):
+    rows, refs = refs[:blocks], refs[blocks:]
+    gain, downs, refs = refs[0], refs[1 : 1 + steps], refs[1 + steps :]
+    lead = len(near_units)
+    pairs_near, refs = dict(zip(near_units, refs[:lead])), refs[lead:]
+    gate_proj, up_proj, keep, send, normed, share, total, pairs, sems = refs
     count = rows[0].shape[0]
     width = gain.shape[1]
-    size = gates.shape[2]
-
-    def copies(i, slot):
-        span = pl.ds(i * size, size)
-        return (
-            pltpu.make_async_copy(gate_proj.at[:, span], gates.at[slot], sems.at[slot, 0]),
-            pltpu.make_async_copy(up_proj.at[:, span], ups.at[slot], sems.at[slot, 1]),
-        )
-
-    def begin(i, slot):
-        for copy in copies(i, slot):
-            copy.start()
-
-    near = gate_first.shape[1]
-    rest = size - near
-    ahead = []
-    if rest:
-        span = pl.ds(near, rest)
-        ahead = start_copies(
-            (
-                (gate_proj.at[:, span], gates.at[0, :, pl.ds(0, rest)]),
-                (up_proj.at[:, span], ups.at[0, :, pl.ds(0, rest)]),
-            ),
-            sems.at[0],
-        )
-    for i in range(1, min(2 if rest else 3, steps)):
-        begin(i, i % 2)
+    size = pairs.shape[2] // 2
+    units = gate_proj.shape[1] // size
+
+    far_units = [i for i in range(units) if i not in near_units]
+
+    def copies(n):
+        slot = n % pairs.shape[0]
+        span = pl.ds(far_units[n] * size, size)
+        return [
+            pltpu.make_async_copy(
+                source.at[:, span], pairs.at[slot, :, pl.ds(which * size, size)], sems.at[slot, which]
+            )
+            for which, source in enumerate((gate_proj, up_proj))
+        ]
+
+    def begin(n):
+        if n < len(far_units):
+            for copy in copies(n):
+                copy.start()
+
+    for n in range(pairs.shape[0]):
+        begin(n)
     expert = lax.axis_index("wide") // group
     lane = lax.broadcasted_iota(jnp.int32, (count, LANES), 1)
     wanted = (lane == expert) | (lane == expert + LANES // 2)
@@ -336,27 +337,26 @@
         shares = jnp.where(wanted, f32(rows[j][:, width:]), 0.0)
         share[span, :] = jnp.broadcast_to(jnp.sum(shares, axis=1, keepdims=True), (count, LANES))
 
-    def inner_of(gate_block, up_block):
-        inputs = normed[...]
-        gate_act = jnp.dot(inputs, gate_block, preferred_element_type=F32)
-        up_act = jnp.dot(inputs, up_block, preferred_element_type=F32)
-        return (sigmoid_times(gate_act) * up_act).astype(BF16)
-
-    inner = inner_of(gate_first[...], up_first[...])
-    if rest:
-        finish(ahead)
-        more = inner_of(gates[0, :, :rest], ups[0, :, :rest])
-        if steps > 2:
-            begin(2, 0)
-        inner = jnp.concatenate([inner, more], axis=1)
-    total[...] = jnp.dot(inner, downs[0][...], preferred_element_type=F32)
-    for i in range(1, steps):
-        slot = i % 2
-        finish(copies(i, slot))
-        inner = inner_of(gates[slot], ups[slot])
-        if i + 2 < steps:
-            begin(i + 2, slot)
-        total[...] += jnp.dot(inner, downs[i][...], preferred_element_type=F32)
+    def inner_of(pair):
+        both = jnp.dot(normed[...], pair, preferred_element_type=F32)
+        return (sigmoid_times(both[:, :size]) * both[:, size:]).astype(BF16)
+
+    for step, down in enumerate(downs):
+        inner = []
+        for i in range(step * units // steps, (step + 1) * units // steps):
+            if i in pairs_near:
+                inner.append(inner_of(pairs_near[i][...]))
+            else:
+                n = far_units.index(i)
+                finish(copies(n))
+                inner.append(inner_of(pairs[n % pairs.shape[0]]))
+                begin(n + pairs.shape[0])
+        inner = jnp.concatenate(inner, axis=1)
+        added = jnp.dot(inner, down[...], preferred_element_type=F32)
+        if step:
+            total[...] += added
+        else:
+            total[...] = added
     weighted = (total[...] * share[:, :1]).astype(BF16)
     kept = keep.shape[0]
     keep[...] = weighted[:kept]
@@ -432,29 +432,37 @@
     def to_narrow(values, k):
         return lax.ppermute(values, "narrow", [(i, i ^ k) for i in range(narrow_count)])
 
-    def fetch_rows(start, number, after):
-        *blocks, token = kernel_call(
-            functools.partial(fetch_rows_kernel, start * block),
-            [((block, width), BF16)] * number + [((8, LANES), F32)],
-            (after, down_proj),
-                far=1,
-            scratch=[pltpu.SemaphoreType.DMA((number * PIECES,))],
+    def fetch_rows(start, number, after, *stored):
+        outs = [((block, width), BF16)] * number
+        outs += [(item.shape, item.dtype) for item in stored]
+        *got, token = kernel_call(
+            functools.partial(fetch_rows_kernel, start * block, len(stored)),
+            [*outs, ((8, LANES), F32)],
+            (after, *stored, down_proj),
+            far=1,
+            scratch=[pltpu.SemaphoreType.DMA((number * PIECES + len(stored),))],
             cost=pl.CostEstimate(
                 flops=0, bytes_accessed=4 * number * block * width, transcendentals=0
             ),
+            far_outs=range(number, number + len(stored)),
         )
-        return blocks, token
-
-    def fetch_columns(size, after):
-        return kernel_call(
-            fetch_columns_kernel,
-            [((width, size), BF16), ((width, size), BF16), (after.shape, BF16)],
+        return got[:number], token, got[number:]
+
+    def fetch_columns(chosen_units, after):
+        if not chosen_units:
+            return [], after
+        number = len(chosen_units)
+        *got, again = kernel_call(
+            functools.partial(fetch_columns_kernel, [i * unit for i in chosen_units]),
+            [((width, 2 * unit), BF16)] * number + [(after.shape, BF16)],
             (after, gate_proj, up_proj),
-                far=2,
-            scratch=[pltpu.SemaphoreType.DMA((2,))],
-            cost=pl.CostEstimate(flops=0, bytes_accessed=8 * size * width, transcendentals=0),
-            pinned=2,
+            far=2,
+            scratch=[pltpu.SemaphoreType.DMA((2 * number,))],
+            cost=pl.CostEstimate(
+                flops=0, bytes_accessed=8 * number * unit * width, transcendentals=0
+            ),
         )
+        return got, again
 
     def plane_gather(block, near):
         same = [near, *[to_chip(block, k) for k in range(1, chips)]]
@@ -475,7 +483,11 @@
     block = next(size for size in (512, 256, 128, hidden_units) if hidden_units % size == 0)
     steps = hidden_units // block
     third = max(1, steps // 3)
-    near = block // 2 if block % (2 * LANES) == 0 else block
+    unit = block // 2 if block % (2 * LANES) == 0 else block
+    units = hidden_units // unit
+    lead = units // 6
+    near_units = tuple(i * units // lead for i in range(lead))
+    lead_first = 2 * lead // 3
     rank = step_weight.shape[1]
     topk = route_experts.shape[1]
     padded = max(LANES, channels, rank)
@@ -533,6 +545,7 @@
             pltpu.VMEM((LANES, padded), F32),
             pltpu.SemaphoreType.DMA((14,)),
         ],
+        limit=16,
         cost=pl.CostEstimate(
             flops=0,
             bytes_accessed=4 * in_weight.size,
@@ -543,11 +556,11 @@
     same, other = plane_gather(hidden, hidden_near)
     interleaved = [item for pair in zip(same, other) for item in pair]
     half = chosen // 2
-    conved, gate, keep, send = kernel_call(
+    conved, normed, keep, send = kernel_call(
         functools.partial(project_kernel, wide_count),
         [
             ((channels, rows), F32),
-            ((channels, rows), F32),
+            ((rows, width), BF16),
             ((half, rows), BF16),
             ((half, rows), BF16),
         ],
@@ -559,12 +572,21 @@
             columns,
             select_near,
         ),
-        scratch=[
-            pltpu.VMEM((rows, width), BF16),
-            pltpu.VMEM((chosen, rows), F32),
-        ],
+        scratch=[pltpu.VMEM((chosen, rows), F32)],
+        limit=16,
     )
     part = add(keep, swap(send))
+    (gate,) = kernel_call(
+        gate_kernel,
+        [((channels, rows), F32)],
+        (in_weight_near, normed),
+        limit=8,
+        cost=pl.CostEstimate(
+            flops=2 * channels * width * rows,
+            bytes_accessed=2 * in_weight.size,
+            transcendentals=channels * rows,
+        ),
+    )
     out_weight_near, step_weight_near, states_near, token = kernel_call(
         fetch_kernel,
         [
@@ -581,8 +603,9 @@
         ),
     )
     part = add(part, *[to_chip(part, k) for k in range(1, chips)], token=token)
-    part = add(part, *[to_narrow(part, k) for k in range(1, narrow_count)])
-    new_state, keep, send = kernel_call(
+    down_first, token, _ = fetch_rows(0, third, part)
+    part = add(part, *[to_narrow(part, k) for k in range(1, narrow_count)], token=token)
+    new_state_near, keep, send = kernel_call(
         functools.partial(state_kernel, wide_count),
         [
             (ssm_cache.shape, BF16),
@@ -608,25 +631,26 @@
             pltpu.VMEM((channels, rows), F32),
             pltpu.VMEM((rows, channels), F32),
         ],
+        limit=16,
     )
     parts = plane_scatter(keep, swap(send))
-    down_first, token = fetch_rows(0, third, parts[0])
+    down_second, token, (new_state,) = fetch_rows(third, third, parts[0], new_state_near)
     mine = add(parts[0], *to_chips(parts), token=token)
-    down_second, token = fetch_rows(third, third, mine)
+    down_third, token, _ = fetch_rows(2 * third, steps - 2 * third, mine)
     step = 1
     while 2 * step < narrow_count:
         mine = add(mine, to_narrow(mine, step), token=token)
         step *= 2
-    down_third, token = fetch_rows(2 * third, steps - 2 * third, mine)
+    pairs_first, again = fetch_columns(near_units[:lead_first], mine)
     (residual,) = kernel_call(
         residual_kernel,
         [((count, width + LANES), BF16)],
-        (mine, to_narrow(mine, step), hidden_near, weights, token),
-    )
-    gate_first, up_first, residual_near = fetch_columns(near, residual)
-    same, other = plane_gather(residual, residual_near)
+        (again, to_narrow(mine, step), hidden_near, weights),
+    )
+    pairs_second, again = fetch_columns(near_units[lead_first:], residual)
+    same, other = plane_gather(residual, again)
     keep, send = kernel_call(
-        functools.partial(expert_kernel, wide_count, steps, wide_count // EXPERTS),
+        functools.partial(expert_kernel, wide_count, steps, near_units, wide_count // EXPERTS),
         [((rows // 2, width), BF16)] * 2,
         (
             *same,
@@ -635,8 +659,8 @@
             *down_first,
             *down_second,
             *down_third,
-            gate_first,
-            up_first,
+            *pairs_first,
+            *pairs_second,
             gate_proj,
             up_proj,
         ),
@@ -645,11 +669,10 @@
             pltpu.VMEM((rows, width), BF16),
             pltpu.VMEM((rows, LANES), F32),
             pltpu.VMEM((rows, width), F32),
-            pltpu.VMEM((2, width, block), BF16),
-            pltpu.VMEM((2, width, block), BF16),
-            pltpu.SemaphoreType.DMA((2, 2)),
+            pltpu.VMEM((3, width, 2 * unit), BF16),
+            pltpu.SemaphoreType.DMA((3, 2)),
         ],
-        limit=22,
+        limit=18 if rows <= 256 else 24,
     )
     parts = plane_scatter(keep, swap(send))
     parts = [parts[0], *to_chips(parts)]

time: 111 us -> 107 us (0.964)
  waiting for transfers between devices: 36.7 us -> 32.1 us
    ppermute x8, waiting for transfers between devices: 12.8 us -> 8.84 us  [to_narrow(): lax.ppermute(values, 'narrow', [(i, i ^ k) for i in range(narrow_count)])]
    pallas_call x19 -> x21, Pallas kernels: 41.9 us -> 41.6 us  [kernel_call(): pl.pallas_call(body, out_shape=[jax.ShapeDtypeStruct(*out) for out in out...]
  transfers between devices with their start and end apart: 35 -> 35, of which waited for: 23 -> 22; matrix products, arithmetic and copies ran while one was open for 0% -> 0% of each run, Pallas kernels for 16% -> 19%
where the time goes in v4:
time: 107 us
  Pallas kernels  41.6 us (39%)
  waiting for transfers between devices  32.1 us (30%)
  starting transfers between devices  32 us (30%)
    pallas_call x21, Pallas kernels, kernel_call(): pl.pallas_call(body, out_shape=[jax.ShapeDtypeStruct(*out) for out in out...  41.6 us
    ppermute x15, starting transfers between devices, to_chip(): lax.ppermute(values, 'wide', [(i, i ^ 2 * k) for i in range(wide_count)])  18.8 us
    ppermute x15, waiting for transfers between devices, to_chip(): lax.ppermute(values, 'wide', [(i, i ^ 2 * k) for i in range(wide_count)])  15.5 us
    ppermute x8, starting transfers between devices, to_narrow(): lax.ppermute(values, 'narrow', [(i, i ^ k) for i in range(narrow_count)])  11.9 us
    ppermute x8, waiting for transfers between devices, to_narrow(): lax.ppermute(values, 'narrow', [(i, i ^ k) for i in range(narrow_count)])  8.84 us
    ppermute x12, waiting for transfers between devices, swap(): return lax.ppermute(values, 'wide', [(i, i ^ 1) for i in range(wide_count)])  7.73 us
  transfers between devices with their start and end apart: 35, of which 22 were waited for; matrix products, arithmetic and copies ran while one was open for 0% of the time, Pallas kernels for 19%

profile of v4, /device:TPU:0, one launch (start us, length us, event | category | flops | bytes accessed | tf_op | source)
XLA Modules:
  0.0 106.6 jit_solution(12735782941940149886)
XLA Ops:
  0.6 3.0 %collective-permute-start.1 = (bf16[16,4096]{1,0:T(8,128)(2,1)}, bf16[16,4096]{1,0:T(8,128)(2,1)S(1)}, u32[]{:S(2)}, u32[]{:S(2)}) collective-permute-start(bf16[16,4096]{1,0:T(8,128)(2,1)} %hidden.1), channel_id=1, source_target_pairs={{0,8},{4,12},{8,0},{12,4},{16,24},{20,28},{24,16},{28,20},{1,9},{5... | collective-permute-start | bytes 393224 | tf_op jit(solution)/shard_map/ppermute | solution.py:430
  3.6 1.5 %collective-permute-start.5 = (bf16[16,4096]{1,0:T(8,128)(2,1)}, bf16[16,4096]{1,0:T(8,128)(2,1)S(1)}, u32[]{:S(2)}, u32[]{:S(2)}) collective-permute-start(bf16[16,4096]{1,0:T(8,128)(2,1)} %hidden.1), channel_id=1, source_target_pairs={{0,24},{4,28},{8,16},{12,20},{16,8},{20,12},{24,0},{28,4},{1,25},{... | collective-permute-start | bytes 393224 | tf_op jit(solution)/shard_map/ppermute | solution.py:430
  5.2 2.5 %shard_map.203 = (bf16[2,256,4096]{2,1,0:T(8,128)(2,1)S(1)}, bf16[3,256,128]{2,1,0:T(8,128)(2,1)S(1)}, bf16[288,256]{1,0:T(8,128)(2,1)S(1)}, bf16[16,4096]{1,0:T...) custom-call(bf16[2,256,4096]{2,1,0:T(8,128)(2,1)} %in_weight.1, ...), custom_call_target="tpu_custom_call" | custom-call | bytes 8388608 | tf_op jit(solution)/shard_map/pallas_call | solution.py:29
  8.3 3.2 %collective-permute-done.5.refs_6_ = bf16[16,4096]{1,0:T(8,128)(2,1)S(1)} collective-permute-done((bf16[16,4096]{1,0:T(8,128)(2,1)}, bf16[16,4096]{1,0:T(8,128)(2,1)S(1)}, u32[]{:S(2)}, u32[]{:S(2)}) %collective-permute-start.5) | collective-permute-done | bytes 131104 | tf_op jit(solution)/shard_map/ppermute | solution.py:430
  11.5 1.4 %collective-permute-done.3.refs_4_ = bf16[16,4096]{1,0:T(8,128)(2,1)S(1)} collective-permute-done((bf16[16,4096]{1,0:T(8,128)(2,1)}, bf16[16,4096]{1,0:T(8,128)(2,1)S(1)}, u32[]{:S(2)}, u32[]{:S(2)}) %collective-permute-start.3) | collective-permute-done | bytes 131104 | tf_op jit(solution)/shard_map/ppermute | solution.py:430
  12.8 1.3 %collective-permute-done.4.refs_5_ = bf16[16,4096]{1,0:T(8,128)(2,1)S(1)} collective-permute-done((bf16[16,4096]{1,0:T(8,128)(2,1)S(1)}, bf16[16,4096]{1,0:T(8,128)(2,1)S(1)}, u32[]{:S(2)}, u32[]{:S(2)}) %collective-permute-start.4) | collective-permute-done | bytes 131104 | tf_op jit(solution)/shard_map/ppermute | solution.py:427
  14.2 1.5 %shard_map.204 = (f32[256,128]{1,0:T(8,128)S(1)}, bf16[128,4096]{1,0:T(8,128)(2,1)S(1)}, bf16[144,128]{1,0:T(8,128)(2,1)S(1)}, bf16[144,128]{1,0:T(8,128)(2,1)S(1)}) custom-call(bf16[16,4096]{1,0:T(8,128)(2,1)S(1)} %get-tuple-element.51.refs_0_.hidden, bf16[16,4096]{1,0:T(8,128)(2,1)S(1)} %collective-permute-done.refs_1_, ...), custom_call_target="tpu_custom_call" | custom-call | tf_op jit(solution)/shard_map/pallas_call | solution.py:29
  15.9 1.1 collective-permute-done.7.refs_1_
  17.0 1.5 %collective-permute-start.10 = (bf16[144,128]{1,0:T(8,128)(2,1)S(1)}, bf16[144,128]{1,0:T(8,128)(2,1)S(1)}, u32[]{:S(2)}, u32[]{:S(2)}) collective-permute-start(bf16[144,128]{1,0:T(8,128)(2,1)S(1)} %shard_map.205.after.refs_0_), channel_id=1, source_target_pairs={{0,24},{4,28},{8,16},{12,20},{16,8},{20,12},{24,0},{28,4},{1,25},{... | collective-permute-start | bytes 110600 | tf_op jit(solution)/shard_map/ppermute | solution.py:430
  18.5 1.5 %collective-permute-start.9 = (bf16[144,128]{1,0:T(8,128)(2,1)S(1)}, bf16[144,128]{1,0:T(8,128)(2,1)S(1)}, u32[]{:S(2)}, u32[]{:S(2)}) collective-permute-start(bf16[144,128]{1,0:T(8,128)(2,1)S(1)} %shard_map.205.after.refs_0_), channel_id=1, source_target_pairs={{0,16},{4,20},{8,24},{12,28},{16,0},{20,4},{24,8},{28,12},{1,17},{... | collective-permute-start | bytes 110600 | tf_op jit(solution)/shard_map/ppermute | solution.py:430
  20.6 1.9 %shard_map.206 = (bf16[256,4096]{1,0:T(8,128)(2,1)S(1)}, bf16[256,256]{1,0:T(8,128)(2,1)S(1)}, bf16[256,16,128]{2,1,0:T(8,128)(2,1)S(1)}, f32[8,128]{1,0:T(8,128)S(1)}) custom-call(bf16[144,128]{1,0:T(8,128)(2,1)S(1)} %shard_map.205.after.refs_0_, bf16[256,4096]{1,0:T(8,128)(2,1)} %first.3, bf16[256,256]{1,0:T(8,128)(2,1)} %second.3, bf16[256,16,128]{2,1,0:T(8,128)(2,1)} %third.1), custom_call_target="tpu_custom_call" | custom-call | bytes 6291456 | tf_op jit(solution)/shard_map/pallas_call | solution.py:29
  22.5 1.5 %collective-permute-done.8.refs_1_ = bf16[144,128]{1,0:T(8,128)(2,1)S(1)} collective-permute-done((bf16[144,128]{1,0:T(8,128)(2,1)S(1)}, bf16[144,128]{1,0:T(8,128)(2,1)S(1)}, u32[]{:S(2)}, u32[]{:S(2)}) %collective-permute-start.8) | collective-permute-done | bytes 36896 | tf_op jit(solution)/shard_map/ppermute | solution.py:430
  24.0 3.7 %collective-permute-start.13 = (bf16[144,128]{1,0:T(8,128)(2,1)S(1)}, bf16[144,128]{1,0:T(8,128)(2,1)S(1)}, u32[]{:S(2)}, u32[]{:S(2)}) collective-permute-start(bf16[144,128]{1,0:T(8,128)(2,1)S(1)} %shard_map.207.after.refs_0_), channel_id=1, source_target_pairs={{0,3},{1,2},{2,1},{3,0},{4,7},{5,6},{6,5},{7,4},{8,11},{9,10},{10,... | collective-permute-start | bytes 110600 | tf_op jit(solution)/shard_map/ppermute | solution.py:433
  27.7 0.8 collective-permute-start.11
  28.5 3.5 %shard_map.208 = (bf16[512,4096]{1,0:T(8,128)(2,1)S(1)}, bf16[512,4096]{1,0:T(8,128)(2,1)S(1)}, f32[8,128]{1,0:T(8,128)S(1)}) custom-call(bf16[144,128]{1,0:T(8,128)(2,1)S(1)} %shard_map.207.after.refs_0_, bf16[3072,4096]{1,0:T(8,128)(2,1)} %refs_0_.3), custom_call_target="tpu_custom_call" | custom-call | bytes 16777216 | tf_op jit(solution)/shard_map/pallas_call | solution.py:29
  32.6 0.7 shard_map.210.gate
  33.8 2.4 %shard_map.211 = (bf16[256,16,128]{2,1,0:T(8,128)(2,1)S(1)}, bf16[64,4096]{1,0:T(8,128)(2,1)S(1)}, bf16[64,4096]{1,0:T(8,128)(2,1)S(1)}) custom-call(bf16[144,128]{1,0:T(8,128)(2,1)S(1)} %shard_map.209.own_half, bf16[144,128]{1,0:T(8,128)(2,1)S(1)} %collective-permute-done.14.other_half, f32[256,128]{1,0:T(8,128)S(1)} %get-tuple-element.61.step_gain, ...), custom_call_target="tpu_custom_call" | custom-call | tf_op jit(solution)/shard_map/pallas_call | solution.py:29
  36.5 1.7 %collective-permute-done.15.got = bf16[64,4096]{1,0:T(8,128)(2,1)S(1)} collective-permute-done((bf16[64,4096]{1,0:T(8,128)(2,1)S(1)}, bf16[64,4096]{1,0:T(8,128)(2,1)S(1)}, u32[]{:S(2)}, u32[]{:S(2)}) %collective-permute-start.15) | collective-permute-done | bytes 524320 | tf_op jit(solution)/shard_map/ppermute | solution.py:427
  38.4 0.6 collective-permute-start.16
  39.5 2.5 %collective-permute-start.18 = (bf16[16,4096]{1,0:T(8,128)(2,1)S(1)}, bf16[16,4096]{1,0:T(8,128)(2,1)S(1)}, u32[]{:S(2)}, u32[]{:S(2)}) collective-permute-start(bf16[16,4096]{1,0:T(8,128)(2,1)S(1)} %get-tuple-element.73), channel_id=1, source_target_pairs={{0,24},{4,28},{8,16},{12,20},{16,8},{20,12},{24,0},{28,4},{1,25},{... | collective-permute-start | bytes 393224 | tf_op jit(solution)/shard_map/ppermute | solution.py:430
  41.9 3.9 %shard_map.213 = (bf16[512,4096]{1,0:T(8,128)(2,1)S(1)}, bf16[512,4096]{1,0:T(8,128)(2,1)S(1)}, bf16[256,16,128]{2,1,0:T(8,128)(2,1)}, f32[8,128]{1,0:T(8,128)S(1)}) custom-call(bf16[16,4096]{1,0:T(8,128)(2,1)S(1)} %get-tuple-element.70.after.refs_0_, bf16[256,16,128]{2,1,0:T(8,128)(2,1)S(1)} %get-tuple-element.74.refs_0_, bf16[3072,4096]{1,0:T(8,128)(2,1)} %refs_0_.3), custom_call_target="tpu_custom_call" | custom-call | bytes 16777216 | tf_op jit(solution)/shard_map/pallas_call | solution.py:29
  45.8 1.2 %collective-permute-done.17.refs_2_ = bf16[16,4096]{1,0:T(8,128)(2,1)S(1)} collective-permute-done((bf16[16,4096]{1,0:T(8,128)(2,1)S(1)}, bf16[16,4096]{1,0:T(8,128)(2,1)S(1)}, u32[]{:S(2)}, u32[]{:S(2)}) %collective-permute-start.17) | collective-permute-done | bytes 131104 | tf_op jit(solution)/shard_map/ppermute | solution.py:430
  47.2 0.8 collective-permute-start.19
  47.9 3.5 %shard_map.215 = (bf16[512,4096]{1,0:T(8,128)(2,1)S(1)}, bf16[512,4096]{1,0:T(8,128)(2,1)S(1)}, f32[8,128]{1,0:T(8,128)S(1)}) custom-call(bf16[16,4096]{1,0:T(8,128)(2,1)S(1)} %shard_map.214.after.refs_0_, bf16[3072,4096]{1,0:T(8,128)(2,1)} %refs_0_.3), custom_call_target="tpu_custom_call" | custom-call | bytes 16777216 | tf_op jit(solution)/shard_map/pallas_call | solution.py:29
  51.4 0.7 collective-permute-done.19.refs_1_
  52.2 2.3 %collective-permute-start.20 = (bf16[16,4096]{1,0:T(8,128)(2,1)S(1)}, bf16[16,4096]{1,0:T(8,128)(2,1)S(1)}, u32[]{:S(2)}, u32[]{:S(2)}) collective-permute-start(bf16[16,4096]{1,0:T(8,128)(2,1)S(1)} %shard_map.216.block), channel_id=1, source_target_pairs={{0,2},{1,3},{2,0},{3,1},{4,6},{5,7},{6,4},{7,5},{8,10},{9,11},{10,... | collective-permute-start | bytes 393224 | tf_op jit(solution)/shard_map/ppermute | solution.py:433
  54.5 2.3 %shard_map.217 = (bf16[4096,512]{1,0:T(8,128)(2,1)S(1)}, bf16[16,4096]{1,0:T(8,128)(2,1)S(1)}) custom-call(bf16[16,4096]{1,0:T(8,128)(2,1)S(1)} %shard_map.216.block, bf16[4096,3072]{1,0:T(8,128)(2,1)} %refs_17_.1, bf16[4096,3072]{1,0:T(8,128)(2,1)} %refs_18_.1), custom_call_target="tpu_custom_call" | custom-call | bytes 8388608 | tf_op jit(solution)/shard_map/pallas_call | solution.py:29
  56.7 3.0 %collective-permute-done.20.got = bf16[16,4096]{1,0:T(8,128)(2,1)S(1)} collective-permute-done((bf16[16,4096]{1,0:T(8,128)(2,1)S(1)}, bf16[16,4096]{1,0:T(8,128)(2,1)S(1)}, u32[]{:S(2)}, u32[]{:S(2)}) %collective-permute-start.20) | collective-permute-done | bytes 131104 | tf_op jit(solution)/shard_map/ppermute | solution.py:433
  59.8 1.3 %collective-permute-start.23 = (bf16[16,4224]{1,0:T(8,128)(2,1)S(1)}, bf16[16,4224]{1,0:T(8,128)(2,1)S(1)}, u32[]{:S(2)}, u32[]{:S(2)}) collective-permute-start(bf16[16,4224]{1,0:T(8,128)(2,1)S(1)} %shard_map.218.block.residual), channel_id=1, source_target_pairs={{0,24},{4,28},{8,16},{12,20},{16,8},{20,12},{24,0},{28,4},{1,25},{... | collective-permute-start | bytes 405512 | tf_op jit(solution)/shard_map/ppermute | solution.py:430
  61.1 1.6 %collective-permute-start.22 = (bf16[16,4224]{1,0:T(8,128)(2,1)S(1)}, bf16[16,4224]{1,0:T(8,128)(2,1)S(1)}, u32[]{:S(2)}, u32[]{:S(2)}) collective-permute-start(bf16[16,4224]{1,0:T(8,128)(2,1)S(1)} %shard_map.218.block.residual), channel_id=1, source_target_pairs={{0,16},{4,20},{8,24},{12,28},{16,0},{20,4},{24,8},{28,12},{1,17},{... | collective-permute-start | bytes 405512 | tf_op jit(solution)/shard_map/ppermute | solution.py:430
  62.8 0.6 collective-permute-start.21
  63.3 2.3 %shard_map.219 = (bf16[4096,512]{1,0:T(8,128)(2,1)S(1)}, bf16[16,4224]{1,0:T(8,128)(2,1)S(1)}) custom-call(bf16[16,4224]{1,0:T(8,128)(2,1)S(1)} %shard_map.218.block.residual, bf16[4096,3072]{1,0:T(8,128)(2,1)} %refs_17_.1, bf16[4096,3072]{1,0:T(8,128)(2,1)} %refs_18_.1), custom_call_target="tpu_custom_call" | custom-call | bytes 8388608 | tf_op jit(solution)/shard_map/pallas_call | solution.py:29
  65.7 1.0 collective-permute-done.23.refs_3_
  66.7 0.8 collective-permute-done.22.refs_2_
  67.4 0.9 collective-permute-done.21.refs_1_
  68.8 0.9 collective-permute-done.25.refs_5_
  69.6 15.9 %shard_map.220 = (bf16[64,4096]{1,0:T(8,128)(2,1)S(1)}, bf16[64,4096]{1,0:T(8,128)(2,1)S(1)}) custom-call(bf16[16,4224]{1,0:T(8,128)(2,1)S(1)} %get-tuple-element.79.refs_0_, bf16[16,4224]{1,0:T(8,128)(2,1)S(1)} %collective-permute-done.21.refs_1_, bf16[16,4224]{1,0:T(8,128)(2,1)S(1)} %collective-permute-done.22.refs_2_, ...), custom_call_target="tpu_custom_call" | custom-call | tf_op jit(solution)/shard_map/pallas_call | solution.py:29
  85.8 1.8 %collective-permute-done.28.got = bf16[64,4096]{1,0:T(8,128)(2,1)S(1)} collective-permute-done((bf16[64,4096]{1,0:T(8,128)(2,1)S(1)}, bf16[64,4096]{1,0:T(8,128)(2,1)S(1)}, u32[]{:S(2)}, u32[]{:S(2)}) %collective-permute-start.28) | collective-permute-done | bytes 524320 | tf_op jit(solution)/shard_map/ppermute | solution.py:427
  87.7 0.9 collective-permute-start.29
  88.6 1.2 %collective-permute-start.30 = (bf16[16,4096]{1,0:T(8,128)(2,1)S(1)}, bf16[16,4096]{1,0:T(8,128)(2,1)S(1)}, u32[]{:S(2)}, u32[]{:S(2)}) collective-permute-start(bf16[16,4096]{1,0:T(8,128)(2,1)S(1)} %get-tuple-element.93), channel_id=1, source_target_pairs={{0,16},{4,20},{8,24},{12,28},{16,0},{20,4},{24,8},{28,12},{1,17},{... | collective-permute-start | bytes 393224 | tf_op jit(solution)/shard_map/ppermute | solution.py:430
  89.7 1.5 %collective-permute-start.31 = (bf16[16,4096]{1,0:T(8,128)(2,1)S(1)}, bf16[16,4096]{1,0:T(8,128)(2,1)S(1)}, u32[]{:S(2)}, u32[]{:S(2)}) collective-permute-start(bf16[16,4096]{1,0:T(8,128)(2,1)S(1)} %get-tuple-element.94), channel_id=1, source_target_pairs={{0,24},{4,28},{8,16},{12,20},{16,8},{20,12},{24,0},{28,4},{1,25},{... | collective-permute-start | bytes 393224 | tf_op jit(solution)/shard_map/ppermute | solution.py:430
  91.2 2.9 %collective-permute-done.29.refs_1_ = bf16[16,4096]{1,0:T(8,128)(2,1)S(1)} collective-permute-done((bf16[16,4096]{1,0:T(8,128)(2,1)S(1)}, bf16[16,4096]{1,0:T(8,128)(2,1)S(1)}, u32[]{:S(2)}, u32[]{:S(2)}) %collective-permute-start.29) | collective-permute-done | bytes 131104 | tf_op jit(solution)/shard_map/ppermute | solution.py:430
  94.1 2.7 %collective-permute-done.30.refs_2_ = bf16[16,4096]{1,0:T(8,128)(2,1)S(1)} collective-permute-done((bf16[16,4096]{1,0:T(8,128)(2,1)S(1)}, bf16[16,4096]{1,0:T(8,128)(2,1)S(1)}, u32[]{:S(2)}, u32[]{:S(2)}) %collective-permute-start.30) | collective-permute-done | bytes 131104 | tf_op jit(solution)/shard_map/ppermute | solution.py:430
  97.0 3.2 %collective-permute-start.33 = (bf16[16,1024]{1,0:T(8,128)(2,1)S(1)}, bf16[16,1024]{1,0:T(8,128)(2,1)S(1)}, u32[]{:S(2)}, u32[]{:S(2)}) collective-permute-start(bf16[16,1024]{1,0:T(8,128)(2,1)S(1)} %get-tuple-element.97), channel_id=1, source_target_pairs={{0,2},{1,3},{2,0},{3,1},{4,6},{5,7},{6,4},{7,5},{8,10},{9,11},{10,... | collective-permute-start | bytes 98312 | tf_op jit(solution)/shard_map/ppermute | solution.py:433
  100.2 1.2 %collective-permute-start.34 = (bf16[16,1024]{1,0:T(8,128)(2,1)S(1)}, bf16[16,1024]{1,0:T(8,128)(2,1)S(1)}, u32[]{:S(2)}, u32[]{:S(2)}) collective-permute-start(bf16[16,1024]{1,0:T(8,128)(2,1)S(1)} %get-tuple-element.98), channel_id=1, source_target_pairs={{0,3},{1,2},{2,1},{3,0},{4,7},{5,6},{6,5},{7,4},{8,11},{9,10},{10,... | collective-permute-start | bytes 98312 | tf_op jit(solution)/shard_map/ppermute | solution.py:433
  101.4 0.7 collective-permute-done.33.refs_2_
  102.1 3.8 %collective-permute-done.34.refs_3_ = bf16[16,1024]{1,0:T(8,128)(2,1)S(1)} collective-permute-done((bf16[16,1024]{1,0:T(8,128)(2,1)S(1)}, bf16[16,1024]{1,0:T(8,128)(2,1)S(1)}, u32[]{:S(2)}, u32[]{:S(2)}) %collective-permute-start.34) | collective-permute-done | bytes 32800 | tf_op jit(solution)/shard_map/ppermute | solution.py:433
  105.9 0.6 shard_map.223
  (43 shorter events, 4.6 us)
Async XLA Ops:
  0.6 7.2 %collective-permute-start.1 = (bf16[16,4096]{1,0:T(8,128)(2,1)}, bf16[16,4096]{1,0:T(8,128)(2,1)S(1)}, u32[]{:S(2)}, u32[]{:S(2)}) collective-permute-start(bf16[16,4096]{1,0:T(8,128)(2,1)} %hidden.1), channel_id=1, source_target_pairs={{0,8},{4,12},{8,0},{12,4},{16,24},{20,28},{24,16},{28,20},{1,9},{5... | collective-permute-start | bytes 393224 | tf_op jit(solution)/shard_map/ppermute | solution.py:430
  3.6 7.8 %collective-permute-start.5 = (bf16[16,4096]{1,0:T(8,128)(2,1)}, bf16[16,4096]{1,0:T(8,128)(2,1)S(1)}, u32[]{:S(2)}, u32[]{:S(2)}) collective-permute-start(bf16[16,4096]{1,0:T(8,128)(2,1)} %hidden.1), channel_id=1, source_target_pairs={{0,24},{4,28},{8,16},{12,20},{16,8},{20,12},{24,0},{28,4},{1,25},{... | collective-permute-start | bytes 393224 | tf_op jit(solution)/shard_map/ppermute | solution.py:430
  5.1 7.7 %collective-permute-start.3 = (bf16[16,4096]{1,0:T(8,128)(2,1)}, bf16[16,4096]{1,0:T(8,128)(2,1)S(1)}, u32[]{:S(2)}, u32[]{:S(2)}) collective-permute-start(bf16[16,4096]{1,0:T(8,128)(2,1)} %hidden.1), channel_id=1, source_target_pairs={{0,16},{4,20},{8,24},{12,28},{16,0},{20,4},{24,8},{28,12},{1,17},{... | collective-permute-start | bytes 393224 | tf_op jit(solution)/shard_map/ppermute | solution.py:430
  7.7 5.1 %collective-permute-start = (bf16[16,4096]{1,0:T(8,128)(2,1)S(1)}, bf16[16,4096]{1,0:T(8,128)(2,1)S(1)}, u32[]{:S(2)}, u32[]{:S(2)}) collective-permute-start(bf16[16,4096]{1,0:T(8,128)(2,1)S(1)} %get-tuple-element.51.refs_0_.hidden), channel_id=1, source_target_pairs={{0,4},{4,0},{8,12},{12,8},{16,20},{20,16},{24,28},{28,24},{1,5},{5... | collective-permute-start | bytes 393224 | tf_op jit(solution)/shard_map/ppermute | solution.py:427
  7.9 5.0 %collective-permute-start.2 = (bf16[16,4096]{1,0:T(8,128)(2,1)S(1)}, bf16[16,4096]{1,0:T(8,128)(2,1)S(1)}, u32[]{:S(2)}, u32[]{:S(2)}) collective-permute-start(bf16[16,4096]{1,0:T(8,128)(2,1)S(1)} %collective-permute-done.1.refs_2_), channel_id=1, source_target_pairs={{0,4},{4,0},{8,12},{12,8},{16,20},{20,16},{24,28},{28,24},{1,5},{5... | collective-permute-start | bytes 393224 | tf_op jit(solution)/shard_map/ppermute | solution.py:427
  11.5 1.4 %collective-permute-start.6 = (bf16[16,4096]{1,0:T(8,128)(2,1)S(1)}, bf16[16,4096]{1,0:T(8,128)(2,1)S(1)}, u32[]{:S(2)}, u32[]{:S(2)}) collective-permute-start(bf16[16,4096]{1,0:T(8,128)(2,1)S(1)} %collective-permute-done.5.refs_6_), channel_id=1, source_target_pairs={{0,4},{4,0},{8,12},{12,8},{16,20},{20,16},{24,28},{28,24},{1,5},{5... | collective-permute-start | bytes 393224 | tf_op jit(solution)/shard_map/ppermute | solution.py:427
  12.8 1.3 %collective-permute-start.4 = (bf16[16,4096]{1,0:T(8,128)(2,1)S(1)}, bf16[16,4096]{1,0:T(8,128)(2,1)S(1)}, u32[]{:S(2)}, u32[]{:S(2)}) collective-permute-start(bf16[16,4096]{1,0:T(8,128)(2,1)S(1)} %collective-permute-done.3.refs_4_), channel_id=1, source_target_pairs={{0,4},{4,0},{8,12},{12,8},{16,20},{20,16},{24,28},{28,24},{1,5},{5... | collective-permute-start | bytes 393224 | tf_op jit(solution)/shard_map/ppermute | solution.py:427
  15.7 1.3 %collective-permute-start.7 = (bf16[144,128]{1,0:T(8,128)(2,1)S(1)}, bf16[144,128]{1,0:T(8,128)(2,1)S(1)}, u32[]{:S(2)}, u32[]{:S(2)}) collective-permute-start(bf16[144,128]{1,0:T(8,128)(2,1)S(1)} %get-tuple-element.58), channel_id=1, source_target_pairs={{0,4},{4,0},{8,12},{12,8},{16,20},{20,16},{24,28},{28,24},{1,5},{5... | collective-permute-start | bytes 110600 | tf_op jit(solution)/shard_map/ppermute | solution.py:427
  17.0 5.5 %collective-permute-start.10 = (bf16[144,128]{1,0:T(8,128)(2,1)S(1)}, bf16[144,128]{1,0:T(8,128)(2,1)S(1)}, u32[]{:S(2)}, u32[]{:S(2)}) collective-permute-start(bf16[144,128]{1,0:T(8,128)(2,1)S(1)} %shard_map.205.after.refs_0_), channel_id=1, source_target_pairs={{0,24},{4,28},{8,16},{12,20},{16,8},{20,12},{24,0},{28,4},{1,25},{... | collective-permute-start | bytes 110600 | tf_op jit(solution)/shard_map/ppermute | solution.py:430
  18.5 4.0 %collective-permute-start.9 = (bf16[144,128]{1,0:T(8,128)(2,1)S(1)}, bf16[144,128]{1,0:T(8,128)(2,1)S(1)}, u32[]{:S(2)}, u32[]{:S(2)}) collective-permute-start(bf16[144,128]{1,0:T(8,128)(2,1)S(1)} %shard_map.205.after.refs_0_), channel_id=1, source_target_pairs={{0,16},{4,20},{8,24},{12,28},{16,0},{20,4},{24,8},{28,12},{1,17},{... | collective-permute-start | bytes 110600 | tf_op jit(solution)/shard_map/ppermute | solution.py:430
  20.0 4.0 %collective-permute-start.8 = (bf16[144,128]{1,0:T(8,128)(2,1)S(1)}, bf16[144,128]{1,0:T(8,128)(2,1)S(1)}, u32[]{:S(2)}, u32[]{:S(2)}) collective-permute-start(bf16[144,128]{1,0:T(8,128)(2,1)S(1)} %shard_map.205.after.refs_0_), channel_id=1, source_target_pairs={{0,8},{4,12},{8,0},{12,4},{16,24},{20,28},{24,16},{28,20},{1,9},{5... | collective-permute-start | bytes 110600 | tf_op jit(solution)/shard_map/ppermute | solution.py:430
  24.0 8.0 %collective-permute-start.13 = (bf16[144,128]{1,0:T(8,128)(2,1)S(1)}, bf16[144,128]{1,0:T(8,128)(2,1)S(1)}, u32[]{:S(2)}, u32[]{:S(2)}) collective-permute-start(bf16[144,128]{1,0:T(8,128)(2,1)S(1)} %shard_map.207.after.refs_0_), channel_id=1, source_target_pairs={{0,3},{1,2},{2,1},{3,0},{4,7},{5,6},{6,5},{7,4},{8,11},{9,10},{10,... | collective-permute-start | bytes 110600 | tf_op jit(solution)/shard_map/ppermute | solution.py:433
  27.7 4.9 %collective-permute-start.12 = (bf16[144,128]{1,0:T(8,128)(2,1)S(1)}, bf16[144,128]{1,0:T(8,128)(2,1)S(1)}, u32[]{:S(2)}, u32[]{:S(2)}) collective-permute-start(bf16[144,128]{1,0:T(8,128)(2,1)S(1)} %shard_map.207.after.refs_0_), channel_id=1, source_target_pairs={{0,2},{1,3},{2,0},{3,1},{4,6},{5,7},{6,4},{7,5},{8,10},{9,11},{10,... | collective-permute-start | bytes 110600 | tf_op jit(solution)/shard_map/ppermute | solution.py:433
  27.7 4.9 %collective-permute-start.11 = (bf16[144,128]{1,0:T(8,128)(2,1)S(1)}, bf16[144,128]{1,0:T(8,128)(2,1)S(1)}, u32[]{:S(2)}, u32[]{:S(2)}) collective-permute-start(bf16[144,128]{1,0:T(8,128)(2,1)S(1)} %shard_map.207.after.refs_0_), channel_id=1, source_target_pairs={{0,1},{1,0},{2,3},{3,2},{4,5},{5,4},{6,7},{7,6},{8,9},{9,8},{10,11... | collective-permute-start | bytes 110600 | tf_op jit(solution)/shard_map/ppermute | solution.py:433
  32.6 1.3 %collective-permute-start.14 = (bf16[144,128]{1,0:T(8,128)(2,1)S(1)}, bf16[144,128]{1,0:T(8,128)(2,1)S(1)}, u32[]{:S(2)}, u32[]{:S(2)}) collective-permute-start(bf16[144,128]{1,0:T(8,128)(2,1)S(1)} %shard_map.209.own_half), channel_id=1, source_target_pairs={{0,4},{4,0},{8,12},{12,8},{16,20},{20,16},{24,28},{28,24},{1,5},{5... | collective-permute-start | bytes 110600 | tf_op jit(solution)/shard_map/ppermute | solution.py:427
  36.3 2.0 %collective-permute-start.15 = (bf16[64,4096]{1,0:T(8,128)(2,1)S(1)}, bf16[64,4096]{1,0:T(8,128)(2,1)S(1)}, u32[]{:S(2)}, u32[]{:S(2)}) collective-permute-start(bf16[64,4096]{1,0:T(8,128)(2,1)S(1)} %get-tuple-element.69), channel_id=1, source_target_pairs={{0,4},{4,0},{8,12},{12,8},{16,20},{20,16},{24,28},{28,24},{1,5},{5... | collective-permute-start | bytes 1572872 | tf_op jit(solution)/shard_map/ppermute | solution.py:427
  38.4 7.4 %collective-permute-start.16 = (bf16[16,4096]{1,0:T(8,128)(2,1)S(1)}, bf16[16,4096]{1,0:T(8,128)(2,1)S(1)}, u32[]{:S(2)}, u32[]{:S(2)}) collective-permute-start(bf16[16,4096]{1,0:T(8,128)(2,1)S(1)} %get-tuple-element.71), channel_id=1, source_target_pairs={{0,8},{4,12},{8,0},{12,4},{16,24},{20,28},{24,16},{28,20},{1,9},{5... | collective-permute-start | bytes 393224 | tf_op jit(solution)/shard_map/ppermute | solution.py:430
  39.0 8.1 %collective-permute-start.17 = (bf16[16,4096]{1,0:T(8,128)(2,1)S(1)}, bf16[16,4096]{1,0:T(8,128)(2,1)S(1)}, u32[]{:S(2)}, u32[]{:S(2)}) collective-permute-start(bf16[16,4096]{1,0:T(8,128)(2,1)S(1)} %get-tuple-element.72), channel_id=1, source_target_pairs={{0,16},{4,20},{8,24},{12,28},{16,0},{20,4},{24,8},{28,12},{1,17},{... | collective-permute-start | bytes 393224 | tf_op jit(solution)/shard_map/ppermute | solution.py:430
  39.5 7.6 %collective-permute-start.18 = (bf16[16,4096]{1,0:T(8,128)(2,1)S(1)}, bf16[16,4096]{1,0:T(8,128)(2,1)S(1)}, u32[]{:S(2)}, u32[]{:S(2)}) collective-permute-start(bf16[16,4096]{1,0:T(8,128)(2,1)S(1)} %get-tuple-element.73), channel_id=1, source_target_pairs={{0,24},{4,28},{8,16},{12,20},{16,8},{20,12},{24,0},{28,4},{1,25},{... | collective-permute-start | bytes 393224 | tf_op jit(solution)/shard_map/ppermute | solution.py:430
  47.2 5.0 %collective-permute-start.19 = (bf16[16,4096]{1,0:T(8,128)(2,1)S(1)}, bf16[16,4096]{1,0:T(8,128)(2,1)S(1)}, u32[]{:S(2)}, u32[]{:S(2)}) collective-permute-start(bf16[16,4096]{1,0:T(8,128)(2,1)S(1)} %shard_map.214.after.refs_0_), channel_id=1, source_target_pairs={{0,1},{1,0},{2,3},{3,2},{4,5},{5,4},{6,7},{7,6},{8,9},{9,8},{10,11... | collective-permute-start | bytes 393224 | tf_op jit(solution)/shard_map/ppermute | solution.py:433
  52.2 7.5 %collective-permute-start.20 = (bf16[16,4096]{1,0:T(8,128)(2,1)S(1)}, bf16[16,4096]{1,0:T(8,128)(2,1)S(1)}, u32[]{:S(2)}, u32[]{:S(2)}) collective-permute-start(bf16[16,4096]{1,0:T(8,128)(2,1)S(1)} %shard_map.216.block), channel_id=1, source_target_pairs={{0,2},{1,3},{2,0},{3,1},{4,6},{5,7},{6,4},{7,5},{8,10},{9,11},{10,... | collective-permute-start | bytes 393224 | tf_op jit(solution)/shard_map/ppermute | solution.py:433
  59.8 6.9 %collective-permute-start.23 = (bf16[16,4224]{1,0:T(8,128)(2,1)S(1)}, bf16[16,4224]{1,0:T(8,128)(2,1)S(1)}, u32[]{:S(2)}, u32[]{:S(2)}) collective-permute-start(bf16[16,4224]{1,0:T(8,128)(2,1)S(1)} %shard_map.218.block.residual), channel_id=1, source_target_pairs={{0,24},{4,28},{8,16},{12,20},{16,8},{20,12},{24,0},{28,4},{1,25},{... | collective-permute-start | bytes 405512 | tf_op jit(solution)/shard_map/ppermute | solution.py:430
  61.1 6.3 %collective-permute-start.22 = (bf16[16,4224]{1,0:T(8,128)(2,1)S(1)}, bf16[16,4224]{1,0:T(8,128)(2,1)S(1)}, u32[]{:S(2)}, u32[]{:S(2)}) collective-permute-start(bf16[16,4224]{1,0:T(8,128)(2,1)S(1)} %shard_map.218.block.residual), channel_id=1, source_target_pairs={{0,16},{4,20},{8,24},{12,28},{16,0},{20,4},{24,8},{28,12},{1,17},{... | collective-permute-start | bytes 405512 | tf_op jit(solution)/shard_map/ppermute | solution.py:430
  62.8 5.5 %collective-permute-start.21 = (bf16[16,4224]{1,0:T(8,128)(2,1)S(1)}, bf16[16,4224]{1,0:T(8,128)(2,1)S(1)}, u32[]{:S(2)}, u32[]{:S(2)}) collective-permute-start(bf16[16,4224]{1,0:T(8,128)(2,1)S(1)} %shard_map.218.block.residual), channel_id=1, source_target_pairs={{0,8},{4,12},{8,0},{12,4},{16,24},{20,28},{24,16},{28,20},{1,9},{5... | collective-permute-start | bytes 405512 | tf_op jit(solution)/shard_map/ppermute | solution.py:430
  65.6 2.7 %collective-permute-start.24 = (bf16[16,4224]{1,0:T(8,128)(2,1)S(1)}, bf16[16,4224]{1,0:T(8,128)(2,1)S(1)}, u32[]{:S(2)}, u32[]{:S(2)}) collective-permute-start(bf16[16,4224]{1,0:T(8,128)(2,1)S(1)} %get-tuple-element.79.refs_0_), channel_id=1, source_target_pairs={{0,4},{4,0},{8,12},{12,8},{16,20},{20,16},{24,28},{28,24},{1,5},{5... | collective-permute-start | bytes 405512 | tf_op jit(solution)/shard_map/ppermute | solution.py:427
  66.7 1.6 %collective-permute-start.27 = (bf16[16,4224]{1,0:T(8,128)(2,1)S(1)}, bf16[16,4224]{1,0:T(8,128)(2,1)S(1)}, u32[]{:S(2)}, u32[]{:S(2)}) collective-permute-start(bf16[16,4224]{1,0:T(8,128)(2,1)S(1)} %collective-permute-done.23.refs_3_), channel_id=1, source_target_pairs={{0,4},{4,0},{8,12},{12,8},{16,20},{20,16},{24,28},{28,24},{1,5},{5... | collective-permute-start | bytes 405512 | tf_op jit(solution)/shard_map/ppermute | solution.py:427
  67.4 1.4 %collective-permute-start.26 = (bf16[16,4224]{1,0:T(8,128)(2,1)S(1)}, bf16[16,4224]{1,0:T(8,128)(2,1)S(1)}, u32[]{:S(2)}, u32[]{:S(2)}) collective-permute-start(bf16[16,4224]{1,0:T(8,128)(2,1)S(1)} %collective-permute-done.22.refs_2_), channel_id=1, source_target_pairs={{0,4},{4,0},{8,12},{12,8},{16,20},{20,16},{24,28},{28,24},{1,5},{5... | collective-permute-start | bytes 405512 | tf_op jit(solution)/shard_map/ppermute | solution.py:427
  68.3 1.4 %collective-permute-start.25 = (bf16[16,4224]{1,0:T(8,128)(2,1)S(1)}, bf16[16,4224]{1,0:T(8,128)(2,1)S(1)}, u32[]{:S(2)}, u32[]{:S(2)}) collective-permute-start(bf16[16,4224]{1,0:T(8,128)(2,1)S(1)} %collective-permute-done.21.refs_1_), channel_id=1, source_target_pairs={{0,4},{4,0},{8,12},{12,8},{16,20},{20,16},{24,28},{28,24},{1,5},{5... | collective-permute-start | bytes 405512 | tf_op jit(solution)/shard_map/ppermute | solution.py:427
  85.6 2.0 %collective-permute-start.28 = (bf16[64,4096]{1,0:T(8,128)(2,1)S(1)}, bf16[64,4096]{1,0:T(8,128)(2,1)S(1)}, u32[]{:S(2)}, u32[]{:S(2)}) collective-permute-start(bf16[64,4096]{1,0:T(8,128)(2,1)S(1)} %get-tuple-element.90), channel_id=1, source_target_pairs={{0,4},{4,0},{8,12},{12,8},{16,20},{20,16},{24,28},{28,24},{1,5},{5... | collective-permute-start | bytes 1572872 | tf_op jit(solution)/shard_map/ppermute | solution.py:427
  87.7 6.4 %collective-permute-start.29 = (bf16[16,4096]{1,0:T(8,128)(2,1)S(1)}, bf16[16,4096]{1,0:T(8,128)(2,1)S(1)}, u32[]{:S(2)}, u32[]{:S(2)}) collective-permute-start(bf16[16,4096]{1,0:T(8,128)(2,1)S(1)} %get-tuple-element.92), channel_id=1, source_target_pairs={{0,8},{4,12},{8,0},{12,4},{16,24},{20,28},{24,16},{28,20},{1,9},{5... | collective-permute-start | bytes 393224 | tf_op jit(solution)/shard_map/ppermute | solution.py:430
  88.6 8.3 %collective-permute-start.30 = (bf16[16,4096]{1,0:T(8,128)(2,1)S(1)}, bf16[16,4096]{1,0:T(8,128)(2,1)S(1)}, u32[]{:S(2)}, u32[]{:S(2)}) collective-permute-start(bf16[16,4096]{1,0:T(8,128)(2,1)S(1)} %get-tuple-element.93), channel_id=1, source_target_pairs={{0,16},{4,20},{8,24},{12,28},{16,0},{20,4},{24,8},{28,12},{1,17},{... | collective-permute-start | bytes 393224 | tf_op jit(solution)/shard_map/ppermute | solution.py:430
  89.7 7.1 %collective-permute-start.31 = (bf16[16,4096]{1,0:T(8,128)(2,1)S(1)}, bf16[16,4096]{1,0:T(8,128)(2,1)S(1)}, u32[]{:S(2)}, u32[]{:S(2)}) collective-permute-start(bf16[16,4096]{1,0:T(8,128)(2,1)S(1)} %get-tuple-element.94), channel_id=1, source_target_pairs={{0,24},{4,28},{8,16},{12,20},{16,8},{20,12},{24,0},{28,4},{1,25},{... | collective-permute-start | bytes 393224 | tf_op jit(solution)/shard_map/ppermute | solution.py:430
  96.9 4.5 %collective-permute-start.32 = (bf16[16,1024]{1,0:T(8,128)(2,1)S(1)}, bf16[16,1024]{1,0:T(8,128)(2,1)S(1)}, u32[]{:S(2)}, u32[]{:S(2)}) collective-permute-start(bf16[16,1024]{1,0:T(8,128)(2,1)S(1)} %get-tuple-element.96), channel_id=1, source_target_pairs={{0,1},{1,0},{2,3},{3,2},{4,5},{5,4},{6,7},{7,6},{8,9},{9,8},{10,11... | collective-permute-start | bytes 98312 | tf_op jit(solution)/shard_map/ppermute | solution.py:433
  97.0 5.1 %collective-permute-start.33 = (bf16[16,1024]{1,0:T(8,128)(2,1)S(1)}, bf16[16,1024]{1,0:T(8,128)(2,1)S(1)}, u32[]{:S(2)}, u32[]{:S(2)}) collective-permute-start(bf16[16,1024]{1,0:T(8,128)(2,1)S(1)} %get-tuple-element.97), channel_id=1, source_target_pairs={{0,2},{1,3},{2,0},{3,1},{4,6},{5,7},{6,4},{7,5},{8,10},{9,11},{10,... | collective-permute-start | bytes 98312 | tf_op jit(solution)/shard_map/ppermute | solution.py:433
  100.2 5.7 %collective-permute-start.34 = (bf16[16,1024]{1,0:T(8,128)(2,1)S(1)}, bf16[16,1024]{1,0:T(8,128)(2,1)S(1)}, u32[]{:S(2)}, u32[]{:S(2)}) collective-permute-start(bf16[16,1024]{1,0:T(8,128)(2,1)S(1)} %get-tuple-element.98), channel_id=1, source_target_pairs={{0,3},{1,2},{2,1},{3,0},{4,7},{5,6},{6,5},{7,4},{8,11},{9,10},{10,... | collective-permute-start | bytes 98312 | tf_op jit(solution)/shard_map/ppermute | solution.py:433

commit v5 on v4

--- a/solution.py
+++ b/solution.py
@@ -258,7 +258,7 @@
         mixed[one, :] = jnp.sum(state * out_coef, axis=0, keepdims=True)
         return carry
 
-    lax.fori_loop(0, channels, channel, 0, unroll=8)
+    lax.fori_loop(0, channels, channel, 0, unroll=32)
     gated = (mixed[...] + columns[:, 6:7] * conved[...]) * gate[...]
     turned[...] = gated.T
     parts = []

time: 107 us -> 106 us (level)
  no operation moved by 1% of the time
where the time goes in v5:
time: 106 us
  Pallas kernels  41.2 us (39%)
  waiting for transfers between devices  32.1 us (30%)
  starting transfers between devices  32 us (30%)
    pallas_call x21, Pallas kernels, kernel_call(): pl.pallas_call(body, out_shape=[jax.ShapeDtypeStruct(*out) for out in out...  41.2 us
    ppermute x15, starting transfers between devices, to_chip(): lax.ppermute(values, 'wide', [(i, i ^ 2 * k) for i in range(wide_count)])  18.8 us
    ppermute x15, waiting for transfers between devices, to_chip(): lax.ppermute(values, 'wide', [(i, i ^ 2 * k) for i in range(wide_count)])  15.5 us
    ppermute x8, starting transfers between devices, to_narrow(): lax.ppermute(values, 'narrow', [(i, i ^ k) for i in range(narrow_count)])  11.9 us
    ppermute x8, waiting for transfers between devices, to_narrow(): lax.ppermute(values, 'narrow', [(i, i ^ k) for i in range(narrow_count)])  8.87 us
    ppermute x12, waiting for transfers between devices, swap(): return lax.ppermute(values, 'wide', [(i, i ^ 1) for i in range(wide_count)])  7.75 us
  transfers between devices with their start and end apart: 35, of which 22 were waited for; matrix products, arithmetic and copies ran while one was open for 0% of the time, Pallas kernels for 19%

profile of v5, /device:TPU:0, one launch (start us, length us, event | category | flops | bytes accessed | tf_op | source)
XLA Modules:
  0.0 106.2 jit_solution(17785474322697610431)
XLA Ops:
  0.6 3.0 %collective-permute-start.1 = (bf16[16,4096]{1,0:T(8,128)(2,1)}, bf16[16,4096]{1,0:T(8,128)(2,1)S(1)}, u32[]{:S(2)}, u32[]{:S(2)}) collective-permute-start(bf16[16,4096]{1,0:T(8,128)(2,1)} %hidden.1), channel_id=1, source_target_pairs={{0,8},{4,12},{8,0},{12,4},{16,24},{20,28},{24,16},{28,20},{1,9},{5... | collective-permute-start | bytes 393224 | tf_op jit(solution)/shard_map/ppermute | solution.py:430
  3.6 1.5 %collective-permute-start.5 = (bf16[16,4096]{1,0:T(8,128)(2,1)}, bf16[16,4096]{1,0:T(8,128)(2,1)S(1)}, u32[]{:S(2)}, u32[]{:S(2)}) collective-permute-start(bf16[16,4096]{1,0:T(8,128)(2,1)} %hidden.1), channel_id=1, source_target_pairs={{0,24},{4,28},{8,16},{12,20},{16,8},{20,12},{24,0},{28,4},{1,25},{... | collective-permute-start | bytes 393224 | tf_op jit(solution)/shard_map/ppermute | solution.py:430
  5.2 2.5 %shard_map.203 = (bf16[2,256,4096]{2,1,0:T(8,128)(2,1)S(1)}, bf16[3,256,128]{2,1,0:T(8,128)(2,1)S(1)}, bf16[288,256]{1,0:T(8,128)(2,1)S(1)}, bf16[16,4096]{1,0:T...) custom-call(bf16[2,256,4096]{2,1,0:T(8,128)(2,1)} %in_weight.1, ...), custom_call_target="tpu_custom_call" | custom-call | bytes 8388608 | tf_op jit(solution)/shard_map/pallas_call | solution.py:29
  8.3 3.2 %collective-permute-done.5.refs_6_ = bf16[16,4096]{1,0:T(8,128)(2,1)S(1)} collective-permute-done((bf16[16,4096]{1,0:T(8,128)(2,1)}, bf16[16,4096]{1,0:T(8,128)(2,1)S(1)}, u32[]{:S(2)}, u32[]{:S(2)}) %collective-permute-start.5) | collective-permute-done | bytes 131104 | tf_op jit(solution)/shard_map/ppermute | solution.py:430
  11.5 1.4 %collective-permute-done.3.refs_4_ = bf16[16,4096]{1,0:T(8,128)(2,1)S(1)} collective-permute-done((bf16[16,4096]{1,0:T(8,128)(2,1)}, bf16[16,4096]{1,0:T(8,128)(2,1)S(1)}, u32[]{:S(2)}, u32[]{:S(2)}) %collective-permute-start.3) | collective-permute-done | bytes 131104 | tf_op jit(solution)/shard_map/ppermute | solution.py:430
  12.8 1.3 %collective-permute-done.4.refs_5_ = bf16[16,4096]{1,0:T(8,128)(2,1)S(1)} collective-permute-done((bf16[16,4096]{1,0:T(8,128)(2,1)S(1)}, bf16[16,4096]{1,0:T(8,128)(2,1)S(1)}, u32[]{:S(2)}, u32[]{:S(2)}) %collective-permute-start.4) | collective-permute-done | bytes 131104 | tf_op jit(solution)/shard_map/ppermute | solution.py:427
  14.2 1.5 %shard_map.204 = (f32[256,128]{1,0:T(8,128)S(1)}, bf16[128,4096]{1,0:T(8,128)(2,1)S(1)}, bf16[144,128]{1,0:T(8,128)(2,1)S(1)}, bf16[144,128]{1,0:T(8,128)(2,1)S(1)}) custom-call(bf16[16,4096]{1,0:T(8,128)(2,1)S(1)} %get-tuple-element.51.refs_0_.hidden, bf16[16,4096]{1,0:T(8,128)(2,1)S(1)} %collective-permute-done.refs_1_, ...), custom_call_target="tpu_custom_call" | custom-call | tf_op jit(solution)/shard_map/pallas_call | solution.py:29
  15.9 1.1 %collective-permute-done.7.refs_1_ = bf16[144,128]{1,0:T(8,128)(2,1)S(1)} collective-permute-done((bf16[144,128]{1,0:T(8,128)(2,1)S(1)}, bf16[144,128]{1,0:T(8,128)(2,1)S(1)}, u32[]{:S(2)}, u32[]{:S(2)}) %collective-permute-start.7) | collective-permute-done | bytes 36896 | tf_op jit(solution)/shard_map/ppermute | solution.py:427
  17.0 1.5 %collective-permute-start.10 = (bf16[144,128]{1,0:T(8,128)(2,1)S(1)}, bf16[144,128]{1,0:T(8,128)(2,1)S(1)}, u32[]{:S(2)}, u32[]{:S(2)}) collective-permute-start(bf16[144,128]{1,0:T(8,128)(2,1)S(1)} %shard_map.205.after.refs_0_), channel_id=1, source_target_pairs={{0,24},{4,28},{8,16},{12,20},{16,8},{20,12},{24,0},{28,4},{1,25},{... | collective-permute-start | bytes 110600 | tf_op jit(solution)/shard_map/ppermute | solution.py:430
  18.5 1.5 %collective-permute-start.9 = (bf16[144,128]{1,0:T(8,128)(2,1)S(1)}, bf16[144,128]{1,0:T(8,128)(2,1)S(1)}, u32[]{:S(2)}, u32[]{:S(2)}) collective-permute-start(bf16[144,128]{1,0:T(8,128)(2,1)S(1)} %shard_map.205.after.refs_0_), channel_id=1, source_target_pairs={{0,16},{4,20},{8,24},{12,28},{16,0},{20,4},{24,8},{28,12},{1,17},{... | collective-permute-start | bytes 110600 | tf_op jit(solution)/shard_map/ppermute | solution.py:430
  20.6 1.9 %shard_map.206 = (bf16[256,4096]{1,0:T(8,128)(2,1)S(1)}, bf16[256,256]{1,0:T(8,128)(2,1)S(1)}, bf16[256,16,128]{2,1,0:T(8,128)(2,1)S(1)}, f32[8,128]{1,0:T(8,128)S(1)}) custom-call(bf16[144,128]{1,0:T(8,128)(2,1)S(1)} %shard_map.205.after.refs_0_, bf16[256,4096]{1,0:T(8,128)(2,1)} %first.3, bf16[256,256]{1,0:T(8,128)(2,1)} %second.3, bf16[256,16,128]{2,1,0:T(8,128)(2,1)} %third.1), custom_call_target="tpu_custom_call" | custom-call | bytes 6291456 | tf_op jit(solution)/shard_map/pallas_call | solution.py:29
  22.5 1.5 %collective-permute-done.8.refs_1_ = bf16[144,128]{1,0:T(8,128)(2,1)S(1)} collective-permute-done((bf16[144,128]{1,0:T(8,128)(2,1)S(1)}, bf16[144,128]{1,0:T(8,128)(2,1)S(1)}, u32[]{:S(2)}, u32[]{:S(2)}) %collective-permute-start.8) | collective-permute-done | bytes 36896 | tf_op jit(solution)/shard_map/ppermute | solution.py:430
  24.0 3.7 %collective-permute-start.13 = (bf16[144,128]{1,0:T(8,128)(2,1)S(1)}, bf16[144,128]{1,0:T(8,128)(2,1)S(1)}, u32[]{:S(2)}, u32[]{:S(2)}) collective-permute-start(bf16[144,128]{1,0:T(8,128)(2,1)S(1)} %shard_map.207.after.refs_0_), channel_id=1, source_target_pairs={{0,3},{1,2},{2,1},{3,0},{4,7},{5,6},{6,5},{7,4},{8,11},{9,10},{10,... | collective-permute-start | bytes 110600 | tf_op jit(solution)/shard_map/ppermute | solution.py:433
  27.7 0.8 collective-permute-start.11
  28.5 3.5 %shard_map.208 = (bf16[512,4096]{1,0:T(8,128)(2,1)S(1)}, bf16[512,4096]{1,0:T(8,128)(2,1)S(1)}, f32[8,128]{1,0:T(8,128)S(1)}) custom-call(bf16[144,128]{1,0:T(8,128)(2,1)S(1)} %shard_map.207.after.refs_0_, bf16[3072,4096]{1,0:T(8,128)(2,1)} %refs_0_.3), custom_call_target="tpu_custom_call" | custom-call | bytes 16777216 | tf_op jit(solution)/shard_map/pallas_call | solution.py:29
  32.6 0.7 shard_map.210.gate
  33.8 2.0 %shard_map.211 = (bf16[256,16,128]{2,1,0:T(8,128)(2,1)S(1)}, bf16[64,4096]{1,0:T(8,128)(2,1)S(1)}, bf16[64,4096]{1,0:T(8,128)(2,1)S(1)}) custom-call(bf16[144,128]{1,0:T(8,128)(2,1)S(1)} %shard_map.209.own_half, bf16[144,128]{1,0:T(8,128)(2,1)S(1)} %collective-permute-done.14.other_half, f32[256,128]{1,0:T(8,128)S(1)} %get-tuple-element.61.step_gain, ...), custom_call_target="tpu_custom_call" | custom-call | tf_op jit(solution)/shard_map/pallas_call | solution.py:29
  36.1 1.7 %collective-permute-done.15.got = bf16[64,4096]{1,0:T(8,128)(2,1)S(1)} collective-permute-done((bf16[64,4096]{1,0:T(8,128)(2,1)S(1)}, bf16[64,4096]{1,0:T(8,128)(2,1)S(1)}, u32[]{:S(2)}, u32[]{:S(2)}) %collective-permute-start.15) | collective-permute-done | bytes 524320 | tf_op jit(solution)/shard_map/ppermute | solution.py:427
  38.0 0.6 collective-permute-start.16
  39.1 2.4 %collective-permute-start.18 = (bf16[16,4096]{1,0:T(8,128)(2,1)S(1)}, bf16[16,4096]{1,0:T(8,128)(2,1)S(1)}, u32[]{:S(2)}, u32[]{:S(2)}) collective-permute-start(bf16[16,4096]{1,0:T(8,128)(2,1)S(1)} %get-tuple-element.73), channel_id=1, source_target_pairs={{0,24},{4,28},{8,16},{12,20},{16,8},{20,12},{24,0},{28,4},{1,25},{... | collective-permute-start | bytes 393224 | tf_op jit(solution)/shard_map/ppermute | solution.py:430
  41.5 3.9 %shard_map.213 = (bf16[512,4096]{1,0:T(8,128)(2,1)S(1)}, bf16[512,4096]{1,0:T(8,128)(2,1)S(1)}, bf16[256,16,128]{2,1,0:T(8,128)(2,1)}, f32[8,128]{1,0:T(8,128)S(1)}) custom-call(bf16[16,4096]{1,0:T(8,128)(2,1)S(1)} %get-tuple-element.70.after.refs_0_, bf16[256,16,128]{2,1,0:T(8,128)(2,1)S(1)} %get-tuple-element.74.refs_0_, bf16[3072,4096]{1,0:T(8,128)(2,1)} %refs_0_.3), custom_call_target="tpu_custom_call" | custom-call | bytes 16777216 | tf_op jit(solution)/shard_map/pallas_call | solution.py:29
  45.4 1.2 %collective-permute-done.17.refs_2_ = bf16[16,4096]{1,0:T(8,128)(2,1)S(1)} collective-permute-done((bf16[16,4096]{1,0:T(8,128)(2,1)S(1)}, bf16[16,4096]{1,0:T(8,128)(2,1)S(1)}, u32[]{:S(2)}, u32[]{:S(2)}) %collective-permute-start.17) | collective-permute-done | bytes 131104 | tf_op jit(solution)/shard_map/ppermute | solution.py:430
  46.7 0.8 collective-permute-start.19
  47.5 3.5 %shard_map.215 = (bf16[512,4096]{1,0:T(8,128)(2,1)S(1)}, bf16[512,4096]{1,0:T(8,128)(2,1)S(1)}, f32[8,128]{1,0:T(8,128)S(1)}) custom-call(bf16[16,4096]{1,0:T(8,128)(2,1)S(1)} %shard_map.214.after.refs_0_, bf16[3072,4096]{1,0:T(8,128)(2,1)} %refs_0_.3), custom_call_target="tpu_custom_call" | custom-call | bytes 16777216 | tf_op jit(solution)/shard_map/pallas_call | solution.py:29
  51.0 0.7 collective-permute-done.19.refs_1_
  51.8 2.3 %collective-permute-start.20 = (bf16[16,4096]{1,0:T(8,128)(2,1)S(1)}, bf16[16,4096]{1,0:T(8,128)(2,1)S(1)}, u32[]{:S(2)}, u32[]{:S(2)}) collective-permute-start(bf16[16,4096]{1,0:T(8,128)(2,1)S(1)} %shard_map.216.block), channel_id=1, source_target_pairs={{0,2},{1,3},{2,0},{3,1},{4,6},{5,7},{6,4},{7,5},{8,10},{9,11},{10,... | collective-permute-start | bytes 393224 | tf_op jit(solution)/shard_map/ppermute | solution.py:433
  54.1 2.3 %shard_map.217 = (bf16[4096,512]{1,0:T(8,128)(2,1)S(1)}, bf16[16,4096]{1,0:T(8,128)(2,1)S(1)}) custom-call(bf16[16,4096]{1,0:T(8,128)(2,1)S(1)} %shard_map.216.block, bf16[4096,3072]{1,0:T(8,128)(2,1)} %refs_17_.1, bf16[4096,3072]{1,0:T(8,128)(2,1)} %refs_18_.1), custom_call_target="tpu_custom_call" | custom-call | bytes 8388608 | tf_op jit(solution)/shard_map/pallas_call | solution.py:29
  56.3 3.0 %collective-permute-done.20.got = bf16[16,4096]{1,0:T(8,128)(2,1)S(1)} collective-permute-done((bf16[16,4096]{1,0:T(8,128)(2,1)S(1)}, bf16[16,4096]{1,0:T(8,128)(2,1)S(1)}, u32[]{:S(2)}, u32[]{:S(2)}) %collective-permute-start.20) | collective-permute-done | bytes 131104 | tf_op jit(solution)/shard_map/ppermute | solution.py:433
  59.4 1.3 %collective-permute-start.23 = (bf16[16,4224]{1,0:T(8,128)(2,1)S(1)}, bf16[16,4224]{1,0:T(8,128)(2,1)S(1)}, u32[]{:S(2)}, u32[]{:S(2)}) collective-permute-start(bf16[16,4224]{1,0:T(8,128)(2,1)S(1)} %shard_map.218.block.residual), channel_id=1, source_target_pairs={{0,24},{4,28},{8,16},{12,20},{16,8},{20,12},{24,0},{28,4},{1,25},{... | collective-permute-start | bytes 405512 | tf_op jit(solution)/shard_map/ppermute | solution.py:430
  60.7 1.6 %collective-permute-start.22 = (bf16[16,4224]{1,0:T(8,128)(2,1)S(1)}, bf16[16,4224]{1,0:T(8,128)(2,1)S(1)}, u32[]{:S(2)}, u32[]{:S(2)}) collective-permute-start(bf16[16,4224]{1,0:T(8,128)(2,1)S(1)} %shard_map.218.block.residual), channel_id=1, source_target_pairs={{0,16},{4,20},{8,24},{12,28},{16,0},{20,4},{24,8},{28,12},{1,17},{... | collective-permute-start | bytes 405512 | tf_op jit(solution)/shard_map/ppermute | solution.py:430
  62.4 0.6 collective-permute-start.21
  62.9 2.3 %shard_map.219 = (bf16[4096,512]{1,0:T(8,128)(2,1)S(1)}, bf16[16,4224]{1,0:T(8,128)(2,1)S(1)}) custom-call(bf16[16,4224]{1,0:T(8,128)(2,1)S(1)} %shard_map.218.block.residual, bf16[4096,3072]{1,0:T(8,128)(2,1)} %refs_17_.1, bf16[4096,3072]{1,0:T(8,128)(2,1)} %refs_18_.1), custom_call_target="tpu_custom_call" | custom-call | bytes 8388608 | tf_op jit(solution)/shard_map/pallas_call | solution.py:29
  65.3 1.0 collective-permute-done.23.refs_3_
  66.3 0.8 collective-permute-done.22.refs_2_
  67.0 0.9 collective-permute-done.21.refs_1_
  68.4 0.9 collective-permute-done.25.refs_5_
  69.2 15.9 %shard_map.220 = (bf16[64,4096]{1,0:T(8,128)(2,1)S(1)}, bf16[64,4096]{1,0:T(8,128)(2,1)S(1)}) custom-call(bf16[16,4224]{1,0:T(8,128)(2,1)S(1)} %get-tuple-element.79.refs_0_, bf16[16,4224]{1,0:T(8,128)(2,1)S(1)} %collective-permute-done.21.refs_1_, bf16[16,4224]{1,0:T(8,128)(2,1)S(1)} %collective-permute-done.22.refs_2_, ...), custom_call_target="tpu_custom_call" | custom-call | tf_op jit(solution)/shard_map/pallas_call | solution.py:29
  85.4 1.8 %collective-permute-done.28.got = bf16[64,4096]{1,0:T(8,128)(2,1)S(1)} collective-permute-done((bf16[64,4096]{1,0:T(8,128)(2,1)S(1)}, bf16[64,4096]{1,0:T(8,128)(2,1)S(1)}, u32[]{:S(2)}, u32[]{:S(2)}) %collective-permute-start.28) | collective-permute-done | bytes 524320 | tf_op jit(solution)/shard_map/ppermute | solution.py:427
  87.3 0.9 collective-permute-start.29
  88.2 1.2 %collective-permute-start.30 = (bf16[16,4096]{1,0:T(8,128)(2,1)S(1)}, bf16[16,4096]{1,0:T(8,128)(2,1)S(1)}, u32[]{:S(2)}, u32[]{:S(2)}) collective-permute-start(bf16[16,4096]{1,0:T(8,128)(2,1)S(1)} %get-tuple-element.93), channel_id=1, source_target_pairs={{0,16},{4,20},{8,24},{12,28},{16,0},{20,4},{24,8},{28,12},{1,17},{... | collective-permute-start | bytes 393224 | tf_op jit(solution)/shard_map/ppermute | solution.py:430
  89.3 1.5 %collective-permute-start.31 = (bf16[16,4096]{1,0:T(8,128)(2,1)S(1)}, bf16[16,4096]{1,0:T(8,128)(2,1)S(1)}, u32[]{:S(2)}, u32[]{:S(2)}) collective-permute-start(bf16[16,4096]{1,0:T(8,128)(2,1)S(1)} %get-tuple-element.94), channel_id=1, source_target_pairs={{0,24},{4,28},{8,16},{12,20},{16,8},{20,12},{24,0},{28,4},{1,25},{... | collective-permute-start | bytes 393224 | tf_op jit(solution)/shard_map/ppermute | solution.py:430
  90.8 2.9 %collective-permute-done.29.refs_1_ = bf16[16,4096]{1,0:T(8,128)(2,1)S(1)} collective-permute-done((bf16[16,4096]{1,0:T(8,128)(2,1)S(1)}, bf16[16,4096]{1,0:T(8,128)(2,1)S(1)}, u32[]{:S(2)}, u32[]{:S(2)}) %collective-permute-start.29) | collective-permute-done | bytes 131104 | tf_op jit(solution)/shard_map/ppermute | solution.py:430
  93.7 2.7 %collective-permute-done.30.refs_2_ = bf16[16,4096]{1,0:T(8,128)(2,1)S(1)} collective-permute-done((bf16[16,4096]{1,0:T(8,128)(2,1)S(1)}, bf16[16,4096]{1,0:T(8,128)(2,1)S(1)}, u32[]{:S(2)}, u32[]{:S(2)}) %collective-permute-start.30) | collective-permute-done | bytes 131104 | tf_op jit(solution)/shard_map/ppermute | solution.py:430
  96.6 3.2 %collective-permute-start.33 = (bf16[16,1024]{1,0:T(8,128)(2,1)S(1)}, bf16[16,1024]{1,0:T(8,128)(2,1)S(1)}, u32[]{:S(2)}, u32[]{:S(2)}) collective-permute-start(bf16[16,1024]{1,0:T(8,128)(2,1)S(1)} %get-tuple-element.97), channel_id=1, source_target_pairs={{0,2},{1,3},{2,0},{3,1},{4,6},{5,7},{6,4},{7,5},{8,10},{9,11},{10,... | collective-permute-start | bytes 98312 | tf_op jit(solution)/shard_map/ppermute | solution.py:433
  99.8 1.1 %collective-permute-start.34 = (bf16[16,1024]{1,0:T(8,128)(2,1)S(1)}, bf16[16,1024]{1,0:T(8,128)(2,1)S(1)}, u32[]{:S(2)}, u32[]{:S(2)}) collective-permute-start(bf16[16,1024]{1,0:T(8,128)(2,1)S(1)} %get-tuple-element.98), channel_id=1, source_target_pairs={{0,3},{1,2},{2,1},{3,0},{4,7},{5,6},{6,5},{7,4},{8,11},{9,10},{10,... | collective-permute-start | bytes 98312 | tf_op jit(solution)/shard_map/ppermute | solution.py:433
  100.9 0.7 collective-permute-done.33.refs_2_
  101.7 3.8 %collective-permute-done.34.refs_3_ = bf16[16,1024]{1,0:T(8,128)(2,1)S(1)} collective-permute-done((bf16[16,1024]{1,0:T(8,128)(2,1)S(1)}, bf16[16,1024]{1,0:T(8,128)(2,1)S(1)}, u32[]{:S(2)}, u32[]{:S(2)}) %collective-permute-start.34) | collective-permute-done | bytes 32800 | tf_op jit(solution)/shard_map/ppermute | solution.py:433
  105.5 0.6 shard_map.223
  (43 shorter events, 4.6 us)
Async XLA Ops:
  0.6 7.2 %collective-permute-start.1 = (bf16[16,4096]{1,0:T(8,128)(2,1)}, bf16[16,4096]{1,0:T(8,128)(2,1)S(1)}, u32[]{:S(2)}, u32[]{:S(2)}) collective-permute-start(bf16[16,4096]{1,0:T(8,128)(2,1)} %hidden.1), channel_id=1, source_target_pairs={{0,8},{4,12},{8,0},{12,4},{16,24},{20,28},{24,16},{28,20},{1,9},{5... | collective-permute-start | bytes 393224 | tf_op jit(solution)/shard_map/ppermute | solution.py:430
  3.6 7.8 %collective-permute-start.5 = (bf16[16,4096]{1,0:T(8,128)(2,1)}, bf16[16,4096]{1,0:T(8,128)(2,1)S(1)}, u32[]{:S(2)}, u32[]{:S(2)}) collective-permute-start(bf16[16,4096]{1,0:T(8,128)(2,1)} %hidden.1), channel_id=1, source_target_pairs={{0,24},{4,28},{8,16},{12,20},{16,8},{20,12},{24,0},{28,4},{1,25},{... | collective-permute-start | bytes 393224 | tf_op jit(solution)/shard_map/ppermute | solution.py:430
  5.1 7.7 %collective-permute-start.3 = (bf16[16,4096]{1,0:T(8,128)(2,1)}, bf16[16,4096]{1,0:T(8,128)(2,1)S(1)}, u32[]{:S(2)}, u32[]{:S(2)}) collective-permute-start(bf16[16,4096]{1,0:T(8,128)(2,1)} %hidden.1), channel_id=1, source_target_pairs={{0,16},{4,20},{8,24},{12,28},{16,0},{20,4},{24,8},{28,12},{1,17},{... | collective-permute-start | bytes 393224 | tf_op jit(solution)/shard_map/ppermute | solution.py:430
  7.7 5.1 %collective-permute-start = (bf16[16,4096]{1,0:T(8,128)(2,1)S(1)}, bf16[16,4096]{1,0:T(8,128)(2,1)S(1)}, u32[]{:S(2)}, u32[]{:S(2)}) collective-permute-start(bf16[16,4096]{1,0:T(8,128)(2,1)S(1)} %get-tuple-element.51.refs_0_.hidden), channel_id=1, source_target_pairs={{0,4},{4,0},{8,12},{12,8},{16,20},{20,16},{24,28},{28,24},{1,5},{5... | collective-permute-start | bytes 393224 | tf_op jit(solution)/shard_map/ppermute | solution.py:427
  7.9 5.0 %collective-permute-start.2 = (bf16[16,4096]{1,0:T(8,128)(2,1)S(1)}, bf16[16,4096]{1,0:T(8,128)(2,1)S(1)}, u32[]{:S(2)}, u32[]{:S(2)}) collective-permute-start(bf16[16,4096]{1,0:T(8,128)(2,1)S(1)} %collective-permute-done.1.refs_2_), channel_id=1, source_target_pairs={{0,4},{4,0},{8,12},{12,8},{16,20},{20,16},{24,28},{28,24},{1,5},{5... | collective-permute-start | bytes 393224 | tf_op jit(solution)/shard_map/ppermute | solution.py:427
  11.5 1.4 %collective-permute-start.6 = (bf16[16,4096]{1,0:T(8,128)(2,1)S(1)}, bf16[16,4096]{1,0:T(8,128)(2,1)S(1)}, u32[]{:S(2)}, u32[]{:S(2)}) collective-permute-start(bf16[16,4096]{1,0:T(8,128)(2,1)S(1)} %collective-permute-done.5.refs_6_), channel_id=1, source_target_pairs={{0,4},{4,0},{8,12},{12,8},{16,20},{20,16},{24,28},{28,24},{1,5},{5... | collective-permute-start | bytes 393224 | tf_op jit(solution)/shard_map/ppermute | solution.py:427
  12.8 1.3 %collective-permute-start.4 = (bf16[16,4096]{1,0:T(8,128)(2,1)S(1)}, bf16[16,4096]{1,0:T(8,128)(2,1)S(1)}, u32[]{:S(2)}, u32[]{:S(2)}) collective-permute-start(bf16[16,4096]{1,0:T(8,128)(2,1)S(1)} %collective-permute-done.3.refs_4_), channel_id=1, source_target_pairs={{0,4},{4,0},{8,12},{12,8},{16,20},{20,16},{24,28},{28,24},{1,5},{5... | collective-permute-start | bytes 393224 | tf_op jit(solution)/shard_map/ppermute | solution.py:427
  15.7 1.3 %collective-permute-start.7 = (bf16[144,128]{1,0:T(8,128)(2,1)S(1)}, bf16[144,128]{1,0:T(8,128)(2,1)S(1)}, u32[]{:S(2)}, u32[]{:S(2)}) collective-permute-start(bf16[144,128]{1,0:T(8,128)(2,1)S(1)} %get-tuple-element.58), channel_id=1, source_target_pairs={{0,4},{4,0},{8,12},{12,8},{16,20},{20,16},{24,28},{28,24},{1,5},{5... | collective-permute-start | bytes 110600 | tf_op jit(solution)/shard_map/ppermute | solution.py:427
  17.0 5.5 %collective-permute-start.10 = (bf16[144,128]{1,0:T(8,128)(2,1)S(1)}, bf16[144,128]{1,0:T(8,128)(2,1)S(1)}, u32[]{:S(2)}, u32[]{:S(2)}) collective-permute-start(bf16[144,128]{1,0:T(8,128)(2,1)S(1)} %shard_map.205.after.refs_0_), channel_id=1, source_target_pairs={{0,24},{4,28},{8,16},{12,20},{16,8},{20,12},{24,0},{28,4},{1,25},{... | collective-permute-start | bytes 110600 | tf_op jit(solution)/shard_map/ppermute | solution.py:430
  18.5 4.0 %collective-permute-start.9 = (bf16[144,128]{1,0:T(8,128)(2,1)S(1)}, bf16[144,128]{1,0:T(8,128)(2,1)S(1)}, u32[]{:S(2)}, u32[]{:S(2)}) collective-permute-start(bf16[144,128]{1,0:T(8,128)(2,1)S(1)} %shard_map.205.after.refs_0_), channel_id=1, source_target_pairs={{0,16},{4,20},{8,24},{12,28},{16,0},{20,4},{24,8},{28,12},{1,17},{... | collective-permute-start | bytes 110600 | tf_op jit(solution)/shard_map/ppermute | solution.py:430
  20.0 4.0 %collective-permute-start.8 = (bf16[144,128]{1,0:T(8,128)(2,1)S(1)}, bf16[144,128]{1,0:T(8,128)(2,1)S(1)}, u32[]{:S(2)}, u32[]{:S(2)}) collective-permute-start(bf16[144,128]{1,0:T(8,128)(2,1)S(1)} %shard_map.205.after.refs_0_), channel_id=1, source_target_pairs={{0,8},{4,12},{8,0},{12,4},{16,24},{20,28},{24,16},{28,20},{1,9},{5... | collective-permute-start | bytes 110600 | tf_op jit(solution)/shard_map/ppermute | solution.py:430
  24.0 8.0 %collective-permute-start.13 = (bf16[144,128]{1,0:T(8,128)(2,1)S(1)}, bf16[144,128]{1,0:T(8,128)(2,1)S(1)}, u32[]{:S(2)}, u32[]{:S(2)}) collective-permute-start(bf16[144,128]{1,0:T(8,128)(2,1)S(1)} %shard_map.207.after.refs_0_), channel_id=1, source_target_pairs={{0,3},{1,2},{2,1},{3,0},{4,7},{5,6},{6,5},{7,4},{8,11},{9,10},{10,... | collective-permute-start | bytes 110600 | tf_op jit(solution)/shard_map/ppermute | solution.py:433
  27.7 4.9 %collective-permute-start.12 = (bf16[144,128]{1,0:T(8,128)(2,1)S(1)}, bf16[144,128]{1,0:T(8,128)(2,1)S(1)}, u32[]{:S(2)}, u32[]{:S(2)}) collective-permute-start(bf16[144,128]{1,0:T(8,128)(2,1)S(1)} %shard_map.207.after.refs_0_), channel_id=1, source_target_pairs={{0,2},{1,3},{2,0},{3,1},{4,6},{5,7},{6,4},{7,5},{8,10},{9,11},{10,... | collective-permute-start | bytes 110600 | tf_op jit(solution)/shard_map/ppermute | solution.py:433
  27.7 4.9 %collective-permute-start.11 = (bf16[144,128]{1,0:T(8,128)(2,1)S(1)}, bf16[144,128]{1,0:T(8,128)(2,1)S(1)}, u32[]{:S(2)}, u32[]{:S(2)}) collective-permute-start(bf16[144,128]{1,0:T(8,128)(2,1)S(1)} %shard_map.207.after.refs_0_), channel_id=1, source_target_pairs={{0,1},{1,0},{2,3},{3,2},{4,5},{5,4},{6,7},{7,6},{8,9},{9,8},{10,11... | collective-permute-start | bytes 110600 | tf_op jit(solution)/shard_map/ppermute | solution.py:433
  32.6 1.3 %collective-permute-start.14 = (bf16[144,128]{1,0:T(8,128)(2,1)S(1)}, bf16[144,128]{1,0:T(8,128)(2,1)S(1)}, u32[]{:S(2)}, u32[]{:S(2)}) collective-permute-start(bf16[144,128]{1,0:T(8,128)(2,1)S(1)} %shard_map.209.own_half), channel_id=1, source_target_pairs={{0,4},{4,0},{8,12},{12,8},{16,20},{20,16},{24,28},{28,24},{1,5},{5... | collective-permute-start | bytes 110600 | tf_op jit(solution)/shard_map/ppermute | solution.py:427
  35.9 2.0 %collective-permute-start.15 = (bf16[64,4096]{1,0:T(8,128)(2,1)S(1)}, bf16[64,4096]{1,0:T(8,128)(2,1)S(1)}, u32[]{:S(2)}, u32[]{:S(2)}) collective-permute-start(bf16[64,4096]{1,0:T(8,128)(2,1)S(1)} %get-tuple-element.69), channel_id=1, source_target_pairs={{0,4},{4,0},{8,12},{12,8},{16,20},{20,16},{24,28},{28,24},{1,5},{5... | collective-permute-start | bytes 1572872 | tf_op jit(solution)/shard_map/ppermute | solution.py:427
  38.0 7.4 %collective-permute-start.16 = (bf16[16,4096]{1,0:T(8,128)(2,1)S(1)}, bf16[16,4096]{1,0:T(8,128)(2,1)S(1)}, u32[]{:S(2)}, u32[]{:S(2)}) collective-permute-start(bf16[16,4096]{1,0:T(8,128)(2,1)S(1)} %get-tuple-element.71), channel_id=1, source_target_pairs={{0,8},{4,12},{8,0},{12,4},{16,24},{20,28},{24,16},{28,20},{1,9},{5... | collective-permute-start | bytes 393224 | tf_op jit(solution)/shard_map/ppermute | solution.py:430
  38.6 8.1 %collective-permute-start.17 = (bf16[16,4096]{1,0:T(8,128)(2,1)S(1)}, bf16[16,4096]{1,0:T(8,128)(2,1)S(1)}, u32[]{:S(2)}, u32[]{:S(2)}) collective-permute-start(bf16[16,4096]{1,0:T(8,128)(2,1)S(1)} %get-tuple-element.72), channel_id=1, source_target_pairs={{0,16},{4,20},{8,24},{12,28},{16,0},{20,4},{24,8},{28,12},{1,17},{... | collective-permute-start | bytes 393224 | tf_op jit(solution)/shard_map/ppermute | solution.py:430
  39.1 7.6 %collective-permute-start.18 = (bf16[16,4096]{1,0:T(8,128)(2,1)S(1)}, bf16[16,4096]{1,0:T(8,128)(2,1)S(1)}, u32[]{:S(2)}, u32[]{:S(2)}) collective-permute-start(bf16[16,4096]{1,0:T(8,128)(2,1)S(1)} %get-tuple-element.73), channel_id=1, source_target_pairs={{0,24},{4,28},{8,16},{12,20},{16,8},{20,12},{24,0},{28,4},{1,25},{... | collective-permute-start | bytes 393224 | tf_op jit(solution)/shard_map/ppermute | solution.py:430
  46.7 5.0 %collective-permute-start.19 = (bf16[16,4096]{1,0:T(8,128)(2,1)S(1)}, bf16[16,4096]{1,0:T(8,128)(2,1)S(1)}, u32[]{:S(2)}, u32[]{:S(2)}) collective-permute-start(bf16[16,4096]{1,0:T(8,128)(2,1)S(1)} %shard_map.214.after.refs_0_), channel_id=1, source_target_pairs={{0,1},{1,0},{2,3},{3,2},{4,5},{5,4},{6,7},{7,6},{8,9},{9,8},{10,11... | collective-permute-start | bytes 393224 | tf_op jit(solution)/shard_map/ppermute | solution.py:433
  51.8 7.5 %collective-permute-start.20 = (bf16[16,4096]{1,0:T(8,128)(2,1)S(1)}, bf16[16,4096]{1,0:T(8,128)(2,1)S(1)}, u32[]{:S(2)}, u32[]{:S(2)}) collective-permute-start(bf16[16,4096]{1,0:T(8,128)(2,1)S(1)} %shard_map.216.block), channel_id=1, source_target_pairs={{0,2},{1,3},{2,0},{3,1},{4,6},{5,7},{6,4},{7,5},{8,10},{9,11},{10,... | collective-permute-start | bytes 393224 | tf_op jit(solution)/shard_map/ppermute | solution.py:433
  59.4 6.9 %collective-permute-start.23 = (bf16[16,4224]{1,0:T(8,128)(2,1)S(1)}, bf16[16,4224]{1,0:T(8,128)(2,1)S(1)}, u32[]{:S(2)}, u32[]{:S(2)}) collective-permute-start(bf16[16,4224]{1,0:T(8,128)(2,1)S(1)} %shard_map.218.block.residual), channel_id=1, source_target_pairs={{0,24},{4,28},{8,16},{12,20},{16,8},{20,12},{24,0},{28,4},{1,25},{... | collective-permute-start | bytes 405512 | tf_op jit(solution)/shard_map/ppermute | solution.py:430
  60.7 6.3 %collective-permute-start.22 = (bf16[16,4224]{1,0:T(8,128)(2,1)S(1)}, bf16[16,4224]{1,0:T(8,128)(2,1)S(1)}, u32[]{:S(2)}, u32[]{:S(2)}) collective-permute-start(bf16[16,4224]{1,0:T(8,128)(2,1)S(1)} %shard_map.218.block.residual), channel_id=1, source_target_pairs={{0,16},{4,20},{8,24},{12,28},{16,0},{20,4},{24,8},{28,12},{1,17},{... | collective-permute-start | bytes 405512 | tf_op jit(solution)/shard_map/ppermute | solution.py:430
  62.4 5.5 %collective-permute-start.21 = (bf16[16,4224]{1,0:T(8,128)(2,1)S(1)}, bf16[16,4224]{1,0:T(8,128)(2,1)S(1)}, u32[]{:S(2)}, u32[]{:S(2)}) collective-permute-start(bf16[16,4224]{1,0:T(8,128)(2,1)S(1)} %shard_map.218.block.residual), channel_id=1, source_target_pairs={{0,8},{4,12},{8,0},{12,4},{16,24},{20,28},{24,16},{28,20},{1,9},{5... | collective-permute-start | bytes 405512 | tf_op jit(solution)/shard_map/ppermute | solution.py:430
  65.2 2.7 %collective-permute-start.24 = (bf16[16,4224]{1,0:T(8,128)(2,1)S(1)}, bf16[16,4224]{1,0:T(8,128)(2,1)S(1)}, u32[]{:S(2)}, u32[]{:S(2)}) collective-permute-start(bf16[16,4224]{1,0:T(8,128)(2,1)S(1)} %get-tuple-element.79.refs_0_), channel_id=1, source_target_pairs={{0,4},{4,0},{8,12},{12,8},{16,20},{20,16},{24,28},{28,24},{1,5},{5... | collective-permute-start | bytes 405512 | tf_op jit(solution)/shard_map/ppermute | solution.py:427
  66.3 1.6 %collective-permute-start.27 = (bf16[16,4224]{1,0:T(8,128)(2,1)S(1)}, bf16[16,4224]{1,0:T(8,128)(2,1)S(1)}, u32[]{:S(2)}, u32[]{:S(2)}) collective-permute-start(bf16[16,4224]{1,0:T(8,128)(2,1)S(1)} %collective-permute-done.23.refs_3_), channel_id=1, source_target_pairs={{0,4},{4,0},{8,12},{12,8},{16,20},{20,16},{24,28},{28,24},{1,5},{5... | collective-permute-start | bytes 405512 | tf_op jit(solution)/shard_map/ppermute | solution.py:427
  67.0 1.4 %collective-permute-start.26 = (bf16[16,4224]{1,0:T(8,128)(2,1)S(1)}, bf16[16,4224]{1,0:T(8,128)(2,1)S(1)}, u32[]{:S(2)}, u32[]{:S(2)}) collective-permute-start(bf16[16,4224]{1,0:T(8,128)(2,1)S(1)} %collective-permute-done.22.refs_2_), channel_id=1, source_target_pairs={{0,4},{4,0},{8,12},{12,8},{16,20},{20,16},{24,28},{28,24},{1,5},{5... | collective-permute-start | bytes 405512 | tf_op jit(solution)/shard_map/ppermute | solution.py:427
  67.9 1.4 %collective-permute-start.25 = (bf16[16,4224]{1,0:T(8,128)(2,1)S(1)}, bf16[16,4224]{1,0:T(8,128)(2,1)S(1)}, u32[]{:S(2)}, u32[]{:S(2)}) collective-permute-start(bf16[16,4224]{1,0:T(8,128)(2,1)S(1)} %collective-permute-done.21.refs_1_), channel_id=1, source_target_pairs={{0,4},{4,0},{8,12},{12,8},{16,20},{20,16},{24,28},{28,24},{1,5},{5... | collective-permute-start | bytes 405512 | tf_op jit(solution)/shard_map/ppermute | solution.py:427
  85.2 2.0 %collective-permute-start.28 = (bf16[64,4096]{1,0:T(8,128)(2,1)S(1)}, bf16[64,4096]{1,0:T(8,128)(2,1)S(1)}, u32[]{:S(2)}, u32[]{:S(2)}) collective-permute-start(bf16[64,4096]{1,0:T(8,128)(2,1)S(1)} %get-tuple-element.90), channel_id=1, source_target_pairs={{0,4},{4,0},{8,12},{12,8},{16,20},{20,16},{24,28},{28,24},{1,5},{5... | collective-permute-start | bytes 1572872 | tf_op jit(solution)/shard_map/ppermute | solution.py:427
  87.3 6.4 %collective-permute-start.29 = (bf16[16,4096]{1,0:T(8,128)(2,1)S(1)}, bf16[16,4096]{1,0:T(8,128)(2,1)S(1)}, u32[]{:S(2)}, u32[]{:S(2)}) collective-permute-start(bf16[16,4096]{1,0:T(8,128)(2,1)S(1)} %get-tuple-element.92), channel_id=1, source_target_pairs={{0,8},{4,12},{8,0},{12,4},{16,24},{20,28},{24,16},{28,20},{1,9},{5... | collective-permute-start | bytes 393224 | tf_op jit(solution)/shard_map/ppermute | solution.py:430
  88.2 8.2 %collective-permute-start.30 = (bf16[16,4096]{1,0:T(8,128)(2,1)S(1)}, bf16[16,4096]{1,0:T(8,128)(2,1)S(1)}, u32[]{:S(2)}, u32[]{:S(2)}) collective-permute-start(bf16[16,4096]{1,0:T(8,128)(2,1)S(1)} %get-tuple-element.93), channel_id=1, source_target_pairs={{0,16},{4,20},{8,24},{12,28},{16,0},{20,4},{24,8},{28,12},{1,17},{... | collective-permute-start | bytes 393224 | tf_op jit(solution)/shard_map/ppermute | solution.py:430
  89.3 7.1 %collective-permute-start.31 = (bf16[16,4096]{1,0:T(8,128)(2,1)S(1)}, bf16[16,4096]{1,0:T(8,128)(2,1)S(1)}, u32[]{:S(2)}, u32[]{:S(2)}) collective-permute-start(bf16[16,4096]{1,0:T(8,128)(2,1)S(1)} %get-tuple-element.94), channel_id=1, source_target_pairs={{0,24},{4,28},{8,16},{12,20},{16,8},{20,12},{24,0},{28,4},{1,25},{... | collective-permute-start | bytes 393224 | tf_op jit(solution)/shard_map/ppermute | solution.py:430
  96.5 4.5 %collective-permute-start.32 = (bf16[16,1024]{1,0:T(8,128)(2,1)S(1)}, bf16[16,1024]{1,0:T(8,128)(2,1)S(1)}, u32[]{:S(2)}, u32[]{:S(2)}) collective-permute-start(bf16[16,1024]{1,0:T(8,128)(2,1)S(1)} %get-tuple-element.96), channel_id=1, source_target_pairs={{0,1},{1,0},{2,3},{3,2},{4,5},{5,4},{6,7},{7,6},{8,9},{9,8},{10,11... | collective-permute-start | bytes 98312 | tf_op jit(solution)/shard_map/ppermute | solution.py:433
  96.6 5.1 %collective-permute-start.33 = (bf16[16,1024]{1,0:T(8,128)(2,1)S(1)}, bf16[16,1024]{1,0:T(8,128)(2,1)S(1)}, u32[]{:S(2)}, u32[]{:S(2)}) collective-permute-start(bf16[16,1024]{1,0:T(8,128)(2,1)S(1)} %get-tuple-element.97), channel_id=1, source_target_pairs={{0,2},{1,3},{2,0},{3,1},{4,6},{5,7},{6,4},{7,5},{8,10},{9,11},{10,... | collective-permute-start | bytes 98312 | tf_op jit(solution)/shard_map/ppermute | solution.py:433
  99.8 5.7 %collective-permute-start.34 = (bf16[16,1024]{1,0:T(8,128)(2,1)S(1)}, bf16[16,1024]{1,0:T(8,128)(2,1)S(1)}, u32[]{:S(2)}, u32[]{:S(2)}) collective-permute-start(bf16[16,1024]{1,0:T(8,128)(2,1)S(1)} %get-tuple-element.98), channel_id=1, source_target_pairs={{0,3},{1,2},{2,1},{3,0},{4,7},{5,6},{6,5},{7,4},{8,11},{9,10},{10,... | collective-permute-start | bytes 98312 | tf_op jit(solution)/shard_map/ppermute | solution.py:433
